TPU v7x, 32 devices: a whole 2x2x4 slice. The times are simulated.
32 devices in a mesh: expert: 4 (over z), dp: 8 (over y, x, core).
Axes of the slice: x: 2, y: 2, z: 4, core: 2. Of those that a mesh axis runs over, the one named last changes fastest.
Arguments:
- tokens: bfloat16 [128, 512, 512], P(('expert', 'dp')), may hold values from -6 to 6
- memory: bfloat16 [128, 512, 512], P(('expert', 'dp')), may hold values from -6 to 6
- cotangent: bfloat16 [128, 512, 512], P(('expert', 'dp')), may hold values from -6 to 6
- target_length: int32 [128], P(('expert', 'dp')), may hold values from 256 to 512, as said below
- memory_length: int32 [128], P(('expert', 'dp')), may hold values from 256 to 512, as said below
- expert_of: int32 [128], replicated, may hold values from 0 to 7, as said below
- self_norm_gain: float32 [512], replicated, may hold values from 0.5 to 1.5
- self_norm_bias: float32 [512], replicated, may hold values from -1.25 to 1.25
- self_query: bfloat16 [512, 512], replicated, may hold values from -0.25 to 0.25
- self_key: bfloat16 [512, 512], replicated, may hold values from -0.25 to 0.25
- self_value: bfloat16 [512, 512], replicated, may hold values from -0.25 to 0.25
- self_out: bfloat16 [512, 512], replicated, may hold values from -1.5 to 1.5
- self_query_bias: float32 [512], replicated, may hold values from -1.25 to 1.25
- self_value_bias: float32 [512], replicated, may hold values from -1.25 to 1.25
- self_out_bias: float32 [512], replicated, may hold values from -1.25 to 1.25
- cross_norm_gain: float32 [512], replicated, may hold values from 0.5 to 1.5
- cross_norm_bias: float32 [512], replicated, may hold values from -1.25 to 1.25
- cross_query: bfloat16 [512, 512], replicated, may hold values from -0.25 to 0.25
- cross_key: bfloat16 [512, 512], replicated, may hold values from -0.25 to 0.25
- cross_value: bfloat16 [512, 512], replicated, may hold values from -0.25 to 0.25
- cross_out: bfloat16 [512, 512], replicated, may hold values from -1.5 to 1.5
- cross_attention_query_bias: float32 [512], replicated, may hold values from -1.25 to 1.25
- cross_value_bias: float32 [512], replicated, may hold values from -1.25 to 1.25
- cross_out_bias: float32 [512], replicated, may hold values from -1.25 to 1.25
- expert_norm_gain: float32 [512], replicated, may hold values from 0.5 to 1.5
- expert_norm_bias: float32 [512], replicated, may hold values from -1.25 to 1.25
- expert_in: bfloat16 [8, 512, 2048], P('expert'), may hold values from -0.25 to 0.25
- expert_in_bias: float32 [8, 2048], P('expert'), may hold values from -0.625 to 0.625
- expert_out: bfloat16 [8, 2048, 512], P('expert'), may hold values from -0.1875 to 0.1875
- expert_out_bias: float32 [8, 512], P('expert'), may hold values from -0.625 to 0.625
Outputs:
- output: bfloat16 [128, 512, 512], P(('expert', 'dp'))
- tokens_grad: float32 [128, 512, 512], P(('expert', 'dp'))
- memory_grad: float32 [128, 512, 512], P(('expert', 'dp'))
- self_norm_gain_grad: float32 [512], replicated
- self_norm_bias_grad: float32 [512], replicated
- self_query_grad: float32 [512, 512], replicated
- self_key_grad: float32 [512, 512], replicated
- self_value_grad: float32 [512, 512], replicated
- self_out_grad: float32 [512, 512], replicated
- self_query_bias_grad: float32 [512], replicated
- self_value_bias_grad: float32 [512], replicated
- self_out_bias_grad: float32 [512], replicated
- cross_norm_gain_grad: float32 [512], replicated
- cross_norm_bias_grad: float32 [512], replicated
- cross_query_grad: float32 [512, 512], replicated
- cross_key_grad: float32 [512, 512], replicated
- cross_value_grad: float32 [512, 512], replicated
- cross_out_grad: float32 [512, 512], replicated
- cross_query_bias_grad: float32 [512], replicated
- cross_value_bias_grad: float32 [512], replicated
- cross_out_bias_grad: float32 [512], replicated
- expert_norm_gain_grad: float32 [512], replicated
- expert_norm_bias_grad: float32 [512], replicated
- expert_in_grad: float32 [8, 512, 2048], P('expert', 'dp')
- expert_in_bias_grad: float32 [8, 2048], P('expert', 'dp')
- expert_out_grad: float32 [8, 2048, 512], P('expert', 'dp')
- expert_out_bias_grad: float32 [8, 512], P('expert', 'dp')
Inputs may be any that keep to these rules, and one draw needn't show every extreme that they name: `target_length`: valid tokens of a sequence stand first. `memory_length`: valid memory tokens of a sequence stand first. `expert_of`: the 4 sequences of one device name experts of 4 different groups, a group being the ids with one quotient by 2.
All inputs are finite; a program needn't handle non-finite values.
Results may differ from a plain program's by a relative error of at most 0.019.
Values may be sent and summed in bfloat16 or wider, within the bound.
No kernel may reach another device: no remote copies, remote signals or barrier semaphores. Data moves between devices by JAX's collectives and lax.ppermute only.
A program may use at most 192 MiB of HBM per device.

v0:
```python
import jax
import jax.numpy as jnp
from jax import lax
from jax.sharding import PartitionSpec as P

HEADS = 8
HEAD_DIM = 64


EPSILON = 1e-05
SCORE_SCALE = 0.125
NEGATIVE = -1e30


def layer_norm(values, norm_gain, norm_shift):
    centre = values - jnp.mean(values, axis=-1, keepdims=True)
    inverse = lax.rsqrt(jnp.mean(centre * centre, axis=-1, keepdims=True) + EPSILON)
    return centre * inverse * norm_gain + norm_shift


def linear(inputs, weight):
    return jnp.dot(inputs, weight, preferred_element_type=jnp.float32)


def linear_back(grads, weight):
    return lax.dot_general(
        grads, weight, (((1,), (1,)), ((), ())), preferred_element_type=jnp.float32
    )


def gradient_of_weight(inputs, grads):
    return lax.dot_general(
        inputs, grads, (((0,), (0,)), ((), ())), preferred_element_type=jnp.float32
    )


def split_heads(inputs, seq_count):
    return inputs.reshape(seq_count, -1, HEADS, HEAD_DIM)


def add_at(running, expert_pick, addend):
    current = lax.dynamic_index_in_dim(running, expert_pick, 0, False)
    return lax.dynamic_update_index_in_dim(running, current + addend, expert_pick, 0)


def score_block(query_heads, key_heads, allowed):
    scores = (
        jnp.einsum("qhd,khd->hqk", query_heads, key_heads, preferred_element_type=jnp.float32)
        * SCORE_SCALE
    )
    return jnp.where(allowed[None], scores, NEGATIVE)


def attend_one(parts):
    query_heads, key_heads, value_heads, allowed = parts
    scores = score_block(query_heads, key_heads, allowed)
    highest = jnp.max(scores, axis=-1, keepdims=True)
    raised = jnp.exp(scores - highest)
    summed = jnp.sum(raised, axis=-1, keepdims=True)
    chance = (raised / summed).astype(jnp.bfloat16)
    context = jnp.einsum("hqk,khd->qhd", chance, value_heads, preferred_element_type=jnp.float32)
    return (context.astype(jnp.bfloat16), highest + jnp.log(summed))


def attend_back(parts):
    query_heads, key_heads, value_heads, allowed, logsum, grad_context = parts
    scores = score_block(query_heads, key_heads, allowed)
    chance = jnp.exp(scores - logsum)
    grad_value = jnp.einsum(
        "hqk,qhd->khd",
        chance.astype(jnp.bfloat16),
        grad_context,
        preferred_element_type=jnp.float32,
    )
    grad_chance = jnp.einsum(
        "qhd,khd->hqk", grad_context, value_heads, preferred_element_type=jnp.float32
    )
    grad_scores = (
        chance * (grad_chance - jnp.sum(chance * grad_chance, axis=-1, keepdims=True))
    ).astype(jnp.bfloat16)
    grad_query = (
        jnp.einsum("hqk,khd->qhd", grad_scores, key_heads, preferred_element_type=jnp.float32)
        * SCORE_SCALE
    )
    grad_key = (
        jnp.einsum("hqk,qhd->khd", grad_scores, query_heads, preferred_element_type=jnp.float32)
        * SCORE_SCALE
    )
    return (
        grad_query.astype(jnp.bfloat16),
        grad_key.astype(jnp.bfloat16),
        grad_value.astype(jnp.bfloat16),
    )


def on_device(
    tokens,
    memory,
    cotangent,
    target_length,
    memory_length,
    expert_of,
    self_norm_gain,
    self_norm_bias,
    self_query,
    self_key,
    self_value,
    self_out,
    self_query_bias,
    self_value_bias,
    self_out_bias,
    cross_norm_gain,
    cross_norm_bias,
    cross_query,
    cross_key,
    cross_value,
    cross_out,
    cross_attention_query_bias,
    cross_value_bias,
    cross_out_bias,
    expert_norm_gain,
    expert_norm_bias,
    expert_in,
    expert_in_bias,
    expert_out,
    expert_out_bias,
):
    seq_here, length, features = tokens.shape
    mem_rows = memory.shape[1]
    row_count = seq_here * length
    local_count = expert_in.shape[0]
    hidden_width = expert_in.shape[2]
    groups = lax.axis_size("expert")
    places = lax.axis_size("dp")
    own_group = lax.axis_index("expert")
    column = lax.axis_index("dp")
    positions = lax.broadcasted_iota(jnp.int32, (seq_here, length), 1)
    valid_rows = (positions < target_length[:, None]).astype(jnp.float32).reshape(row_count, 1)
    start_rows = tokens.reshape(row_count, features).astype(jnp.float32) * valid_rows
    causal = lax.broadcasted_iota(jnp.int32, (length, length), 0) >= lax.broadcasted_iota(
        jnp.int32, (length, length), 1
    )
    self_allowed = jnp.broadcast_to(causal, (seq_here, length, length))
    key_places = lax.broadcasted_iota(jnp.int32, (seq_here, length, mem_rows), 2)
    cross_allowed = key_places < memory_length[:, None, None]
    normed_self, self_norm_vjp = jax.vjp(layer_norm, start_rows, self_norm_gain, self_norm_bias)
    self_inputs = normed_self.astype(jnp.bfloat16)
    query_one = split_heads(
        (linear(self_inputs, self_query) + self_query_bias).astype(jnp.bfloat16), seq_here
    )
    key_one = split_heads(linear(self_inputs, self_key).astype(jnp.bfloat16), seq_here)
    value_one = split_heads(
        (linear(self_inputs, self_value) + self_value_bias).astype(jnp.bfloat16), seq_here
    )
    context_one, logsum_one = lax.map(attend_one, (query_one, key_one, value_one, self_allowed))
    context_one = context_one.reshape(row_count, features)
    middle_rows = start_rows + linear(context_one, self_out) + self_out_bias
    normed_cross, cross_norm_vjp = jax.vjp(
        layer_norm, middle_rows, cross_norm_gain, cross_norm_bias
    )
    cross_inputs = normed_cross.astype(jnp.bfloat16)
    memory_rows = memory.reshape(seq_here * mem_rows, features)
    query_two = split_heads(
        (linear(cross_inputs, cross_query) + cross_attention_query_bias).astype(jnp.bfloat16),
        seq_here,
    )
    key_two = split_heads(linear(memory_rows, cross_key).astype(jnp.bfloat16), seq_here)
    value_two = split_heads(
        (linear(memory_rows, cross_value) + cross_value_bias).astype(jnp.bfloat16), seq_here
    )
    context_two, logsum_two = lax.map(attend_one, (query_two, key_two, value_two, cross_allowed))
    context_two = context_two.reshape(row_count, features)
    later_rows = middle_rows + linear(context_two, cross_out) + cross_out_bias
    normed_expert, expert_norm_vjp = jax.vjp(
        layer_norm, later_rows, expert_norm_gain, expert_norm_bias
    )
    rows_per_expert = normed_expert.astype(jnp.bfloat16).reshape(seq_here, length, features)
    id_table = expert_of.reshape(groups, places, seq_here)
    own_ids = lax.dynamic_index_in_dim(
        lax.dynamic_index_in_dim(id_table, own_group, 0, False), column, 0, False
    )
    group_iota = lax.broadcasted_iota(jnp.int32, (groups, seq_here), 0)
    expert_assignment = (own_ids[None, :] // local_count == group_iota).astype(jnp.bfloat16)
    send_rows = jnp.einsum(
        "hp,pmc->hmc", expert_assignment, rows_per_expert, preferred_element_type=jnp.float32
    ).astype(jnp.bfloat16)
    incoming = lax.dynamic_index_in_dim(id_table, column, 1, False)
    arriving = incoming // local_count == own_group
    slot_expert = jnp.sum(jnp.where(arriving, incoming % local_count, 0), axis=1)
    slot_used = jnp.any(arriving, axis=1)

    def hidden_of(slot_item):
        slot_rows, expert_pick, used = slot_item

        def hidden_compute(_):
            weight_in = lax.dynamic_index_in_dim(expert_in, expert_pick, 0, False)
            bias_in = lax.dynamic_index_in_dim(expert_in_bias, expert_pick, 0, False)
            return jax.nn.silu(linear(slot_rows, weight_in) + bias_in).astype(jnp.bfloat16)

        def hidden_empty_slot(_):
            return jnp.zeros((slot_rows.shape[0], hidden_width), jnp.bfloat16)

        return lax.cond(used, hidden_compute, hidden_empty_slot, 0)

    def output_of(slot_item):
        hidden_per_slot, expert_pick, used = slot_item

        def output_compute(_):
            weight_out = lax.dynamic_index_in_dim(expert_out, expert_pick, 0, False)
            bias_out = lax.dynamic_index_in_dim(expert_out_bias, expert_pick, 0, False)
            return (linear(hidden_per_slot, weight_out) + bias_out).astype(jnp.bfloat16)

        def output_empty_slot(_):
            return jnp.zeros((hidden_per_slot.shape[0], features), jnp.bfloat16)

        return lax.cond(used, output_compute, output_empty_slot, 0)

    hidden = lax.map(
        hidden_of,
        (
            lax.all_to_all(send_rows, "expert", split_axis=0, concat_axis=0, tiled=True),
            slot_expert,
            slot_used,
        ),
    )
    made_rows = lax.map(output_of, (hidden, slot_expert, slot_used))
    rows_returned_home = lax.all_to_all(
        made_rows, "expert", split_axis=0, concat_axis=0, tiled=True
    )
    returned = jnp.einsum(
        "ur,uzt->rzt", expert_assignment, rows_returned_home, preferred_element_type=jnp.float32
    ).reshape(row_count, features)
    output = (
        ((later_rows + returned) * valid_rows)
        .astype(jnp.bfloat16)
        .reshape(seq_here, length, features)
    )
    grad_later = cotangent.reshape(row_count, features).astype(jnp.float32) * valid_rows
    gradient_computed_locally = grad_later.astype(jnp.bfloat16).reshape(seq_here, length, features)
    send_grads = jnp.einsum(
        "hp,pmc->hmc",
        expert_assignment,
        gradient_computed_locally,
        preferred_element_type=jnp.float32,
    ).astype(jnp.bfloat16)
    rows_in, grads_in = (
        lax.all_to_all(send_rows, "expert", split_axis=0, concat_axis=0, tiled=True),
        lax.all_to_all(send_grads, "expert", split_axis=0, concat_axis=0, tiled=True),
    )

    def slot_back(running, slot_item):
        slot_rows, slot_grads, expert_pick, used = slot_item

        def slot_compute(carried):
            grad_in, grad_in_bias, grad_out, grad_out_bias = carried
            weight_in = lax.dynamic_index_in_dim(expert_in, expert_pick, 0, False)
            bias_in = lax.dynamic_index_in_dim(expert_in_bias, expert_pick, 0, False)
            weight_out = lax.dynamic_index_in_dim(expert_out, expert_pick, 0, False)
            pre_active = linear(slot_rows, weight_in) + bias_in
            sigmoid_part = jax.nn.sigmoid(pre_active)
            hidden_per_slot = jax.nn.silu(pre_active).astype(jnp.bfloat16)
            grad_hidden = linear_back(slot_grads, weight_out).astype(jnp.bfloat16)
            slope = sigmoid_part * (1.0 + pre_active * (1.0 - sigmoid_part))
            grad_pre = (grad_hidden.astype(jnp.float32) * slope).astype(jnp.bfloat16)
            grad_out = add_at(
                grad_out, expert_pick, gradient_of_weight(hidden_per_slot, slot_grads)
            )
            grad_out_bias = add_at(
                grad_out_bias, expert_pick, jnp.sum(slot_grads, axis=0, dtype=jnp.float32)
            )
            grad_in = add_at(grad_in, expert_pick, gradient_of_weight(slot_rows, grad_pre))
            grad_in_bias = add_at(
                grad_in_bias, expert_pick, jnp.sum(grad_pre, axis=0, dtype=jnp.float32)
            )
            grad_rows = linear_back(grad_pre, weight_in).astype(jnp.bfloat16)
            return ((grad_in, grad_in_bias, grad_out, grad_out_bias), grad_rows)

        def slot_empty_slot(carried):
            return (carried, jnp.zeros((slot_rows.shape[0], features), jnp.bfloat16))

        return lax.cond(used, slot_compute, slot_empty_slot, running)

    zero_sums = (
        jnp.zeros(expert_in.shape, jnp.float32),
        jnp.zeros(expert_in_bias.shape, jnp.float32),
        jnp.zeros(expert_out.shape, jnp.float32),
        jnp.zeros(expert_out_bias.shape, jnp.float32),
    )
    expert_sums, grad_slots = lax.scan(
        slot_back, zero_sums, (rows_in, grads_in, slot_expert, slot_used)
    )
    gradient_returned_home = lax.all_to_all(
        grad_slots, "expert", split_axis=0, concat_axis=0, tiled=True
    )
    grad_normed_expert = jnp.einsum(
        "ur,uzt->rzt", expert_assignment, gradient_returned_home, preferred_element_type=jnp.float32
    ).reshape(row_count, features)
    expert_parts = (
        lax.psum_scatter(
            expert_sums[0].astype(jnp.bfloat16), "dp", scatter_dimension=1, tiled=True
        ).astype(jnp.float32),
        lax.psum_scatter(
            expert_sums[1].astype(jnp.bfloat16), "dp", scatter_dimension=1, tiled=True
        ).astype(jnp.float32),
        lax.psum_scatter(
            expert_sums[2].astype(jnp.bfloat16), "dp", scatter_dimension=1, tiled=True
        ).astype(jnp.float32),
        lax.psum_scatter(
            expert_sums[3].astype(jnp.bfloat16), "dp", scatter_dimension=1, tiled=True
        ).astype(jnp.float32),
    )
    grad_later_norm, expert_gain_grad, expert_bias_grad = expert_norm_vjp(grad_normed_expert)
    grad_later = grad_later + grad_later_norm
    grad_branch_two = grad_later.astype(jnp.bfloat16)
    cross_out_grad = gradient_of_weight(context_two, grad_branch_two)
    cross_out_bias_grad = jnp.sum(grad_branch_two, axis=0, dtype=jnp.float32)
    grad_context_two = split_heads(
        linear_back(grad_branch_two, cross_out).astype(jnp.bfloat16), seq_here
    )
    grad_query_two, grad_key_two, grad_value_two = lax.map(
        attend_back, (query_two, key_two, value_two, cross_allowed, logsum_two, grad_context_two)
    )
    grad_query_two = grad_query_two.reshape(row_count, features)
    grad_key_two = grad_key_two.reshape(seq_here * mem_rows, features)
    grad_value_two = grad_value_two.reshape(seq_here * mem_rows, features)
    cross_query_grad = gradient_of_weight(cross_inputs, grad_query_two)
    cross_query_bias_grad = jnp.sum(grad_query_two, axis=0, dtype=jnp.float32)
    cross_key_grad = gradient_of_weight(memory_rows, grad_key_two)
    cross_value_grad = gradient_of_weight(memory_rows, grad_value_two)
    cross_value_bias_grad = jnp.sum(grad_value_two, axis=0, dtype=jnp.float32)
    memory_grad = (
        linear_back(grad_key_two, cross_key) + linear_back(grad_value_two, cross_value)
    ).reshape(seq_here, mem_rows, features)
    grad_middle_norm, cross_gain_grad, cross_bias_grad = cross_norm_vjp(
        linear_back(grad_query_two, cross_query)
    )
    grad_middle = grad_later + grad_middle_norm
    grad_branch_one = grad_middle.astype(jnp.bfloat16)
    self_out_grad = gradient_of_weight(context_one, grad_branch_one)
    self_out_bias_grad = jnp.sum(grad_branch_one, axis=0, dtype=jnp.float32)
    grad_context_one = split_heads(
        linear_back(grad_branch_one, self_out).astype(jnp.bfloat16), seq_here
    )
    grad_query_one, grad_key_one, grad_value_one = lax.map(
        attend_back, (query_one, key_one, value_one, self_allowed, logsum_one, grad_context_one)
    )
    grad_query_one = grad_query_one.reshape(row_count, features)
    grad_key_one = grad_key_one.reshape(row_count, features)
    grad_value_one = grad_value_one.reshape(row_count, features)
    self_query_grad = gradient_of_weight(self_inputs, grad_query_one)
    self_key_grad = gradient_of_weight(self_inputs, grad_key_one)
    self_value_grad = gradient_of_weight(self_inputs, grad_value_one)
    self_query_bias_grad = jnp.sum(grad_query_one, axis=0, dtype=jnp.float32)
    self_value_bias_grad = jnp.sum(grad_value_one, axis=0, dtype=jnp.float32)
    grad_normed_self = (
        linear_back(grad_query_one, self_query)
        + linear_back(grad_key_one, self_key)
        + linear_back(grad_value_one, self_value)
    )
    grad_start_norm, self_gain_grad, self_bias_grad = self_norm_vjp(grad_normed_self)
    tokens_grad = ((grad_middle + grad_start_norm) * valid_rows).reshape(seq_here, length, features)
    dense_sums = lax.psum(
        (
            self_gain_grad,
            self_bias_grad,
            self_query_grad,
            self_key_grad,
            self_value_grad,
            self_out_grad,
            self_query_bias_grad,
            self_value_bias_grad,
            self_out_bias_grad,
            cross_gain_grad,
            cross_bias_grad,
            cross_query_grad,
            cross_key_grad,
            cross_value_grad,
            cross_out_grad,
            cross_query_bias_grad,
            cross_value_bias_grad,
            cross_out_bias_grad,
            expert_gain_grad,
            expert_bias_grad,
        ),
        ("expert", "dp"),
    )
    return (
        output,
        tokens_grad,
        memory_grad,
        dense_sums[0],
        dense_sums[1],
        dense_sums[2],
        dense_sums[3],
        dense_sums[4],
        dense_sums[5],
        dense_sums[6],
        dense_sums[7],
        dense_sums[8],
        dense_sums[9],
        dense_sums[10],
        dense_sums[11],
        dense_sums[12],
        dense_sums[13],
        dense_sums[14],
        dense_sums[15],
        dense_sums[16],
        dense_sums[17],
        dense_sums[18],
        dense_sums[19],
        expert_parts[0],
        expert_parts[1],
        expert_parts[2],
        expert_parts[3],
    )


def solution(mesh):
    placed = (
        P(("expert", "dp"), None, None),
        P(("expert", "dp"), None, None),
        P(("expert", "dp"), None, None),
        P(("expert", "dp")),
        P(("expert", "dp")),
        P(),
        P(),
        P(),
        P(),
        P(),
        P(),
        P(),
        P(),
        P(),
        P(),
        P(),
        P(),
        P(),
        P(),
        P(),
        P(),
        P(),
        P(),
        P(),
        P(),
        P(),
        P("expert", None, None),
        P("expert", None),
        P("expert", None, None),
        P("expert", None),
    )
    return jax.shard_map(
        on_device,
        mesh=mesh,
        in_specs=placed,
        out_specs=(
            P(("expert", "dp"), None, None),
            P(("expert", "dp"), None, None),
            P(("expert", "dp"), None, None),
            P(),
            P(),
            P(),
            P(),
            P(),
            P(),
            P(),
            P(),
            P(),
            P(),
            P(),
            P(),
            P(),
            P(),
            P(),
            P(),
            P(),
            P(),
            P(),
            P(),
            P("expert", "dp", None),
            P("expert", "dp"),
            P("expert", "dp", None),
            P("expert", "dp"),
        ),
        check_vma=False,
    )
```

profile of v0, /device:TPU:0, one launch (start us, length us, event | category | flops | bytes accessed | tf_op | source)
XLA Modules:
  0.0 1055.8 jit_solution(12238135847914198730)
XLA Ops:
  20.3 6.1 reshape.524
  36.1 6.1 reshape.525
  51.9 6.1 reshape.526
  65.3 35.1 %while.90 = (s32[]{:T(128)}, bf16[4,512,8,64]{1,3,2,0:T(8,128)(2,1)}, f32[4,8,512,1]{2,1,3,0:T(8,128)S(1)}, bf16[4,512,8,64]{1,3,2,0:T(8,128)(2,1)}, pred[4,512,...) while((s32[]{:T(128)}, ...), condition=%wide.region_5.6_spmd, body=%wide.region_2.5_spmd.sunk | while | flops 562294784 | bytes 28706908 | solution.py:155
  113.9 6.1 reshape.528
  128.5 6.1 reshape.527
  142.8 6.1 reshape.529
  156.3 35.0 %while.91 = (s32[]{:T(128)}, bf16[4,512,8,64]{1,3,2,0:T(8,128)(2,1)}, f32[4,8,512,1]{2,1,3,0:T(8,128)S(1)}, bf16[4,512,8,64]{1,3,2,0:T(8,128)(2,1)}, pred[4,512,...) while((s32[]{:T(128)}, ...), condition=%wide.region_11.12_spmd, body=%wide.region_8.11_spmd.sunk | while | flops 562294784 | bytes 28706908 | solution.py:171
  207.5 6.3 all-to-all-start
  222.0 40.2 %all-to-all-done = bf16[4,512,512]{2,1,0:T(8,128)(2,1)} async-done(((bf16[4,512,512]{2,1,0:T(8,128)(2,1)}), bf16[4,512,512]{2,1,0:T(8,128)(2,1)}, u32[]{:S(2)}, u32[]{:S(2)}) %all-to-all-start) | async-done | bytes 2097184 | tf_op jit(solution)/shard_map/all_to_all | solution.py:221
  267.0 47.5 %all-to-all-done.2 = bf16[4,512,512]{2,1,0:T(8,128)(2,1)} async-done(((bf16[4,512,512]{2,1,0:T(8,128)(2,1)}), bf16[4,512,512]{2,1,0:T(8,128)(2,1)}, u32[]{:S(2)}, u32[]{:S(2)}) %all-to-all-start.2) | async-done | bytes 2097184 | tf_op jit(solution)/shard_map/all_to_all | solution.py:248
  324.7 106.5 %while.94 = (s32[]{:T(128)}, f32[2,512,2048]{2,1,0:T(8,128)}, f32[2,2048]{1,0:T(2,128)S(1)}, f32[2,2048,512]{2,1,0:T(8,128)}, f32[2,512]{1,0:T(2,128)S(1)}, /*in...) while((s32[]{:T(128)}, f32[2,512,2048]{2,1,0:T(8,128)}, ...), condition=%wide.region_29.30_spmd, body=%wide.region_24.29_spmd.sunk | while | flops 5392564224 | bytes 214006864 | solution.py:289
  326.2 24.5 %conditional.8 = (f32[2,512,2048]{2,1,0:T(8,128)}, f32[2,2048]{1,0:T(2,128)S(1)}, f32[2,2048,512]{2,1,0:T(8,128)}, f32[2,512]{1,0:T(2,128)S(1)}, bf16[1,512,512]{2,1,0:T(8,128)(2,1)S(1)}) conditional(s32[]{:T(128)} %bitcast.441, (f32[2,512,2048]{2,1,0:T(8,128)}, f32[2,2048]{1,0:T(2,128)S(1)}, f32[2,2048,512]{2,1,0:T(8,128)}, ...), branch_computations={%region_25.25_spmd, %region_26.28_spmd} | conditional | flops 5392564224 | bytes 212957504 | solution.py:281
  352.7 24.5 %conditional.8 = (f32[2,512,2048]{2,1,0:T(8,128)}, f32[2,2048]{1,0:T(2,128)S(1)}, f32[2,2048,512]{2,1,0:T(8,128)}, f32[2,512]{1,0:T(2,128)S(1)}, bf16[1,512,512]{2,1,0:T(8,128)(2,1)S(1)}) conditional(s32[]{:T(128)} %bitcast.441, (f32[2,512,2048]{2,1,0:T(8,128)}, f32[2,2048]{1,0:T(2,128)S(1)}, f32[2,2048,512]{2,1,0:T(8,128)}, ...), branch_computations={%region_25.25_spmd, %region_26.28_spmd} | conditional | flops 5392564224 | bytes 212957504 | solution.py:281
  379.3 24.5 %conditional.8 = (f32[2,512,2048]{2,1,0:T(8,128)}, f32[2,2048]{1,0:T(2,128)S(1)}, f32[2,2048,512]{2,1,0:T(8,128)}, f32[2,512]{1,0:T(2,128)S(1)}, bf16[1,512,512]{2,1,0:T(8,128)(2,1)S(1)}) conditional(s32[]{:T(128)} %bitcast.441, (f32[2,512,2048]{2,1,0:T(8,128)}, f32[2,2048]{1,0:T(2,128)S(1)}, f32[2,2048,512]{2,1,0:T(8,128)}, ...), branch_computations={%region_25.25_spmd, %region_26.28_spmd} | conditional | flops 5392564224 | bytes 212957504 | solution.py:281
  405.9 24.5 %conditional.8 = (f32[2,512,2048]{2,1,0:T(8,128)}, f32[2,2048]{1,0:T(2,128)S(1)}, f32[2,2048,512]{2,1,0:T(8,128)}, f32[2,512]{1,0:T(2,128)S(1)}, bf16[1,512,512]{2,1,0:T(8,128)(2,1)S(1)}) conditional(s32[]{:T(128)} %bitcast.441, (f32[2,512,2048]{2,1,0:T(8,128)}, f32[2,2048]{1,0:T(2,128)S(1)}, f32[2,2048,512]{2,1,0:T(8,128)}, ...), branch_computations={%region_25.25_spmd, %region_26.28_spmd} | conditional | flops 5392564224 | bytes 212957504 | solution.py:281
  443.8 47.3 %while.92 = (s32[]{:T(128)}, bf16[4,512,2048]{2,1,0:T(8,128)(2,1)}, pred[4]{0:T(512)(128)(4,1)S(1)}, bf16[4,512,512]{2,1,0:T(8,128)(2,1)}, s32[4]{0:T(128)S(1)},...) while((s32[]{:T(128)}, bf16[4,512,2048]{2,1,0:T(8,128)(2,1)}, ...), condition=%wide.region_19.20_spmd, body=%wide.region_16.19_spmd.sunk | while | flops 1080033280 | bytes 8938694 | solution.py:218
  445.1 7.4 conditional.6
  456.8 7.4 conditional.6
  468.6 7.4 conditional.6
  480.5 7.4 conditional.6
  492.6 33.0 %while.93 = (s32[]{:T(128)}, bf16[4,512,512]{2,1,0:T(8,128)(2,1)}, pred[4]{0:T(512)(128)(4,1)S(1)}, bf16[4,512,2048]{2,1,0:T(8,128)(2,1)}, s32[4]{0:T(128)S(1)},...) while((s32[]{:T(128)}, bf16[4,512,512]{2,1,0:T(8,128)(2,1)}, ...), condition=%wide.region_23.24_spmd, body=%wide.region_20.23_spmd.sunk | while | flops 1074266112 | bytes 5774534 | solution.py:226
  493.9 6.0 conditional.7
  502.0 6.0 conditional.7
  510.1 6.6 conditional.7
  548.8 28.7 %all-to-all-done.1 = bf16[4,512,512]{2,1,0:T(8,128)(2,1)} async-done(((bf16[4,512,512]{2,1,0:T(8,128)(2,1)}), bf16[4,512,512]{2,1,0:T(8,128)(2,1)}, u32[]{:S(2)}, u32[]{:S(2)}) %all-to-all-start.1) | async-done | bytes 2097184 | tf_op jit(solution)/shard_map/all_to_all | solution.py:227
  595.2 6.3 reshape.518
  611.7 80.4 %while.95 = (s32[]{:T(128)}, bf16[4,512,8,64]{1,3,2,0:T(8,128)(2,1)}, bf16[4,512,8,64]{1,3,2,0:T(8,128)(2,1)}, bf16[4,512,8,64]{1,3,2,0:T(8,128)(2,1)}, bf16[4,5...) while((s32[]{:T(128)}, ...), condition=%wide.region_34.35_spmd, body=%wide.region_32.34_spmd.sunk | while | flops 1374941184 | bytes 77976720 | solution.py:320
  707.1 6.1 reshape.519
  723.4 80.5 %while.96 = (s32[]{:T(128)}, bf16[4,512,8,64]{1,3,2,0:T(8,128)(2,1)}, bf16[4,512,8,64]{1,3,2,0:T(8,128)(2,1)}, bf16[4,512,8,64]{1,3,2,0:T(8,128)(2,1)}, bf16[4,5...) while((s32[]{:T(128)}, ...), condition=%wide.region_39.40_spmd, body=%wide.region_37.39_spmd.sunk | while | flops 1374941184 | bytes 77976720 | solution.py:344
  865.8 40.4 %all-reduce = (f32[512]{0:T(512)}, f32[512]{0:T(512)}, f32[512]{0:T(512)}, f32[512]{0:T(512)}, f32[512]{0:T(512)}, /*index=5*/f32[512]{0:T(512)}, f32[512]{0:T(5...) all-reduce(f32[512]{0:T(512)S(1)} %get-tuple-element.806, ...), channel_id=1, replica_groups=mesh['expert'=4,'dp'=8] {'expert','dp'}, use_global_device_ids=true, to_apply=%region_43.44 | all-reduce | flops 6144 | bytes 49152 | tf_op jit(solution)/shard_map/psum | solution.py:362
  924.3 110.1 %all-reduce.4.cloned.1.call-done = (f32[512,512]{1,0:T(8,128)}, f32[512,512]{1,0:T(8,128)}, f32[512,512]{1,0:T(8,128)}, f32[512,512]{1,0:T(8,128)}, f32[512,512]...) async-done(((f32[512,512]{1,0:T(8,128)}, f32[512,512]{1,0:T(8,128)}, f32[512,512]{1,0:T(8,128)}, f32[512,512]{1,0:T(8,128)}, ...) | async-done | bytes 8388624 | tf_op jit(solution)/shard_map/psum | solution.py:362
  (698 shorter events, 688.3 us)
Async XLA Ops:
  8.0 117.9 %copy-start = (bf16[4,512,512]{2,1,0:T(8,128)(2,1)S(1)}, bf16[4,512,512]{2,1,0:T(8,128)(2,1)}, u32[]{:S(2)}) copy-start(bf16[4,512,512]{2,1,0:T(8,128)(2,1)} %param.51) | copy-start | bytes 6291460
  8.1 7.2 copy-start.94
  8.1 7.2 copy-start.101
  8.2 7.1 copy-start.9
  9.1 8.6 copy-start.58
  9.1 8.6 copy-start.123
  14.7 90.1 %copy-start.65 = (f32[1,4,4,128]{3,1,2,0:T(4,128)}, f32[1,4,4,128]{3,1,2,0:T(4,128)S(1)}, u32[]{:S(2)}) copy-start(f32[1,4,4,128]{3,1,2,0:T(4,128)S(1)} %copy.225) | copy-start | bytes 24580
  197.2 6.2 copy-start.70
  203.4 14.5 %copy-start.110 = (s32[4]{0:T(128)}, s32[4]{0:T(128)S(1)}, u32[]{:S(2)}) copy-start(s32[4]{0:T(128)S(1)} %and_select_fusion) | copy-start | bytes 52
  205.8 8.1 copy-start.79
  205.8 8.1 copy-start.83
  205.8 8.1 copy-start.95
  205.8 8.1 copy-start.97
  205.8 8.1 copy-start.102
  207.5 54.6 %all-to-all-start = ((bf16[4,512,512]{2,1,0:T(8,128)(2,1)}), bf16[4,512,512]{2,1,0:T(8,128)(2,1)}, u32[]{:S(2)}, u32[]{:S(2)}) async-start(bf16[4,512,512]{2,1,0:T(8,128)(2,1)} %copy.167), calls=%async_computation | async-start | bytes 4194304 | tf_op jit(solution)/shard_map/all_to_all | solution.py:221
  262.2 52.3 %all-to-all-start.2 = ((bf16[4,512,512]{2,1,0:T(8,128)(2,1)}), bf16[4,512,512]{2,1,0:T(8,128)(2,1)}, u32[]{:S(2)}, u32[]{:S(2)}) async-start(bf16[4,512,512]{2,1,0:T(8,128)(2,1)} %copy.172), calls=%async_computation.2 | async-start | bytes 4194304 | tf_op jit(solution)/shard_map/all_to_all | solution.py:248
  266.6 270.5 %reduce-scatter.15.cloned.1.call-start = ((), (), s32[]{:S(2)}) async-start(), calls=%async_computation.11 | async-start | bytes 147456
  328.7 6.8 slice-start
  342.0 6.0 copy-start.20
  355.3 6.8 slice-start
  381.9 6.8 slice-start
  408.4 6.8 slice-start
  432.0 106.4 %reduce-scatter.13.cloned.1.call-start = ((), (), s32[]{:S(2)}) async-start(), calls=%async_computation.10 | async-start | bytes 589824
  433.2 486.8 %reduce-scatter.9.cloned.1.call-start = ((), (), s32[]{:S(2)}) async-start(), calls=%async_computation.8 | async-start | bytes 4718592 | tf_op jit(solution)/shard_map/reduce_scatter | solution.py:299
  439.3 86.4 %all-to-all-start.3 = ((bf16[4,512,512]{2,1,0:T(8,128)(2,1)}), bf16[4,512,512]{2,1,0:T(8,128)(2,1)}, u32[]{:S(2)}, u32[]{:S(2)}) async-start(bf16[4,512,512]{2,1,0:T(8,128)(2,1)} %get-tuple-element.566), calls=%async_computation.3 | async-start | bytes 4194304 | tf_op jit(solution)/shard_map/all_to_all | solution.py:292
  443.8 48.8 %copy-start.98 = (f32[2,512]{1,0:T(2,128)S(1)}, f32[2,512]{1,0:T(2,128)}, u32[]{:S(2)}) copy-start(f32[2,512]{1,0:T(2,128)} %param.79) | copy-start | bytes 12292
  525.7 51.9 %all-to-all-start.1 = ((bf16[4,512,512]{2,1,0:T(8,128)(2,1)}), bf16[4,512,512]{2,1,0:T(8,128)(2,1)}, u32[]{:S(2)}, u32[]{:S(2)}) async-start(bf16[4,512,512]{2,1,0:T(8,128)(2,1)} %get-tuple-element.565), calls=%async_computation.1 | async-start | bytes 4194304 | tf_op jit(solution)/shard_map/all_to_all | solution.py:227
  530.7 391.5 %reduce-scatter.11.cloned.1.call-start = ((), (), s32[]{:S(2)}) async-start(), calls=%async_computation.9 | async-start | bytes 4718592 | tf_op jit(solution)/shard_map/reduce_scatter | solution.py:305
  536.6 497.8 %all-reduce.4.cloned.1.call-start = ((), (), s32[]{:S(2)}) async-start(), calls=%async_computation.12 | async-start | bytes 16777216 | tf_op jit(solution)/shard_map/psum | solution.py:362
  860.9 45.3 %copy-start.91 = (f32[1,4,4,128]{3,1,2,0:T(4,128)S(1)}, f32[1,4,4,128]{3,1,2,0:T(4,128)}, u32[]{:S(2)}) copy-start(f32[1,4,4,128]{3,1,2,0:T(4,128)} %copy-done.90) | copy-start | bytes 24580
  1036.9 8.4 copy-start.52
  1039.6 6.7 copy-start.51
  (139 other events, 484.2 us)
Sparse Core Ops, SparseCore 0:
  432.2 32.4 reduce-scatter.14
  468.6 34.2 reduce-scatter.12
  506.3 51.3 reduce-scatter.8
  561.2 51.3 reduce-scatter.10
Sparse Core Ops, SparseCore 1:
  853.9 180.4 all-reduce.3
where the time goes:
time: 1070 us; the launch traced here: 1060 us
  matrix products  344 us (32%)
  local copies, waits for them, and re-layouts  275 us (26%)
  waiting for transfers between devices  227 us (21%)
  other arithmetic  97.7 us (9%)
  blocking collectives  40.4 us (4%)
  loops' own time  34.1 us (3%)
  starting transfers between devices  20.9 us (2%)
  between operations  17 us (2%)
    psum x1, waiting for transfers between devices, on_device(): lax.psum((self_gain_grad, self_bias_grad, self_query_grad, self_key_grad,...  110 us
    dot_general x20, matrix products, linear(): return jnp.dot(inputs, weight, preferred_element_type=jnp.float32)  68 us
    unnamed x267, local copies, waits for them, and re-layouts  49.7 us
    reshape x8, local copies, waits for them, and re-layouts, split_heads(): return inputs.reshape(seq_count, -1, HEADS, HEAD_DIM)  49.2 us
    all_to_all x1, waiting for transfers between devices, on_device(): lax.all_to_all(send_grads, 'expert', split_axis=0, concat_axis=0, tiled=T...  47.5 us
    dot_general x16, matrix products, score_block(): jnp.einsum('qhd,khd->hqk', query_heads, key_heads, preferred_element_type...  42.6 us
    dot_general x16, matrix products, linear_back(): lax.dot_general(grads, weight, (((1,), (1,)), ((), ())), preferred_elemen...  42 us
    dot_general x16, matrix products, gradient_of_weight(): lax.dot_general(inputs, grads, (((0,), (0,)), ((), ())), preferred_elemen...  41.6 us
  transfers between devices with their start and end apart: 9, of which 4 were waited for; matrix products, arithmetic and copies ran while one was open for 37% of the time, Pallas kernels for 0%

commit v1 on v0

v1 whole, which is shorter than its diff:
```python
import functools

import jax
import jax.numpy as jnp
from jax import lax
from jax.experimental import pallas as pl
from jax.experimental.pallas import tpu as pltpu
from jax.sharding import PartitionSpec as P

HEADS = 8
HEAD_DIM = 64
PAIR = 2 * HEAD_DIM
EPSILON = 1e-05
SCORE_SCALE = 0.125
NEGATIVE = -1e30
LOG2E = 1.4426950408889634
LN2 = 0.6931471805599453
VMEM_LIMIT = 60 * 1024 * 1024
F32 = jnp.float32
BF16 = jnp.bfloat16


def contract(left, right, left_dim, right_dim):
    return lax.dot_general(
        left, right, (((left_dim,), (right_dim,)), ((), ())), preferred_element_type=F32
    )


def nn(left, right):
    return contract(left, right, 1, 0)


def nt(left, right):
    return contract(left, right, 1, 1)


def tn(left, right):
    return contract(left, right, 0, 0)


def normalise(rows):
    centre = rows - jnp.mean(rows, axis=-1, keepdims=True)
    inverse = lax.rsqrt(jnp.mean(centre * centre, axis=-1, keepdims=True) + EPSILON)
    return centre * inverse, inverse


def normalise_back(grad, normed, inverse, gain):
    scaled = grad * gain
    return inverse * (
        scaled
        - jnp.mean(scaled, axis=-1, keepdims=True)
        - normed * jnp.mean(scaled * normed, axis=-1, keepdims=True)
    )


def column_sum(rows):
    return jnp.sum(rows.astype(F32), axis=0, keepdims=True)


def head_masks():
    lane = lax.broadcasted_iota(jnp.int32, (1, PAIR), 1)
    mine = [(lane // HEAD_DIM == half).astype(F32).astype(BF16) for half in (0, 1)]
    spare = [(lane == HEAD_DIM * (1 - half)).astype(F32).astype(BF16) for half in (0, 1)]
    return mine, spare


def key_bias(count, mem_rows):
    place = lax.broadcasted_iota(jnp.int32, (mem_rows, PAIR), 0)
    return jnp.where(place < count, 0.0, NEGATIVE).astype(BF16)


def score_operands(keys, queries, half, mine, spare, bias):
    picked = queries * mine[half]
    if bias is None:
        return keys, picked
    return keys * (1 - spare[half]) + bias * spare[half], picked + spare[half]


def causal_scores(scores, query_start, block):
    last = scores.shape[0] - block
    key_at = lax.broadcasted_iota(jnp.int32, (block, block), 0)
    query_at = lax.broadcasted_iota(jnp.int32, (block, block), 1)
    edge = jnp.where(key_at <= query_at, scores[last:], NEGATIVE)
    return jnp.concatenate([scores[:last], edge], axis=0) if last else edge


def attend(query_ref, key_ref, value_t_ref, context_t_ref, logsum_ref, bias):
    length = query_ref.shape[0]
    block = length // 2
    mine, spare = head_masks()

    def pair_step(pair, carry):
        columns = pl.ds(pl.multiple_of(pair * PAIR, PAIR), PAIR)
        keys, queries = key_ref[:, columns], query_ref[:, columns]
        for half in (0, 1):
            rows = pl.ds(pl.multiple_of(pair * PAIR + half * HEAD_DIM, HEAD_DIM), HEAD_DIM)
            left, right = score_operands(keys, queries, half, mine, spare, bias)
            for part in (0, 1):
                place = slice(part * block, (part + 1) * block)
                reach = key_ref.shape[0] if bias is not None else (part + 1) * block
                scores = nt(left[:reach], right[place])
                if bias is None:
                    scores = causal_scores(scores, part * block, block)
                highest = jnp.max(scores, axis=0, keepdims=True)
                raised = jnp.exp2(scores - highest)
                summed = jnp.sum(raised, axis=0, keepdims=True)
                context = nn(value_t_ref[rows, :reach], raised.astype(BF16))
                context_t_ref[rows, place] = (context * (1.0 / summed)).astype(BF16)
                logsum_ref[pl.ds(2 * pair + half, 1), place] = highest + LOG2E * jnp.log(summed)
        return carry

    lax.fori_loop(0, HEADS // 2, pair_step, 0)


def attend_back(
    query_ref,
    key_ref,
    value_ref,
    key_t_ref,
    grad_ref,
    delta_ref,
    logsum_ref,
    grad_query_t_ref,
    grad_key_ref,
    grad_value_ref,
    bias,
):
    length = query_ref.shape[0]
    keys_all = key_ref.shape[0]
    block = length // 2
    mine, spare = head_masks()

    def pair_step(pair, carry):
        columns = pl.ds(pl.multiple_of(pair * PAIR, PAIR), PAIR)
        keys, queries, values = key_ref[:, columns], query_ref[:, columns], value_ref[:, columns]
        grads = grad_ref[:, columns]
        chances, slopes, picked_grads, picked_queries = {}, {}, [], []
        for half in (0, 1):
            head = pl.ds(2 * pair + half, 1)
            rows = pl.ds(pl.multiple_of(pair * PAIR + half * HEAD_DIM, HEAD_DIM), HEAD_DIM)
            left, right = score_operands(keys, queries, half, mine, spare, bias)
            grad_half = grads * mine[half]
            picked_grads.append(grad_half)
            picked_queries.append(queries * mine[half])
            for part in (0, 1):
                place = slice(part * block, (part + 1) * block)
                reach = keys_all if bias is not None else (part + 1) * block
                scores = nt(left[:reach], right[place])
                if bias is None:
                    scores = causal_scores(scores, part * block, block)
                chance = jnp.exp2(scores - logsum_ref[head, place])
                grad_chance = nt(values[:reach], grad_half[place])
                slope = (chance * (grad_chance - delta_ref[head, place])).astype(BF16)
                chances[half, part] = chance.astype(BF16)
                slopes[half, part] = slope
                grad_query_t_ref[rows, place] = (
                    nn(key_t_ref[rows, :reach], slope) * SCORE_SCALE
                ).astype(BF16)

        def gather(table, others):
            if bias is not None:
                wide = jnp.concatenate([table[h, p] for h in (0, 1) for p in (0, 1)], axis=1)
                return nn(wide, jnp.concatenate(others, axis=0))
            upper = jnp.concatenate([table[h, p][:block] for h in (0, 1) for p in (0, 1)], axis=1)
            lower = jnp.concatenate([table[h, 1][block:] for h in (0, 1)], axis=1)
            return jnp.concatenate(
                [
                    nn(upper, jnp.concatenate(others, axis=0)),
                    nn(lower, jnp.concatenate([item[block:] for item in others], axis=0)),
                ],
                axis=0,
            )

        grad_value_ref[:, columns] = gather(chances, picked_grads).astype(BF16)
        grad_key_ref[:, columns] = (gather(slopes, picked_queries) * LN2).astype(BF16)
        return carry

    lax.fori_loop(0, HEADS // 2, pair_step, 0)


def head_sums(grad, context_t):
    product = grad.T.astype(F32) * context_t.astype(F32)
    return jnp.sum(product.reshape(HEADS, HEAD_DIM, product.shape[1]), axis=1)


def valid_rows_of(count, length):
    return (lax.broadcasted_iota(jnp.int32, (length, 1), 0) < count).astype(F32)


def forward_kernel(
    order_ref,
    target_ref,
    memory_length_ref,
    tokens_ref,
    memory_ref,
    vectors_ref,
    self_query,
    self_key,
    self_value,
    self_out,
    cross_query,
    cross_key,
    cross_value,
    cross_out,
    normed_expert_ref,
    later_ref,
    middle_ref,
    query_one_ref,
    key_one_ref,
    value_one_ref,
    context_one_ref,
    logsum_one_ref,
    query_two_ref,
    key_two_ref,
    value_two_ref,
    context_two_ref,
    logsum_two_ref,
    value_t_ref,
):
    sequence = order_ref[pl.program_id(0)]
    length = tokens_ref.shape[1]
    vector = lambda at: vectors_ref[at : at + 1, :]
    start = tokens_ref[0].astype(F32) * valid_rows_of(target_ref[sequence], length)
    normed = (normalise(start)[0] * vector(0) + vector(1)).astype(BF16)
    scale = SCORE_SCALE * LOG2E
    query_one_ref[0] = ((nn(normed, self_query[...]) + vector(2)) * scale).astype(BF16)
    key_one_ref[0] = nn(normed, self_key[...]).astype(BF16)
    value = (nn(normed, self_value[...]) + vector(3)).astype(BF16)
    value_one_ref[0] = value
    value_t_ref[...] = value.T
    attend(
        query_one_ref.at[0],
        key_one_ref.at[0],
        value_t_ref,
        context_one_ref.at[0],
        logsum_one_ref.at[0],
        None,
    )
    middle = start + tn(context_one_ref[0], self_out[...]) + vector(4)
    middle_ref[0] = middle
    normed = (normalise(middle)[0] * vector(5) + vector(6)).astype(BF16)
    memory = memory_ref[0]
    query_two_ref[0] = ((nn(normed, cross_query[...]) + vector(7)) * scale).astype(BF16)
    key_two_ref[0] = nn(memory, cross_key[...]).astype(BF16)
    value = (nn(memory, cross_value[...]) + vector(8)).astype(BF16)
    value_two_ref[0] = value
    value_t_ref[...] = value.T
    attend(
        query_two_ref.at[0],
        key_two_ref.at[0],
        value_t_ref,
        context_two_ref.at[0],
        logsum_two_ref.at[0],
        key_bias(memory_length_ref[sequence], memory.shape[0]),
    )
    later = middle_ref[0] + tn(context_two_ref[0], cross_out[...]) + vector(9)
    later_ref[0] = later
    normed_expert_ref[0] = (normalise(later)[0] * vector(10) + vector(11)).astype(BF16)


def silu_parts(pre):
    gate = 1.0 / (1.0 + jnp.exp2(pre * -LOG2E))
    return gate, pre * gate


def expert_kernel(
    pick_ref,
    used_ref,
    rows_ref,
    grads_ref,
    weight_in,
    bias_in,
    weight_out,
    bias_out,
    hidden_ref,
    grad_pre_ref,
    made_ref,
    grad_rows_ref,
    made_sum,
    grad_sum,
):
    tile = pl.program_id(0)
    last = pl.num_programs(0) - 1
    used = used_ref[0] > 0

    @pl.when(used)
    def _():
        pre = nn(rows_ref[...], weight_in[0]) + bias_in[0]
        gate, active = silu_parts(pre)
        hidden = active.astype(BF16)
        hidden_ref[...] = hidden
        grad_hidden = nt(grads_ref[...], weight_out[0]).astype(BF16).astype(F32)
        grad_pre = (grad_hidden * (gate * (1.0 + pre * (1.0 - gate)))).astype(BF16)
        grad_pre_ref[...] = grad_pre
        made = nn(hidden, weight_out[0])
        grad_rows = nt(grad_pre, weight_in[0])

        @pl.when(tile == 0)
        def _():
            made_sum[...] = made
            grad_sum[...] = grad_rows

        @pl.when(tile > 0)
        def _():
            made_sum[...] += made
            grad_sum[...] += grad_rows

        @pl.when(tile == last)
        def _():
            made_ref[...] = (made_sum[...] + bias_out[0]).astype(BF16)
            grad_rows_ref[...] = grad_sum[...].astype(BF16)

    @pl.when(jnp.logical_not(used))
    def _():
        hidden_ref[...] = jnp.zeros_like(hidden_ref)
        grad_pre_ref[...] = jnp.zeros_like(grad_pre_ref)
        made_ref[...] = jnp.zeros_like(made_ref)
        grad_rows_ref[...] = jnp.zeros_like(grad_rows_ref)


def expert_weights_kernel(slots, pick_ref, used_ref, *refs):
    rows, grads = refs[:slots], refs[slots : 2 * slots]
    hidden, grad_pre = refs[2 * slots : 3 * slots], refs[3 * slots : 4 * slots]
    in_ref, out_ref, in_bias_ref, out_bias_ref, in_sum, out_sum, in_bias, out_bias = refs[4 * slots :]
    for total in (in_sum, out_sum, in_bias, out_bias):
        total[...] = jnp.zeros_like(total)
    for slot in range(slots):

        @pl.when(used_ref[slot] > 0)
        def _():
            pick = pick_ref[slot]
            in_sum[pick] += tn(rows[slot][...], grad_pre[slot][...])
            out_sum[pick] += tn(hidden[slot][...], grads[slot][...])
            in_bias[pick] += column_sum(grad_pre[slot][...])
            out_bias[pick] += column_sum(grads[slot][...])

    in_ref[...] = in_sum[...].astype(BF16)
    out_ref[...] = out_sum[...].astype(BF16)
    in_bias_ref[...] = in_bias[...]
    out_bias_ref[...] = out_bias[...]


def output_kernel(slots, order_ref, target_ref, later_ref, *refs):
    made, output_ref = refs[:slots], refs[slots]
    position = pl.program_id(0)
    valid = valid_rows_of(target_ref[order_ref[position]], later_ref.shape[1])
    for at in range(slots):

        @pl.when(position == at)
        def _():
            output_ref[0] = ((later_ref[0] + made[at][...].astype(F32)) * valid).astype(BF16)


def cross_back_kernel(slots, order_ref, target_ref, memory_length_ref, *refs):
    grad_normed = refs[:slots]
    (
        cotangent_ref,
        memory_ref,
        later_ref,
        middle_ref,
        query_ref,
        key_ref,
        value_ref,
        context_ref,
        logsum_ref,
        vectors_ref,
        cross_query,
        cross_key,
        cross_value,
        cross_out,
        grad_middle_ref,
        memory_grad_ref,
        weights_ref,
        sums_ref,
        weight_sum,
        grad_expert,
        key_t,
        grad_context,
        delta,
        grad_query_t,
        grad_key,
        grad_value,
    ) = refs[slots:]
    position = pl.program_id(0)
    sequence = order_ref[position]
    length = cotangent_ref.shape[1]
    vector = lambda at: vectors_ref[at : at + 1, :]

    @pl.when(position == 0)
    def _():
        weight_sum[...] = jnp.zeros_like(weight_sum)
        sums_ref[...] = jnp.zeros_like(sums_ref)

    for at in range(slots):

        @pl.when(position == at)
        def _():
            grad_expert[...] = grad_normed[at][...]

    def add_vector(at, value):
        sums_ref[at : at + 1, :] += value

    valid = valid_rows_of(target_ref[sequence], length)
    normed, inverse = normalise(later_ref[0])
    grad = grad_expert[...].astype(F32)
    add_vector(0, column_sum(grad * normed))
    add_vector(1, column_sum(grad))
    grad_later = cotangent_ref[0].astype(F32) * valid + normalise_back(
        grad, normed, inverse, vector(10)
    )
    branch = grad_later.astype(BF16)
    grad_middle_ref[0] = grad_later
    add_vector(2, column_sum(branch))
    weight_sum[3] += nn(context_ref[0], branch)
    context_grad = nt(branch, cross_out[...]).astype(BF16)
    grad_context[...] = context_grad
    delta[...] = head_sums(context_grad, context_ref[0])
    key_t[...] = key_ref[0].T
    attend_back(
        query_ref.at[0],
        key_ref.at[0],
        value_ref.at[0],
        key_t,
        grad_context,
        delta,
        logsum_ref.at[0],
        grad_query_t,
        grad_key,
        grad_value,
        key_bias(memory_length_ref[sequence], memory_ref.shape[1]),
    )
    memory_t = memory_ref[0].T
    weight_sum[1] += nn(memory_t, grad_key[...])
    weight_sum[2] += nn(memory_t, grad_value[...])
    add_vector(3, column_sum(grad_value[...]))
    memory_grad_ref[0] = nt(grad_key[...], cross_key[...]) + nt(grad_value[...], cross_value[...])
    normed, inverse = normalise(middle_ref[0])
    weight_sum[0] += nn(grad_query_t[...], (normed * vector(5) + vector(6)).astype(BF16))
    grad_query = grad_query_t[...].T
    add_vector(4, column_sum(grad_query))
    grad = nt(grad_query, cross_query[...])
    add_vector(5, column_sum(grad * normed))
    add_vector(6, column_sum(grad))
    grad_middle_ref[0] += normalise_back(grad, normed, inverse, vector(5))

    @pl.when(position == pl.num_programs(0) - 1)
    def _():
        width = weight_sum.shape[1]
        weights_ref[:width] = weight_sum[0].T.astype(BF16)
        for at in (1, 2, 3):
            weights_ref[at * width : (at + 1) * width] = weight_sum[at].astype(BF16)


def self_back_kernel(
    order_ref,
    target_ref,
    tokens_ref,
    grad_middle_ref,
    query_ref,
    key_ref,
    value_ref,
    context_ref,
    logsum_ref,
    vectors_ref,
    self_query,
    self_key,
    self_value,
    self_out,
    tokens_grad_ref,
    weights_ref,
    sums_ref,
    weight_sum,
    key_t,
    grad_context,
    delta,
    grad_query_t,
    grad_key,
    grad_value,
):
    position = pl.program_id(0)
    sequence = order_ref[position]
    length = tokens_ref.shape[1]
    vector = lambda at: vectors_ref[at : at + 1, :]

    @pl.when(position == 0)
    def _():
        weight_sum[...] = jnp.zeros_like(weight_sum)
        sums_ref[...] = jnp.zeros_like(sums_ref)

    def add_vector(at, value):
        sums_ref[at : at + 1, :] += value

    valid = valid_rows_of(target_ref[sequence], length)
    branch = grad_middle_ref[0].astype(BF16)
    add_vector(0, column_sum(branch))
    weight_sum[3] += nn(context_ref[0], branch)
    context_grad = nt(branch, self_out[...]).astype(BF16)
    grad_context[...] = context_grad
    delta[...] = head_sums(context_grad, context_ref[0])
    key_t[...] = key_ref[0].T
    attend_back(
        query_ref.at[0],
        key_ref.at[0],
        value_ref.at[0],
        key_t,
        grad_context,
        delta,
        logsum_ref.at[0],
        grad_query_t,
        grad_key,
        grad_value,
        None,
    )
    normed, inverse = normalise(tokens_ref[0].astype(F32) * valid)
    inputs = (normed * vector(0) + vector(1)).astype(BF16)
    inputs_t = inputs.T
    weight_sum[0] += nn(grad_query_t[...], inputs)
    weight_sum[1] += nn(inputs_t, grad_key[...])
    weight_sum[2] += nn(inputs_t, grad_value[...])
    grad_query = grad_query_t[...].T
    add_vector(1, column_sum(grad_query))
    add_vector(2, column_sum(grad_value[...]))
    grad = (
        nt(grad_query, self_query[...])
        + nt(grad_key[...], self_key[...])
        + nt(grad_value[...], self_value[...])
    )
    add_vector(3, column_sum(grad * normed))
    add_vector(4, column_sum(grad))
    tokens_grad_ref[0] = (
        grad_middle_ref[0] + normalise_back(grad, normed, inverse, vector(0))
    ) * valid

    @pl.when(position == pl.num_programs(0) - 1)
    def _():
        width = weight_sum.shape[1]
        weights_ref[:width] = weight_sum[0].T.astype(BF16)
        for at in (1, 2, 3):
            weights_ref[at * width : (at + 1) * width] = weight_sum[at].astype(BF16)


def params(dims=1):
    return pltpu.CompilerParams(
        dimension_semantics=("arbitrary",) * dims, vmem_limit_bytes=VMEM_LIMIT
    )


def fixed(shape):
    return pl.BlockSpec(shape, lambda *_: (0,) * len(shape))


def at_position(shape):
    return pl.BlockSpec((1,) + shape, lambda step, *_: (step,) + (0,) * len(shape))


def at_sequence(shape):
    return pl.BlockSpec((1,) + shape, lambda step, order, *_: (order[step],) + (0,) * len(shape))


def struct(shape, kind):
    return jax.ShapeDtypeStruct(shape, kind)


def halves_step(parts, axis, bit):
    size = lax.axis_size(axis)
    route = [(place, place ^ bit) for place in range(size)]
    high = (lax.axis_index(axis) // bit) % 2
    kept = []
    for part in parts:
        half = part.shape[0] // 2
        given = lax.dynamic_slice_in_dim(part, (1 - high) * half, half, 0)
        mine = lax.dynamic_slice_in_dim(part, high * half, half, 0)
        got = lax.ppermute(given, axis, route)
        kept.append((mine.astype(F32) + got.astype(F32)).astype(BF16))
    return kept


def join_step(parts, axis, bit):
    size = lax.axis_size(axis)
    route = [(place, place ^ bit) for place in range(size)]
    high = (lax.axis_index(axis) // bit) % 2
    joined = []
    for part in parts:
        got = lax.ppermute(part, axis, route)
        low = jnp.where(high == 0, part, got)
        top = jnp.where(high == 0, got, part)
        joined.append(jnp.concatenate([low, top], axis=0))
    return joined


def bits_of(axis):
    return [1 << at for at in range(lax.axis_size(axis).bit_length() - 1)]


def sum_everywhere(rows):
    steps = [("dp", bit) for bit in bits_of("dp")] + [("expert", bit) for bit in bits_of("expert")]
    parts = [rows]
    for axis, bit in steps:
        parts = halves_step(parts, axis, bit)
    for axis, bit in steps[::-1]:
        parts = join_step(parts, axis, bit)
    return parts[0]


def on_device(
    tokens,
    memory,
    cotangent,
    target_length,
    memory_length,
    expert_of,
    self_norm_gain,
    self_norm_bias,
    self_query,
    self_key,
    self_value,
    self_out,
    self_query_bias,
    self_value_bias,
    self_out_bias,
    cross_norm_gain,
    cross_norm_bias,
    cross_query,
    cross_key,
    cross_value,
    cross_out,
    cross_attention_query_bias,
    cross_value_bias,
    cross_out_bias,
    expert_norm_gain,
    expert_norm_bias,
    expert_in,
    expert_in_bias,
    expert_out,
    expert_out_bias,
):
    seqs, length, width = tokens.shape
    mem_rows = memory.shape[1]
    local_count, _, hidden_width = expert_in.shape
    groups = lax.axis_size("expert")
    places = lax.axis_size("dp")
    own_group = lax.axis_index("expert")
    column = lax.axis_index("dp")

    shifts = [2, 1, 3, 0] if groups == 4 else [s for s in range(1, groups)] + [0]
    id_table = expert_of.reshape(groups, places, seqs)
    column_ids = lax.dynamic_index_in_dim(id_table, column, 1, False)
    own_ids = lax.dynamic_index_in_dim(column_ids, own_group, 0, False)
    distance = (own_ids // local_count - own_group) % groups
    shift_rank = jnp.zeros((groups,), jnp.int32).at[jnp.array(shifts)].set(jnp.arange(groups))
    rank = shift_rank[distance]
    position_of = jnp.sum(rank[:, None] > rank[None, :], axis=1).astype(jnp.int32)
    order = jnp.sum(
        jnp.where(position_of[None, :] == jnp.arange(seqs)[:, None], jnp.arange(seqs)[None, :], 0),
        axis=1,
    ).astype(jnp.int32)
    arriving = column_ids // local_count == own_group
    from_group_pick = jnp.sum(jnp.where(arriving, column_ids % local_count, 0), axis=1)
    from_group_used = jnp.any(arriving, axis=1)
    source = (own_group - jnp.array(shifts)) % groups
    picks = from_group_pick[source].astype(jnp.int32)
    used = from_group_used[source].astype(jnp.int32)
    whole = groups == seqs
    position_distance = distance[order]

    def outgoing(stack, slot):
        if whole:
            return stack[slot]
        match = position_distance == shifts[slot]
        return lax.dynamic_index_in_dim(stack, jnp.argmax(match), 0, False)

    def move(rows, slot, back=False):
        shift = shifts[slot]
        if shift == 0:
            return rows
        turn = -shift if back else shift
        return lax.ppermute(rows, "expert", [(g, (g + turn) % groups) for g in range(groups)])

    def arranged(per_slot):
        if whole:
            return per_slot
        stack = jnp.stack(per_slot)
        slot_at = shift_rank[position_distance]
        return [lax.dynamic_index_in_dim(stack, slot_at[at], 0, False) for at in range(seqs)]

    vectors = jnp.stack(
        [
            self_norm_gain,
            self_norm_bias,
            self_query_bias,
            self_value_bias,
            self_out_bias,
            cross_norm_gain,
            cross_norm_bias,
            cross_attention_query_bias,
            cross_value_bias,
            cross_out_bias,
            expert_norm_gain,
            expert_norm_bias,
        ]
        + [jnp.zeros_like(self_norm_gain)] * 4
    )
    rows_shape, square = (length, width), (width, width)
    mem_shape, heads_shape = (mem_rows, width), (HEADS, length)
    weights = [fixed(square)] * 4

    grads_home = (
        cotangent
        * (lax.broadcasted_iota(jnp.int32, cotangent.shape, 1) < target_length[:, None, None])
    )[order]
    grads_in = [move(outgoing(grads_home, slot), slot) for slot in range(groups)]

    saved = [
        (rows_shape, BF16),
        (rows_shape, F32),
        (rows_shape, F32),
        (rows_shape, BF16),
        (rows_shape, BF16),
        (rows_shape, BF16),
        ((width, length), BF16),
        (heads_shape, F32),
        (rows_shape, BF16),
        (mem_shape, BF16),
        (mem_shape, BF16),
        ((width, length), BF16),
        (heads_shape, F32),
    ]
    (
        normed_expert,
        later,
        middle,
        query_one,
        key_one,
        value_one,
        context_one,
        logsum_one,
        query_two,
        key_two,
        value_two,
        context_two,
        logsum_two,
    ) = pl.pallas_call(
        forward_kernel,
        grid_spec=pltpu.PrefetchScalarGridSpec(
            num_scalar_prefetch=3,
            grid=(seqs,),
            in_specs=[at_sequence(rows_shape), at_sequence(mem_shape), fixed(vectors.shape)]
            + weights
            + weights,
            out_specs=[at_position(shape) for shape, _ in saved],
            scratch_shapes=[pltpu.VMEM((width, length), BF16)],
        ),
        out_shape=[struct((seqs,) + shape, kind) for shape, kind in saved],
        compiler_params=params(),
        name="forward",
    )(
        order,
        target_length,
        memory_length,
        tokens,
        memory,
        vectors,
        self_query,
        self_key,
        self_value,
        self_out,
        cross_query,
        cross_key,
        cross_value,
        cross_out,
    )

    rows_in = [move(outgoing(normed_expert, slot), slot) for slot in range(groups)]
    tiles = 4
    tile_width = hidden_width // tiles
    in_tile = pl.BlockSpec((1, width, tile_width), lambda t, pick, _: (pick[0], 0, t))
    out_tile = pl.BlockSpec((1, tile_width, width), lambda t, pick, _: (pick[0], t, 0))
    hidden_tile = pl.BlockSpec((length, tile_width), lambda t, *_: (0, t))
    hidden, grad_pre, made, grad_rows = [], [], [], []
    for slot in range(groups):
        results = pl.pallas_call(
            expert_kernel,
            grid_spec=pltpu.PrefetchScalarGridSpec(
                num_scalar_prefetch=2,
                grid=(tiles,),
                in_specs=[
                    fixed(rows_shape),
                    fixed(rows_shape),
                    in_tile,
                    pl.BlockSpec((1, 1, tile_width), lambda t, pick, _: (pick[0], 0, t)),
                    out_tile,
                    pl.BlockSpec((1, 1, width), lambda t, pick, _: (pick[0], 0, 0)),
                ],
                out_specs=[hidden_tile, hidden_tile, fixed(rows_shape), fixed(rows_shape)],
                scratch_shapes=[pltpu.VMEM(rows_shape, F32)] * 2,
            ),
            out_shape=[struct((length, hidden_width), BF16)] * 2 + [struct(rows_shape, BF16)] * 2,
            compiler_params=params(),
            name="expert",
        )(
            picks[slot : slot + 1],
            used[slot : slot + 1],
            rows_in[slot],
            grads_in[slot],
            expert_in,
            expert_in_bias[:, None, :],
            expert_out,
            expert_out_bias[:, None, :],
        )
        for table, result in zip((hidden, grad_pre, made, grad_rows), results):
            table.append(result)

    grad_home = arranged([move(grad_rows[slot], slot, True) for slot in range(groups)])
    made_home = arranged([move(made[slot], slot, True) for slot in range(groups)])

    in_sums, out_sums, in_bias_sums, out_bias_sums = pl.pallas_call(
        functools.partial(expert_weights_kernel, groups),
        grid_spec=pltpu.PrefetchScalarGridSpec(
            num_scalar_prefetch=2,
            grid=(tiles,),
            in_specs=[fixed(rows_shape)] * (2 * groups) + [hidden_tile] * (2 * groups),
            out_specs=[
                pl.BlockSpec((local_count, width, tile_width), lambda t, *_: (0, 0, t)),
                pl.BlockSpec((local_count, tile_width, width), lambda t, *_: (0, t, 0)),
                pl.BlockSpec((local_count, 1, tile_width), lambda t, *_: (0, 0, t)),
                fixed((local_count, 1, width)),
            ],
            scratch_shapes=[
                pltpu.VMEM((local_count, width, tile_width), F32),
                pltpu.VMEM((local_count, tile_width, width), F32),
                pltpu.VMEM((local_count, 1, tile_width), F32),
                pltpu.VMEM((local_count, 1, width), F32),
            ],
        ),
        out_shape=[
            struct((local_count, width, hidden_width), BF16),
            struct((local_count, hidden_width, width), BF16),
            struct((local_count, 1, hidden_width), F32),
            struct((local_count, 1, width), F32),
        ],
        compiler_params=params(),
        name="expert_weights",
    )(picks, used, *rows_in, *grads_in, *hidden, *grad_pre)
    expert_in_grad = lax.psum_scatter(in_sums, "dp", scatter_dimension=1, tiled=True)
    expert_out_grad = lax.psum_scatter(out_sums, "dp", scatter_dimension=1, tiled=True)

    back_scratch = [
        pltpu.VMEM((4,) + square, F32),
        pltpu.VMEM((width, mem_rows), BF16),
        pltpu.VMEM(rows_shape, BF16),
        pltpu.VMEM(heads_shape, F32),
        pltpu.VMEM((width, length), BF16),
        pltpu.VMEM(mem_shape, BF16),
        pltpu.VMEM(mem_shape, BF16),
    ]
    grad_middle, memory_grad, cross_weights, cross_sums = pl.pallas_call(
        functools.partial(cross_back_kernel, seqs),
        grid_spec=pltpu.PrefetchScalarGridSpec(
            num_scalar_prefetch=3,
            grid=(seqs,),
            in_specs=[fixed(rows_shape)] * seqs
            + [
                at_sequence(rows_shape),
                at_sequence(mem_shape),
                at_position(rows_shape),
                at_position(rows_shape),
                at_position(rows_shape),
                at_position(mem_shape),
                at_position(mem_shape),
                at_position((width, length)),
                at_position(heads_shape),
                fixed(vectors.shape),
            ]
            + weights,
            out_specs=[
                at_position(rows_shape),
                at_sequence(mem_shape),
                fixed((4 * width, width)),
                fixed((8, width)),
            ],
            scratch_shapes=back_scratch[:1] + [pltpu.VMEM(rows_shape, BF16)] + back_scratch[1:],
        ),
        out_shape=[
            struct((seqs,) + rows_shape, F32),
            struct((seqs,) + mem_shape, F32),
            struct((4 * width, width), BF16),
            struct((8, width), F32),
        ],
        compiler_params=params(),
        name="cross_back",
    )(
        order,
        target_length,
        memory_length,
        *grad_home,
        cotangent,
        memory,
        later,
        middle,
        query_two,
        key_two,
        value_two,
        context_two,
        logsum_two,
        vectors,
        cross_query,
        cross_key,
        cross_value,
        cross_out,
    )
    cross_totals = sum_everywhere(cross_weights)

    tokens_grad, self_weights, self_sums = pl.pallas_call(
        self_back_kernel,
        grid_spec=pltpu.PrefetchScalarGridSpec(
            num_scalar_prefetch=2,
            grid=(seqs,),
            in_specs=[
                at_sequence(rows_shape),
                at_position(rows_shape),
                at_position(rows_shape),
                at_position(rows_shape),
                at_position(rows_shape),
                at_position((width, length)),
                at_position(heads_shape),
                fixed(vectors.shape),
            ]
            + weights,
            out_specs=[at_sequence(rows_shape), fixed((4 * width, width)), fixed((8, width))],
            scratch_shapes=back_scratch,
        ),
        out_shape=[
            struct((seqs,) + rows_shape, F32),
            struct((4 * width, width), BF16),
            struct((8, width), F32),
        ],
        compiler_params=params(),
        name="self_back",
    )(
        order,
        target_length,
        tokens,
        grad_middle,
        query_one,
        key_one,
        value_one,
        context_one,
        logsum_one,
        vectors,
        self_query,
        self_key,
        self_value,
        self_out,
    )
    self_totals = sum_everywhere(self_weights)
    output = pl.pallas_call(
        functools.partial(output_kernel, seqs),
        grid_spec=pltpu.PrefetchScalarGridSpec(
            num_scalar_prefetch=2,
            grid=(seqs,),
            in_specs=[at_position(rows_shape)] + [fixed(rows_shape)] * seqs,
            out_specs=[at_sequence(rows_shape)],
        ),
        out_shape=[struct((seqs,) + rows_shape, BF16)],
        compiler_params=params(),
        name="output",
    )(order, target_length, later, *made_home)[0]

    totals = lax.psum(jnp.concatenate([self_sums, cross_sums], axis=0), ("expert", "dp"))
    cross_q, cross_k, cross_v, cross_o = [
        cross_totals[at * width : (at + 1) * width].astype(F32) for at in range(4)
    ]
    self_q, self_k, self_v, self_o = [
        self_totals[at * width : (at + 1) * width].astype(F32) for at in range(4)
    ]
    bias_share = lax.psum_scatter(in_bias_sums[:, 0], "dp", scatter_dimension=1, tiled=True)
    out_bias_share = lax.psum_scatter(out_bias_sums[:, 0], "dp", scatter_dimension=1, tiled=True)
    return (
        output,
        tokens_grad,
        memory_grad,
        totals[3],
        totals[4],
        self_q,
        self_k,
        self_v,
        self_o,
        totals[1],
        totals[2],
        totals[0],
        totals[13],
        totals[14],
        cross_q,
        cross_k,
        cross_v,
        cross_o,
        totals[12],
        totals[11],
        totals[10],
        totals[8],
        totals[9],
        expert_in_grad.astype(F32),
        bias_share,
        expert_out_grad.astype(F32),
        out_bias_share,
    )


def solution(mesh):
    rows = P(("expert", "dp"), None, None)
    counts = P(("expert", "dp"))
    split = (P("expert", None, None), P("expert", None)) * 2
    shares = (P("expert", "dp", None), P("expert", "dp")) * 2
    return jax.shard_map(
        on_device,
        mesh=mesh,
        in_specs=(rows,) * 3 + (counts,) * 2 + (P(),) * 21 + split,
        out_specs=(rows,) * 3 + (P(),) * 20 + shares,
        check_vma=False,
    )
```

time: 1070 us -> 559 us (0.52)
  matrix products: 344 us -> 0 us
  local copies, waits for them, and re-layouts: 275 us -> 29.8 us
  Pallas kernels: 0 us -> 243 us
  other arithmetic: 97.7 us -> 22.5 us
  waiting for transfers between devices: 227 us -> 152 us
  loops' own time: 34.1 us -> 0 us
  starting transfers between devices: 20.9 us -> 52.2 us
    dot_general x112 -> x0, matrix products: 344 us -> none  [the longest x20 68 us: linear(): return jnp.dot(inputs, weight, preferred_element_type=jnp.float32)]
    pallas_call x0 -> x9, Pallas kernels: none -> 243 us  [the longest x1 71.3 us: on_device(): pl.pallas_call(forward_kernel, grid_spec=pltpu.PrefetchScalarGridSpec(num...]
    ppermute x0 -> x32, waiting for transfers between devices: none -> 151 us  [the longest x12 108 us: move(): lax.ppermute(rows, 'expert', [(g, (g + turn) % groups) for g in range(gro...]
    all_to_all x4 -> x0, waiting for transfers between devices: 116 us -> none  [the longest x1 47.5 us: on_device(): lax.all_to_all(send_grads, 'expert', split_axis=0, concat_axis=0, tiled=T...]
    psum x1 -> x0, waiting for transfers between devices: 110 us -> none  [on_device(): lax.psum((self_gain_grad, self_bias_grad, self_query_grad, self_key_grad,...]
    while x32 -> x0, local copies, waits for them, and re-layouts: 68.2 us -> none  [the longest x4 20.5 us: on_device(): lax.map(attend_one, (query_two, key_two, value_two, cross_allowed))]
    ppermute x0 -> x32, starting transfers between devices: none -> 52.1 us  [the longest x12 19.5 us: move(): lax.ppermute(rows, 'expert', [(g, (g + turn) % groups) for g in range(gro...]
    reshape x9 -> x1, local copies, waits for them, and re-layouts: 49.3 us -> 0.75 us  [on_device(): id_table = expert_of.reshape(groups, places, seqs)]
  transfers between devices with their start and end apart: 9 -> 36, of which waited for: 4 -> 18; matrix products, arithmetic and copies ran while one was open for 37% -> 7% of each run, Pallas kernels for 0% -> 25%
where the time goes in v1:
time: 559 us; the launch traced here: 552 us
  Pallas kernels  243 us (43%)
  waiting for transfers between devices  152 us (27%)
  starting transfers between devices  52.2 us (9%)
  blocking collectives  38.1 us (7%)
  local copies, waits for them, and re-layouts  29.8 us (5%)
  other arithmetic  22.5 us (4%)
  between operations  14.8 us (3%)
    ppermute x12, waiting for transfers between devices, move(): lax.ppermute(rows, 'expert', [(g, (g + turn) % groups) for g in range(gro...  108 us
    pallas_call x1, Pallas kernels, on_device(): pl.pallas_call(forward_kernel, grid_spec=pltpu.PrefetchScalarGridSpec(num...  71.3 us
    pallas_call x1, Pallas kernels, on_device(): pl.pallas_call(functools.partial(cross_back_kernel, seqs), grid_spec=pltp...  54.5 us
    pallas_call x1, Pallas kernels, on_device(): pl.pallas_call(self_back_kernel, grid_spec=pltpu.PrefetchScalarGridSpec(n...  46 us
    pallas_call x4, Pallas kernels, on_device(): pl.pallas_call(expert_kernel, grid_spec=pltpu.PrefetchScalarGridSpec(num_...  44.1 us
    psum x1, blocking collectives, on_device(): lax.psum(jnp.concatenate([self_sums, cross_sums], axis=0), ('expert', 'dp'))  38.1 us
    ppermute x10, waiting for transfers between devices, halves_step(): got = lax.ppermute(given, axis, route)  29 us
    pallas_call x1, Pallas kernels, on_device(): pl.pallas_call(functools.partial(expert_weights_kernel, groups), grid_spe...  20.8 us
  transfers between devices with their start and end apart: 36, of which 18 were waited for; matrix products, arithmetic and copies ran while one was open for 7% of the time, Pallas kernels for 25%

profile of v1, /device:TPU:0, one launch (start us, length us, event | category | flops | bytes accessed | tf_op | source)
XLA Modules:
  0.0 551.6 jit_solution(10605660428041750072)
XLA Ops:
  10.2 2.8 stack.55.vectors_ref.refs_13_
  12.9 71.3 %forward.1 = (bf16[4,512,512]{2,1,0:T(8,128)(2,1)}, f32[4,512,512]{2,1,0:T(8,128)}, f32[4,512,512]{2,1,0:T(8,128)}, bf16[4,512,512]{2,1,0:T(8,128)(2,1)}, bf16[4...) custom-call(s32[4]{0:T(128)} %select_reduce_fusion.order_ref, ...), custom_call_target="tpu_custom_call" | custom-call | tf_op jit(solution)/shard_map/forward/pallas_call | solution.py:742
  84.3 2.8 slice_bitcast_fusion.4
  87.1 3.0 collective-permute-start.3
  101.4 3.8 collective-permute-done.3.rows_ref.refs_1_
  109.5 11.0 %expert.7 = (bf16[512,2048]{1,0:T(8,128)(2,1)}, bf16[512,2048]{1,0:T(8,128)(2,1)}, bf16[512,512]{1,0:T(8,128)(2,1)}, bf16[512,512]{1,0:T(8,128)(2,1)}) custom-call(s32[1]{0:T(128)} %get-tuple-element.168.pick_ref, s32[1]{0:T(128)} %get-tuple-element.157.used_ref, bf16[512,512]{1,0:T(8,128)(2,1)} %get-tuple-element.117.rows_ref.refs_3_, ...), custom_call_target="tpu_custom_call" | custom-call | tf_op jit(solution)/shard_map/expert/pallas_call | solution.py:781
  121.4 11.0 %expert.5 = (bf16[512,2048]{1,0:T(8,128)(2,1)}, bf16[512,2048]{1,0:T(8,128)(2,1)}, bf16[512,512]{1,0:T(8,128)(2,1)}, bf16[512,512]{1,0:T(8,128)(2,1)}) custom-call(s32[1]{0:T(128)} %get-tuple-element.166.pick_ref, s32[1]{0:T(128)} %get-tuple-element.159.used_ref, bf16[512,512]{1,0:T(8,128)(2,1)} %copy-done.3, bf16[512,512]{1,0:T(8,128)(2,1)} %copy-done.4, ...), custom_call_target="tpu_custom_call" | custom-call | tf_op jit(solution)/shard_map/expert/pallas_call | solution.py:781
  132.4 5.6 %collective-permute-done.7.grads_ref.refs_6_ = bf16[512,512]{1,0:T(8,128)(2,1)S(1)} collective-permute-done((bf16[512,512]{1,0:T(8,128)(2,1)}, bf16[512,512]{1,0:T(8,128)(2,1)S(1)}, u32[]{:S(2)}, u32[]{:S(2)}) %collective-permute-start.7) | collective-permute-done | bytes 524320 | tf_op jit(solution)/shard_map/ppermute | solution.py:677
  138.8 11.1 %expert.6 = (bf16[512,2048]{1,0:T(8,128)(2,1)}, bf16[512,2048]{1,0:T(8,128)(2,1)}, bf16[512,512]{1,0:T(8,128)(2,1)}, bf16[512,512]{1,0:T(8,128)(2,1)}) custom-call(s32[1]{0:T(128)} %get-tuple-element.167.pick_ref, s32[1]{0:T(128)} %get-tuple-element.158.used_ref, bf16[512,512]{1,0:T(8,128)(2,1)} %copy-done.5, bf16[512,512]{1,0:T(8,128)(2,1)} %copy-done.6, ...), custom_call_target="tpu_custom_call" | custom-call | tf_op jit(solution)/shard_map/expert/pallas_call | solution.py:781
  149.9 21.9 %collective-permute-done.rows_ref.refs_0_ = bf16[512,512]{1,0:T(8,128)(2,1)S(1)} collective-permute-done((bf16[512,512]{1,0:T(8,128)(2,1)S(1)}, bf16[512,512]{1,0:T(8,128)(2,1)S(1)}, u32[]{:S(2)}, u32[]{:S(2)}) %collective-permute-start) | collective-permute-done | bytes 524320 | tf_op jit(solution)/shard_map/ppermute | solution.py:677
  171.8 11.2 %collective-permute-done.1.grads_ref.refs_4_ = bf16[512,512]{1,0:T(8,128)(2,1)} collective-permute-done((bf16[512,512]{1,0:T(8,128)(2,1)}, bf16[512,512]{1,0:T(8,128)(2,1)}, u32[]{:S(2)}, u32[]{:S(2)}) %collective-permute-start.1) | collective-permute-done | bytes 524320 | tf_op jit(solution)/shard_map/ppermute | solution.py:677
  183.0 11.0 %expert.4 = (bf16[512,2048]{1,0:T(8,128)(2,1)}, bf16[512,2048]{1,0:T(8,128)(2,1)}, bf16[512,512]{1,0:T(8,128)(2,1)}, bf16[512,512]{1,0:T(8,128)(2,1)}) custom-call(s32[1]{0:T(128)} %get-tuple-element.165.pick_ref, s32[1]{0:T(128)} %get-tuple-element.160.used_ref, bf16[512,512]{1,0:T(8,128)(2,1)} %copy-done.7, ...), custom_call_target="tpu_custom_call" | custom-call | tf_op jit(solution)/shard_map/expert/pallas_call | solution.py:781
  194.0 20.8 %expert_weights.1 = (bf16[2,512,2048]{2,1,0:T(8,128)(2,1)}, bf16[2,2048,512]{2,1,0:T(8,128)(2,1)}, f32[2,1,2048]{2,1,0:T(1,128)}, f32[2,1,512]{2,1,0:T(1,128)}) custom-call(s32[4]{0:T(128)} %copy-done.12, s32[4]{0:T(128)} %copy-done.17, bf16[512,512]{1,0:T(8,128)(2,1)} %copy-done.7, bf16[512,512]{1,0:T(8,128)(2,1)} %copy-done.3, bf16[512,512]{1,0:T(8,128)(2,1)} %copy-done.5, ...), custom_call_target="tpu_custom_call" | custom-call | tf_op jit(solution)/shard_map/expert_weights/pallas_call | solution.py:816
  222.2 3.7 collective-permute-start.9
  225.9 20.7 %collective-permute-done.10.refs_1_ = bf16[512,512]{1,0:T(8,128)(2,1)S(1)} collective-permute-done((bf16[512,512]{1,0:T(8,128)(2,1)S(1)}, bf16[512,512]{1,0:T(8,128)(2,1)S(1)}, u32[]{:S(2)}, u32[]{:S(2)}) %collective-permute-start.10) | collective-permute-done | bytes 524320 | tf_op jit(solution)/shard_map/ppermute | solution.py:677
  249.3 15.7 %collective-permute-done.9.refs_0_ = bf16[512,512]{1,0:T(8,128)(2,1)S(1)} collective-permute-done((bf16[512,512]{1,0:T(8,128)(2,1)S(1)}, bf16[512,512]{1,0:T(8,128)(2,1)S(1)}, u32[]{:S(2)}, u32[]{:S(2)}) %collective-permute-start.9) | collective-permute-done | bytes 524320 | tf_op jit(solution)/shard_map/ppermute | solution.py:677
  265.8 54.5 %cross_back.1 = (f32[4,512,512]{2,1,0:T(8,128)}, f32[4,512,512]{2,1,0:T(8,128)}, bf16[2048,512]{1,0:T(8,128)(2,1)}, f32[8,512]{1,0:T(8,128)}) custom-call(s32[4]{0:T(128)} %select_reduce_fusion.order_ref, s32[4]{0:T(128)} %target_ref.7, s32[4]{0:T(128)} %memory_length_ref.3, bf16[512,512]{1,0:T(8,128)(2,1)} %copy-done.11, bf16[512,512]{1,0:T(8,128)(2,1)} %copy-done.9, ...), custom_call_target="tpu_custom_call" | custom-call | tf_op jit(solution)/shard_map/cross_back/pallas_call | solution.py:856
  321.6 46.0 %self_back.1 = (f32[4,512,512]{2,1,0:T(8,128)}, bf16[2048,512]{1,0:T(8,128)(2,1)}, f32[8,512]{1,0:T(8,128)}) custom-call(s32[4]{0:T(128)} %select_reduce_fusion.order_ref, s32[4]{0:T(128)} %target_ref.7, bf16[4,512,512]{2,1,0:T(8,128)(2,1)} %tokens_ref.3, f32[4,512,512]{2,1,0:T(8,128)} %get-tuple-element.83.grad_middle_ref, ...), custom_call_target="tpu_custom_call" | custom-call | tf_op jit(solution)/shard_map/self_back/pallas_call | solution.py:913
  377.5 10.6 %collective-permute-done.23 = bf16[512,512]{1,0:T(8,128)(2,1)S(1)} collective-permute-done((bf16[512,512]{1,0:T(8,128)(2,1)}, bf16[512,512]{1,0:T(8,128)(2,1)S(1)}, u32[]{:S(2)}, u32[]{:S(2)}) %collective-permute-start.23) | collective-permute-done | bytes 524320 | tf_op jit(solution)/shard_map/ppermute | solution.py:573
  389.9 8.5 %collective-permute-done.13 = bf16[512,512]{1,0:T(8,128)(2,1)S(1)} collective-permute-done((bf16[512,512]{1,0:T(8,128)(2,1)}, bf16[512,512]{1,0:T(8,128)(2,1)S(1)}, u32[]{:S(2)}, u32[]{:S(2)}) %collective-permute-start.13) | collective-permute-done | bytes 524320 | tf_op jit(solution)/shard_map/ppermute | solution.py:573
  402.1 8.0 %collective-permute-done.14 = bf16[256,512]{1,0:T(8,128)(2,1)S(1)} collective-permute-done((bf16[256,512]{1,0:T(8,128)(2,1)S(1)}, bf16[256,512]{1,0:T(8,128)(2,1)S(1)}, u32[]{:S(2)}, u32[]{:S(2)}) %collective-permute-start.14) | collective-permute-done | bytes 262176 | tf_op jit(solution)/shard_map/ppermute | solution.py:573
  412.0 4.4 collective-permute-start.26
  416.5 4.2 collective-permute-start.16
  423.8 2.7 collective-permute-start.17
  426.5 2.7 collective-permute-start.28
  436.2 5.5 collective-permute-done.29
  443.4 2.9 collective-permute-start.5
  449.4 7.2 %collective-permute-done.30 = bf16[512,512]{1,0:T(8,128)(2,1)S(1)} collective-permute-done((bf16[512,512]{1,0:T(8,128)(2,1)S(1)}, bf16[512,512]{1,0:T(8,128)(2,1)S(1)}, u32[]{:S(2)}, u32[]{:S(2)}) %collective-permute-start.30) | collective-permute-done | bytes 524320 | tf_op jit(solution)/shard_map/ppermute | solution.py:584
  462.4 7.7 %collective-permute-done.8.refs_2_ = bf16[512,512]{1,0:T(8,128)(2,1)} collective-permute-done((bf16[512,512]{1,0:T(8,128)(2,1)}, bf16[512,512]{1,0:T(8,128)(2,1)}, u32[]{:S(2)}, u32[]{:S(2)}) %collective-permute-start.8) | collective-permute-done | bytes 524320 | tf_op jit(solution)/shard_map/ppermute | solution.py:677
  470.1 16.9 %collective-permute-done.2.refs_0_ = bf16[512,512]{1,0:T(8,128)(2,1)} collective-permute-done((bf16[512,512]{1,0:T(8,128)(2,1)}, bf16[512,512]{1,0:T(8,128)(2,1)}, u32[]{:S(2)}, u32[]{:S(2)}) %collective-permute-start.2) | collective-permute-done | bytes 524320 | tf_op jit(solution)/shard_map/ppermute | solution.py:677
  487.1 5.9 %output.1 = bf16[4,512,512]{2,1,0:T(8,128)(2,1)} custom-call(s32[4]{0:T(128)} %select_reduce_fusion.order_ref, s32[4]{0:T(128)} %target_ref.7, f32[4,512,512]{2,1,0:T(8,128)} %get-tuple-element.67.later_ref.refs_6_, bf16[512,512]{1,0:T(8,128)(2,1)} %collective-permute-done.2.refs_0_, bf16[512,512]{1,0:T(8,128)(2,1)} %copy-done.8, ...), custom_call_target="tpu_custom_call" | custom-call | tf_op jit(solution)/shard_map/output/pallas_call | solution.py:956
  493.0 38.1 %psum.7 = f32[16,512]{1,0:T(8,128)S(1)} all-reduce(f32[16,512]{1,0:T(8,128)S(1)} %pad_maximum_fusion.8), channel_id=1, replica_groups=mesh['expert'=4,'dp'=8] {'expert','dp'}, use_global_device_ids=true, to_apply=%region_5.6 | all-reduce | flops 8192 | bytes 65536 | tf_op jit(solution)/shard_map/psum | solution.py:969
  (177 shorter events, 83.5 us)
Async XLA Ops:
  7.2 450.6 %reduce-scatter.15.cloned.1.call-start = ((), (), s32[]{:S(2)}) async-start(), calls=%async_computation.7 | async-start | bytes 294912
  87.1 18.2 %collective-permute-start.3 = (bf16[512,512]{1,0:T(8,128)(2,1)}, bf16[512,512]{1,0:T(8,128)(2,1)S(1)}, u32[]{:S(2)}, u32[]{:S(2)}) collective-permute-start(bf16[512,512]{1,0:T(8,128)(2,1)} %get-tuple-element.119), channel_id=1, source_target_pairs={{0,8},{8,16},{16,24},{24,0},{1,9},{9,17},{17,25},{25,1},{2,10},{10... | collective-permute-start | bytes 1572872 | tf_op jit(solution)/shard_map/ppermute | solution.py:677
  96.2 24.4 %collective-permute-start.4 = (bf16[512,512]{1,0:T(8,128)(2,1)}, bf16[512,512]{1,0:T(8,128)(2,1)S(1)}, u32[]{:S(2)}, u32[]{:S(2)}) collective-permute-start(bf16[512,512]{1,0:T(8,128)(2,1)} %get-tuple-element.115), channel_id=1, source_target_pairs={{0,8},{8,16},{16,24},{24,0},{1,9},{9,17},{17,25},{25,1},{2,10},{10... | collective-permute-start | bytes 1572872 | tf_op jit(solution)/shard_map/ppermute | solution.py:677
  97.8 34.6 %collective-permute-start.6 = (bf16[512,512]{1,0:T(8,128)(2,1)}, bf16[512,512]{1,0:T(8,128)(2,1)S(1)}, u32[]{:S(2)}, u32[]{:S(2)}) collective-permute-start(bf16[512,512]{1,0:T(8,128)(2,1)} %get-tuple-element.118), channel_id=1, source_target_pairs={{0,24},{8,0},{16,8},{24,16},{1,25},{9,1},{17,9},{25,17},{2,26},{10... | collective-permute-start | bytes 1572872 | tf_op jit(solution)/shard_map/ppermute | solution.py:677
  100.0 38.0 %collective-permute-start.7 = (bf16[512,512]{1,0:T(8,128)(2,1)}, bf16[512,512]{1,0:T(8,128)(2,1)S(1)}, u32[]{:S(2)}, u32[]{:S(2)}) collective-permute-start(bf16[512,512]{1,0:T(8,128)(2,1)} %get-tuple-element.114), channel_id=1, source_target_pairs={{0,24},{8,0},{16,8},{24,16},{1,25},{9,1},{17,9},{25,17},{2,26},{10... | collective-permute-start | bytes 1572872 | tf_op jit(solution)/shard_map/ppermute | solution.py:677
  100.4 71.4 %collective-permute-start = (bf16[512,512]{1,0:T(8,128)(2,1)S(1)}, bf16[512,512]{1,0:T(8,128)(2,1)S(1)}, u32[]{:S(2)}, u32[]{:S(2)}) collective-permute-start(bf16[512,512]{1,0:T(8,128)(2,1)S(1)} %get-tuple-element.120), channel_id=1, source_target_pairs={{0,16},{8,24},{16,0},{24,8},{1,17},{9,25},{17,1},{25,9},{2,18},{10... | collective-permute-start | bytes 1572872 | tf_op jit(solution)/shard_map/ppermute | solution.py:677
  105.3 77.8 %collective-permute-start.1 = (bf16[512,512]{1,0:T(8,128)(2,1)}, bf16[512,512]{1,0:T(8,128)(2,1)}, u32[]{:S(2)}, u32[]{:S(2)}) collective-permute-start(bf16[512,512]{1,0:T(8,128)(2,1)} %get-tuple-element.116), channel_id=1, source_target_pairs={{0,16},{8,24},{16,0},{24,8},{1,17},{9,25},{17,1},{25,9},{2,18},{10... | collective-permute-start | bytes 1572872 | tf_op jit(solution)/shard_map/ppermute | solution.py:677
  216.4 242.8 %reduce-scatter.13.cloned.1.call-start = ((), (), s32[]{:S(2)}) async-start(), calls=%async_computation.6 | async-start | bytes 1179648
  218.5 321.9 %reduce-scatter.9.cloned.1.call-start = ((), (), s32[]{:S(2)}) async-start(), calls=%async_computation.4 | async-start | bytes 4718592 | tf_op jit(solution)/shard_map/reduce_scatter | solution.py:844
  219.3 323.2 %reduce-scatter.11.cloned.1.call-start = ((), (), s32[]{:S(2)}) async-start(), calls=%async_computation.5 | async-start | bytes 4718592 | tf_op jit(solution)/shard_map/reduce_scatter | solution.py:845
  219.6 27.0 %collective-permute-start.10 = (bf16[512,512]{1,0:T(8,128)(2,1)S(1)}, bf16[512,512]{1,0:T(8,128)(2,1)S(1)}, u32[]{:S(2)}, u32[]{:S(2)}) collective-permute-start(bf16[512,512]{1,0:T(8,128)(2,1)S(1)} %copy-done.20), channel_id=1, source_target_pairs={{0,24},{8,0},{16,8},{24,16},{1,25},{9,1},{17,9},{25,17},{2,26},{10... | collective-permute-start | bytes 1572872 | tf_op jit(solution)/shard_map/ppermute | solution.py:677
  221.3 28.0 %collective-permute-start.11 = (bf16[512,512]{1,0:T(8,128)(2,1)S(1)}, bf16[512,512]{1,0:T(8,128)(2,1)S(1)}, u32[]{:S(2)}, u32[]{:S(2)}) collective-permute-start(bf16[512,512]{1,0:T(8,128)(2,1)S(1)} %copy-done.21), channel_id=1, source_target_pairs={{0,8},{8,16},{16,24},{24,0},{1,9},{9,17},{17,25},{25,1},{2,10},{10... | collective-permute-start | bytes 1572872 | tf_op jit(solution)/shard_map/ppermute | solution.py:677
  222.2 42.8 %collective-permute-start.9 = (bf16[512,512]{1,0:T(8,128)(2,1)S(1)}, bf16[512,512]{1,0:T(8,128)(2,1)S(1)}, u32[]{:S(2)}, u32[]{:S(2)}) collective-permute-start(bf16[512,512]{1,0:T(8,128)(2,1)S(1)} %copy-done.22), channel_id=1, source_target_pairs={{0,16},{8,24},{16,0},{24,8},{1,17},{9,25},{17,1},{25,9},{2,18},{10... | collective-permute-start | bytes 1572872 | tf_op jit(solution)/shard_map/ppermute | solution.py:677
  321.6 49.0 %collective-permute-start.22 = (bf16[1024,512]{1,0:T(8,128)(2,1)S(1)}, bf16[1024,512]{1,0:T(8,128)(2,1)}, u32[]{:S(2)}, u32[]{:S(2)}) collective-permute-start(bf16[1024,512]{1,0:T(8,128)(2,1)S(1)} %constant_dynamic-slice_fusion.4), channel_id=1, source_target_pairs={{0,1},{1,0},{2,3},{3,2},{4,5},{5,4},{6,7},{7,6},{8,9},{9,8},{10,11... | collective-permute-start | bytes 3145736 | tf_op jit(solution)/shard_map/ppermute | solution.py:573
  373.1 15.0 %collective-permute-start.23 = (bf16[512,512]{1,0:T(8,128)(2,1)}, bf16[512,512]{1,0:T(8,128)(2,1)S(1)}, u32[]{:S(2)}, u32[]{:S(2)}) collective-permute-start(bf16[512,512]{1,0:T(8,128)(2,1)} %constant_dynamic-slice_fusion.3), channel_id=1, source_target_pairs={{0,2},{1,3},{2,0},{3,1},{4,6},{5,7},{6,4},{7,5},{8,10},{9,11},{10,... | collective-permute-start | bytes 1572872 | tf_op jit(solution)/shard_map/ppermute | solution.py:573
  377.0 21.4 %collective-permute-start.13 = (bf16[512,512]{1,0:T(8,128)(2,1)}, bf16[512,512]{1,0:T(8,128)(2,1)S(1)}, u32[]{:S(2)}, u32[]{:S(2)}) collective-permute-start(bf16[512,512]{1,0:T(8,128)(2,1)} %constant_dynamic-slice_fusion.8), channel_id=1, source_target_pairs={{0,2},{1,3},{2,0},{3,1},{4,6},{5,7},{6,4},{7,5},{8,10},{9,11},{10,... | collective-permute-start | bytes 1572872 | tf_op jit(solution)/shard_map/ppermute | solution.py:573
  388.3 11.9 %collective-permute-start.24 = (bf16[256,512]{1,0:T(8,128)(2,1)S(1)}, bf16[256,512]{1,0:T(8,128)(2,1)S(1)}, u32[]{:S(2)}, u32[]{:S(2)}) collective-permute-start(bf16[256,512]{1,0:T(8,128)(2,1)S(1)} %constant_dynamic-slice_fusion.2), channel_id=1, source_target_pairs={{0,4},{1,5},{2,6},{3,7},{4,0},{5,1},{6,2},{7,3},{8,12},{9,13},{10,... | collective-permute-start | bytes 786440 | tf_op jit(solution)/shard_map/ppermute | solution.py:573
  398.6 11.5 %collective-permute-start.14 = (bf16[256,512]{1,0:T(8,128)(2,1)S(1)}, bf16[256,512]{1,0:T(8,128)(2,1)S(1)}, u32[]{:S(2)}, u32[]{:S(2)}) collective-permute-start(bf16[256,512]{1,0:T(8,128)(2,1)S(1)} %constant_dynamic-slice_fusion.7), channel_id=1, source_target_pairs={{0,4},{1,5},{2,6},{3,7},{4,0},{5,1},{6,2},{7,3},{8,12},{9,13},{10,... | collective-permute-start | bytes 786440 | tf_op jit(solution)/shard_map/ppermute | solution.py:573
  400.3 11.6 %collective-permute-start.25 = (bf16[128,512]{1,0:T(8,128)(2,1)S(1)}, bf16[128,512]{1,0:T(8,128)(2,1)S(1)}, u32[]{:S(2)}, u32[]{:S(2)}) collective-permute-start(bf16[128,512]{1,0:T(8,128)(2,1)S(1)} %constant_dynamic-slice_fusion.1), channel_id=1, source_target_pairs={{0,8},{8,0},{16,24},{24,16},{1,9},{9,1},{17,25},{25,17},{2,10},{10... | collective-permute-start | bytes 393224 | tf_op jit(solution)/shard_map/ppermute | solution.py:573
  410.2 6.3 %collective-permute-start.15 = (bf16[128,512]{1,0:T(8,128)(2,1)S(1)}, bf16[128,512]{1,0:T(8,128)(2,1)S(1)}, u32[]{:S(2)}, u32[]{:S(2)}) collective-permute-start(bf16[128,512]{1,0:T(8,128)(2,1)S(1)} %constant_dynamic-slice_fusion.6), channel_id=1, source_target_pairs={{0,8},{8,0},{16,24},{24,16},{1,9},{9,1},{17,25},{25,17},{2,10},{10... | collective-permute-start | bytes 393224 | tf_op jit(solution)/shard_map/ppermute | solution.py:573
  412.0 8.7 %collective-permute-start.26 = (bf16[64,512]{1,0:T(8,128)(2,1)S(1)}, bf16[64,512]{1,0:T(8,128)(2,1)S(1)}, u32[]{:S(2)}, u32[]{:S(2)}) collective-permute-start(bf16[64,512]{1,0:T(8,128)(2,1)S(1)} %constant_dynamic-slice_fusion), channel_id=1, source_target_pairs={{0,16},{8,24},{16,0},{24,8},{1,17},{9,25},{17,1},{25,9},{2,18},{10... | collective-permute-start | bytes 196616 | tf_op jit(solution)/shard_map/ppermute | solution.py:573
  416.5 7.2 %collective-permute-start.16 = (bf16[64,512]{1,0:T(8,128)(2,1)S(1)}, bf16[64,512]{1,0:T(8,128)(2,1)S(1)}, u32[]{:S(2)}, u32[]{:S(2)}) collective-permute-start(bf16[64,512]{1,0:T(8,128)(2,1)S(1)} %constant_dynamic-slice_fusion.5), channel_id=1, source_target_pairs={{0,16},{8,24},{16,0},{24,8},{1,17},{9,25},{17,1},{25,9},{2,18},{10... | collective-permute-start | bytes 196616 | tf_op jit(solution)/shard_map/ppermute | solution.py:573
  420.7 5.7 %collective-permute-start.27 = (bf16[64,512]{1,0:T(8,128)(2,1)S(1)}, bf16[64,512]{1,0:T(8,128)(2,1)S(1)}, u32[]{:S(2)}, u32[]{:S(2)}) collective-permute-start(bf16[64,512]{1,0:T(8,128)(2,1)S(1)} %add_convert_fusion.8), channel_id=1, source_target_pairs={{0,16},{8,24},{16,0},{24,8},{1,17},{9,25},{17,1},{25,9},{2,18},{10... | collective-permute-start | bytes 196616 | tf_op jit(solution)/shard_map/ppermute | solution.py:584
  426.5 5.6 %collective-permute-start.28 = (bf16[128,512]{1,0:T(8,128)(2,1)S(1)}, bf16[128,512]{1,0:T(8,128)(2,1)S(1)}, u32[]{:S(2)}, u32[]{:S(2)}) collective-permute-start(bf16[128,512]{1,0:T(8,128)(2,1)S(1)} %pad_maximum_fusion.7), channel_id=1, source_target_pairs={{0,8},{8,0},{16,24},{24,16},{1,9},{9,1},{17,25},{25,17},{2,10},{10... | collective-permute-start | bytes 393224 | tf_op jit(solution)/shard_map/ppermute | solution.py:584
  432.2 9.5 %collective-permute-start.29 = (bf16[256,512]{1,0:T(8,128)(2,1)S(1)}, bf16[256,512]{1,0:T(8,128)(2,1)S(1)}, u32[]{:S(2)}, u32[]{:S(2)}) collective-permute-start(bf16[256,512]{1,0:T(8,128)(2,1)S(1)} %pad_maximum_fusion.5), channel_id=1, source_target_pairs={{0,4},{1,5},{2,6},{3,7},{4,0},{5,1},{6,2},{7,3},{8,12},{9,13},{10,... | collective-permute-start | bytes 786440 | tf_op jit(solution)/shard_map/ppermute | solution.py:584
  434.5 13.1 %collective-permute-start.19 = (bf16[256,512]{1,0:T(8,128)(2,1)S(1)}, bf16[256,512]{1,0:T(8,128)(2,1)S(1)}, u32[]{:S(2)}, u32[]{:S(2)}) collective-permute-start(bf16[256,512]{1,0:T(8,128)(2,1)S(1)} %pad_maximum_fusion.4), channel_id=1, source_target_pairs={{0,4},{1,5},{2,6},{3,7},{4,0},{5,1},{6,2},{7,3},{8,12},{9,13},{10,... | collective-permute-start | bytes 786440 | tf_op jit(solution)/shard_map/ppermute | solution.py:584
  441.8 14.7 %collective-permute-start.30 = (bf16[512,512]{1,0:T(8,128)(2,1)S(1)}, bf16[512,512]{1,0:T(8,128)(2,1)S(1)}, u32[]{:S(2)}, u32[]{:S(2)}) collective-permute-start(bf16[512,512]{1,0:T(8,128)(2,1)S(1)} %pad_maximum_fusion.3), channel_id=1, source_target_pairs={{0,2},{1,3},{2,0},{3,1},{4,6},{5,7},{6,4},{7,5},{8,10},{9,11},{10,... | collective-permute-start | bytes 1572872 | tf_op jit(solution)/shard_map/ppermute | solution.py:584
  443.4 19.0 %collective-permute-start.5 = (bf16[512,512]{1,0:T(8,128)(2,1)}, bf16[512,512]{1,0:T(8,128)(2,1)S(1)}, u32[]{:S(2)}, u32[]{:S(2)}) collective-permute-start(bf16[512,512]{1,0:T(8,128)(2,1)} %get-tuple-element.70), channel_id=1, source_target_pairs={{0,24},{8,0},{16,8},{24,16},{1,25},{9,1},{17,9},{25,17},{2,26},{10... | collective-permute-start | bytes 1572872 | tf_op jit(solution)/shard_map/ppermute | solution.py:677
  446.3 23.8 %collective-permute-start.8 = (bf16[512,512]{1,0:T(8,128)(2,1)}, bf16[512,512]{1,0:T(8,128)(2,1)}, u32[]{:S(2)}, u32[]{:S(2)}) collective-permute-start(bf16[512,512]{1,0:T(8,128)(2,1)} %get-tuple-element.71), channel_id=1, source_target_pairs={{0,8},{8,16},{16,24},{24,0},{1,9},{9,17},{17,25},{25,1},{2,10},{10... | collective-permute-start | bytes 1572872 | tf_op jit(solution)/shard_map/ppermute | solution.py:677
  446.3 40.7 %collective-permute-start.2 = (bf16[512,512]{1,0:T(8,128)(2,1)}, bf16[512,512]{1,0:T(8,128)(2,1)}, u32[]{:S(2)}, u32[]{:S(2)}) collective-permute-start(bf16[512,512]{1,0:T(8,128)(2,1)} %get-tuple-element.69), channel_id=1, source_target_pairs={{0,16},{8,24},{16,0},{24,8},{1,17},{9,25},{17,1},{25,9},{2,18},{10... | collective-permute-start | bytes 1572872 | tf_op jit(solution)/shard_map/ppermute | solution.py:677
  448.4 82.7 %collective-permute-start.20 = (bf16[512,512]{1,0:T(8,128)(2,1)}, bf16[512,512]{1,0:T(8,128)(2,1)}, u32[]{:S(2)}, u32[]{:S(2)}) collective-permute-start(bf16[512,512]{1,0:T(8,128)(2,1)} %pad_maximum_fusion.2), channel_id=1, source_target_pairs={{0,2},{1,3},{2,0},{3,1},{4,6},{5,7},{6,4},{7,5},{8,10},{9,11},{10,... | collective-permute-start | bytes 1572872 | tf_op jit(solution)/shard_map/ppermute | solution.py:584
  457.8 75.4 %collective-permute-start.31 = (bf16[1024,512]{1,0:T(8,128)(2,1)}, bf16[1024,512]{1,0:T(8,128)(2,1)S(1)}, u32[]{:S(2)}, u32[]{:S(2)}) collective-permute-start(bf16[1024,512]{1,0:T(8,128)(2,1)} %pad_maximum_fusion.1), channel_id=1, source_target_pairs={{0,1},{1,0},{2,3},{3,2},{4,5},{5,4},{6,7},{7,6},{8,9},{9,8},{10,11... | collective-permute-start | bytes 3145736 | tf_op jit(solution)/shard_map/ppermute | solution.py:584
  (28 other events, 215.8 us)
Sparse Core Ops, SparseCore 0:
  216.5 35.2 reduce-scatter.14
  255.9 36.0 reduce-scatter.12
  295.7 51.3 reduce-scatter.8
  377.6 60.3 reduce-scatter.10

commit v2 on v1

v2 whole, which is shorter than its diff:
```python
import functools

import jax
import jax.numpy as jnp
from jax import lax
from jax.experimental import pallas as pl
from jax.experimental.pallas import tpu as pltpu
from jax.sharding import PartitionSpec as P

HEADS = 8
HEAD_DIM = 64
PAIR = 2 * HEAD_DIM
EPSILON = 1e-05
SCORE_SCALE = 0.125
NEGATIVE = -1e30
SAFE_SCORE = 80.0
SHARED_LINES = 16
EXPERT_LINES = 16
LINES = SHARED_LINES + EXPERT_LINES
LOG2E = 1.4426950408889634
LN2 = 0.6931471805599453
VMEM_LIMIT = 63 * 1024 * 1024
F32 = jnp.float32
BF16 = jnp.bfloat16


def contract(left, right, left_dim, right_dim):
    return lax.dot_general(
        left, right, (((left_dim,), (right_dim,)), ((), ())), preferred_element_type=F32
    )


def nn(left, right):
    return contract(left, right, 1, 0)


def nt(left, right):
    return contract(left, right, 1, 1)


def tn(left, right):
    return contract(left, right, 0, 0)


def normalise(rows):
    centre = rows - jnp.mean(rows, axis=-1, keepdims=True)
    inverse = lax.rsqrt(jnp.mean(centre * centre, axis=-1, keepdims=True) + EPSILON)
    return centre * inverse, inverse


def normalise_back(grad, normed, inverse, gain):
    scaled = grad * gain
    return inverse * (
        scaled
        - jnp.mean(scaled, axis=-1, keepdims=True)
        - normed * jnp.mean(scaled * normed, axis=-1, keepdims=True)
    )


def column_sum(rows):
    return jnp.sum(rows.astype(F32), axis=0, keepdims=True)


def head_masks():
    lane = lax.broadcasted_iota(jnp.int32, (1, PAIR), 1)
    mine = [(lane // HEAD_DIM == half).astype(F32).astype(BF16) for half in (0, 1)]
    spare = [(lane == HEAD_DIM * (1 - half)).astype(F32).astype(BF16) for half in (0, 1)]
    return mine, spare


def key_bias(count, mem_rows):
    place = lax.broadcasted_iota(jnp.int32, (mem_rows, PAIR), 0)
    return jnp.where(place < count, 0.0, NEGATIVE).astype(BF16)


def score_operands(keys, queries, half, mine, spare, bias):
    picked = queries * mine[half]
    if bias is None:
        return keys, picked
    return keys * (1 - spare[half]) + bias * spare[half], picked + spare[half]


def causal(scores, block):
    key_at = lax.broadcasted_iota(jnp.int32, (scores.shape[0], block), 0)
    query_at = lax.broadcasted_iota(jnp.int32, (scores.shape[0], block), 1)
    return jnp.where(key_at <= query_at, scores, NEGATIVE)


def lower(items, block):
    return jnp.concatenate([item[block:] for item in items], axis=0)


def lower_columns(items, block):
    return jnp.concatenate([item[:, block:] for item in items], axis=1)


def head_rows(pair, half):
    return pl.ds(pl.multiple_of(pair * PAIR + half * HEAD_DIM, HEAD_DIM), HEAD_DIM)


def pair_span(pair):
    return pl.ds(pl.multiple_of(pair * PAIR, PAIR), PAIR)


def head_part(both, half, block):
    return both[half * HEAD_DIM : (half + 1) * HEAD_DIM, half * block : (half + 1) * block]


def causal_pair_scores(keys, picked, block):
    upper = []
    for half in (0, 1):
        scores = nt(keys[:block], picked[half])
        upper.append(
            jnp.concatenate([causal(scores[:, :block], block), scores[:, block:]], axis=1)
        )
    scores = nt(keys[block:], lower(picked, block))
    low = jnp.concatenate([causal(scores[:, :block], block), causal(scores[:, block:], block)], axis=1)
    return upper, low


def head_blocks():
    feature = lax.broadcasted_iota(jnp.int32, (HEADS * HEAD_DIM, 128), 0)
    return (feature // HEAD_DIM == lax.broadcasted_iota(jnp.int32, (HEADS * HEAD_DIM, 128), 1)).astype(BF16)


def scores_small(query_ref, key_ref):
    blocks = head_blocks()
    squares = [nn(ref[...] * ref[...], blocks) for ref in (query_ref, key_ref)]
    most = [jnp.max(item, axis=0, keepdims=True) for item in squares]
    return jnp.max(most[0] * most[1]) < SAFE_SCORE * SAFE_SCORE


def attend_cross(plain, query_ref, key_ref, value_t_ref, context_t_ref, logsum_ref, bias):
    mine, spare = head_masks()

    def pair_step(pair, carry):
        columns = pair_span(pair)
        keys, queries = key_ref[:, columns], query_ref[:, columns]
        for half in (0, 1):
            rows = head_rows(pair, half)
            left, right = score_operands(keys, queries, half, mine, spare, bias)
            scores = nt(left, right)
            highest = 0.0 if plain else jnp.max(scores, axis=0, keepdims=True)
            raised = jnp.exp2(scores if plain else scores - highest)
            summed = jnp.sum(raised, axis=0, keepdims=True)
            context = nn(value_t_ref[rows, :], raised.astype(BF16))
            context_t_ref[rows, :] = (context * (1.0 / summed)).astype(BF16)
            logsum_ref[pl.ds(2 * pair + half, 1), :] = highest + LOG2E * jnp.log(summed)
        return carry

    lax.fori_loop(0, HEADS // 2, pair_step, 0)


def attend_self(plain, query_ref, key_ref, value_t_ref, context_t_ref, logsum_ref):
    block = query_ref.shape[0] // 2
    mine, _ = head_masks()

    def pair_step(pair, carry):
        columns = pair_span(pair)
        keys, queries = key_ref[:, columns], query_ref[:, columns]
        upper, low = causal_pair_scores(keys, [queries * mine[0], queries * mine[1]], block)
        if plain:
            highest = [0.0, 0.0]
            low = jnp.exp2(low)
        else:
            low_top = jnp.max(low, axis=0, keepdims=True)
            highest = []
            for half in (0, 1):
                top = jnp.max(upper[half], axis=0, keepdims=True)
                other = low_top[:, half * block : (half + 1) * block]
                highest.append(
                    jnp.concatenate([top[:, :block], jnp.maximum(top[:, block:], other)], axis=1)
                )
            low = jnp.exp2(low - lower_columns(highest, block))
        low_sum = jnp.sum(low, axis=0, keepdims=True)
        low_context = nn(value_t_ref[columns, block:], low.astype(BF16))
        for half in (0, 1):
            rows = head_rows(pair, half)
            raised = jnp.exp2(upper[half] if plain else upper[half] - highest[half])
            summed = jnp.sum(raised, axis=0, keepdims=True)
            part = low_sum[:, half * block : (half + 1) * block]
            summed = jnp.concatenate([summed[:, :block], summed[:, block:] + part], axis=1)
            context = nn(value_t_ref[rows, :block], raised.astype(BF16))
            context = jnp.concatenate(
                [context[:, :block], context[:, block:] + head_part(low_context, half, block)],
                axis=1,
            )
            context_t_ref[rows, :] = (context * (1.0 / summed)).astype(BF16)
            logsum_ref[pl.ds(2 * pair + half, 1), :] = highest[half] + LOG2E * jnp.log(summed)
        return carry

    lax.fori_loop(0, HEADS // 2, pair_step, 0)


def attend(kind, query_ref, key_ref, *refs):
    small = scores_small(query_ref, key_ref)

    @pl.when(small)
    def _():
        kind(True, query_ref, key_ref, *refs)

    @pl.when(jnp.logical_not(small))
    def _():
        kind(False, query_ref, key_ref, *refs)


def attend_cross_back(
    query_ref,
    key_ref,
    value_ref,
    key_t_ref,
    grad_ref,
    delta_ref,
    logsum_ref,
    grad_query_t_ref,
    grad_key_ref,
    grad_value_ref,
    bias,
):
    mine, spare = head_masks()

    def pair_step(pair, carry):
        columns = pair_span(pair)
        keys, queries, values = key_ref[:, columns], query_ref[:, columns], value_ref[:, columns]
        grads = grad_ref[:, columns]
        chances, slopes, picked_grads, picked_queries = [], [], [], []
        for half in (0, 1):
            head, rows = pl.ds(2 * pair + half, 1), head_rows(pair, half)
            left, right = score_operands(keys, queries, half, mine, spare, bias)
            picked_grads.append(grads * mine[half])
            picked_queries.append(queries * mine[half])
            chance = jnp.exp2(nt(left, right) - logsum_ref[head, :])
            slope = chance * (nt(values, picked_grads[half]) - delta_ref[head, :])
            chances.append(chance.astype(BF16))
            slopes.append(slope.astype(BF16))
            grad_query_t_ref[rows, :] = (nn(key_t_ref[rows, :], slopes[half]) * SCORE_SCALE).astype(
                BF16
            )
        grad_value_ref[:, columns] = nn(
            jnp.concatenate(chances, axis=1), jnp.concatenate(picked_grads, axis=0)
        ).astype(BF16)
        grad_key_ref[:, columns] = (
            nn(jnp.concatenate(slopes, axis=1), jnp.concatenate(picked_queries, axis=0)) * LN2
        ).astype(BF16)
        return carry

    lax.fori_loop(0, HEADS // 2, pair_step, 0)


def attend_self_back(
    query_ref,
    key_ref,
    value_ref,
    key_t_ref,
    grad_ref,
    delta_ref,
    logsum_ref,
    grad_query_t_ref,
    grad_key_ref,
    grad_value_ref,
):
    block = query_ref.shape[0] // 2
    mine, _ = head_masks()

    def pair_step(pair, carry):
        columns = pair_span(pair)
        keys, queries, values = key_ref[:, columns], query_ref[:, columns], value_ref[:, columns]
        grads = grad_ref[:, columns]
        picked = [queries * mine[0], queries * mine[1]]
        picked_grads = [grads * mine[0], grads * mine[1]]
        upper, low = causal_pair_scores(keys, picked, block)
        logsum = [logsum_ref[pl.ds(2 * pair + half, 1), :] for half in (0, 1)]
        delta = [delta_ref[pl.ds(2 * pair + half, 1), :] for half in (0, 1)]
        low_grads = lower(picked_grads, block)
        low = jnp.exp2(low - lower_columns(logsum, block))
        low_slope = (
            low * (nt(values[block:], low_grads) - lower_columns(delta, block))
        ).astype(BF16)
        low_query = nn(key_t_ref[columns, block:], low_slope)
        chances, slopes = [], []
        for half in (0, 1):
            chance = jnp.exp2(upper[half] - logsum[half])
            slope = chance * (nt(values[:block], picked_grads[half]) - delta[half])
            chances.append(chance.astype(BF16))
            slopes.append(slope.astype(BF16))
            rows = head_rows(pair, half)
            grad = nn(key_t_ref[rows, :block], slopes[half])
            grad = jnp.concatenate(
                [grad[:, :block], grad[:, block:] + head_part(low_query, half, block)], axis=1
            )
            grad_query_t_ref[rows, :] = (grad * SCORE_SCALE).astype(BF16)
        grad_value_ref[:block, columns] = nn(
            jnp.concatenate(chances, axis=1), jnp.concatenate(picked_grads, axis=0)
        ).astype(BF16)
        grad_value_ref[block:, columns] = nn(low.astype(BF16), low_grads).astype(BF16)
        grad_key_ref[:block, columns] = (
            nn(jnp.concatenate(slopes, axis=1), jnp.concatenate(picked, axis=0)) * LN2
        ).astype(BF16)
        grad_key_ref[block:, columns] = (nn(low_slope, lower(picked, block)) * LN2).astype(BF16)
        return carry

    lax.fori_loop(0, HEADS // 2, pair_step, 0)


def head_sums(grad, context_t):
    product = grad.T.astype(F32) * context_t.astype(F32)
    return jnp.sum(product.reshape(HEADS, HEAD_DIM, product.shape[1]), axis=1)


def valid_rows_of(count, length):
    return (lax.broadcasted_iota(jnp.int32, (length, 1), 0) < count).astype(F32)


def forward_kernel(
    start_at,
    steps,
    order_ref,
    target_ref,
    memory_length_ref,
    tokens_ref,
    memory_ref,
    vectors_ref,
    self_query,
    self_key,
    self_value,
    self_out,
    cross_query,
    cross_key,
    cross_value,
    cross_out,
    *refs,
):
    normed_refs, refs = refs[:steps], refs[steps:]
    (
    later_ref,
    middle_ref,
    query_one_ref,
    key_one_ref,
    value_one_ref,
    context_one_ref,
    logsum_one_ref,
    query_two_ref,
    key_two_ref,
    value_two_ref,
    context_two_ref,
    logsum_two_ref,
    value_t_ref,
    ) = refs
    step = pl.program_id(0)
    sequence = order_ref[start_at + step]
    length = tokens_ref.shape[1]
    vector = lambda at: vectors_ref[at : at + 1, :]
    start = tokens_ref[0].astype(F32) * valid_rows_of(target_ref[sequence], length)
    normed = (normalise(start)[0] * vector(0) + vector(1)).astype(BF16)
    scale = SCORE_SCALE * LOG2E
    query_one_ref[0] = ((nn(normed, self_query[...]) + vector(2)) * scale).astype(BF16)
    key_one_ref[0] = nn(normed, self_key[...]).astype(BF16)
    value = (nn(normed, self_value[...]) + vector(3)).astype(BF16)
    value_one_ref[0] = value
    value_t_ref[...] = value.T
    attend(
        attend_self,
        query_one_ref.at[0],
        key_one_ref.at[0],
        value_t_ref,
        context_one_ref.at[0],
        logsum_one_ref.at[0],
    )
    middle = start + tn(context_one_ref[0], self_out[...]) + vector(4)
    middle_ref[0] = middle
    normed = (normalise(middle)[0] * vector(5) + vector(6)).astype(BF16)
    memory = memory_ref[0]
    query_two_ref[0] = ((nn(normed, cross_query[...]) + vector(7)) * scale).astype(BF16)
    key_two_ref[0] = nn(memory, cross_key[...]).astype(BF16)
    value = (nn(memory, cross_value[...]) + vector(8)).astype(BF16)
    value_two_ref[0] = value
    value_t_ref[...] = value.T
    attend(
        attend_cross,
        query_two_ref.at[0],
        key_two_ref.at[0],
        value_t_ref,
        context_two_ref.at[0],
        logsum_two_ref.at[0],
        key_bias(memory_length_ref[sequence], memory.shape[0]),
    )
    later = middle_ref[0] + tn(context_two_ref[0], cross_out[...]) + vector(9)
    later_ref[0] = later
    normed = (normalise(later)[0] * vector(10) + vector(11)).astype(BF16)
    for at in range(steps):

        @pl.when(step == at)
        def _():
            normed_refs[at][...] = normed


def expert_kernel(
    slot,
    pick_ref,
    used_ref,
    rows_ref,
    grads_ref,
    weight_in,
    bias_in,
    weight_out,
    bias_out,
    hidden_ref,
    grad_pre_ref,
    made_ref,
    grad_rows_ref,
    pre_sum_ref,
    grads_sum_ref,
    made_sum,
    grad_sum,
):
    tile = pl.program_id(0)
    last = pl.num_programs(0) - 1
    used = used_ref[slot] > 0
    pick = pl.ds(pick_ref[slot], 1)

    @pl.when(used)
    def _():
        pre = nn(rows_ref[...], weight_in[0]) + bias_in[pick, :]
        grad_hidden = nt(grads_ref[...], weight_out[0])
        gate = 0.5 * jnp.tanh(0.5 * pre) + 0.5
        active = pre * gate
        hidden = active.astype(BF16)
        hidden_ref[...] = hidden
        grad_pre = grad_hidden * (gate + active * (1.0 - gate))
        pre_sum_ref[...] = jnp.sum(grad_pre, axis=0, keepdims=True)
        grad_pre = grad_pre.astype(BF16)
        grad_pre_ref[...] = grad_pre
        made = nn(hidden, weight_out[0])
        grad_rows = nt(grad_pre, weight_in[0])

        @pl.when(tile == 0)
        def _():
            made_sum[...] = made
            grad_sum[...] = grad_rows
            grads_sum_ref[...] = column_sum(grads_ref[...])

        @pl.when(tile > 0)
        def _():
            made_sum[...] += made
            grad_sum[...] += grad_rows

        @pl.when(tile == last)
        def _():
            made_ref[...] = (made_sum[...] + bias_out[pick, :]).astype(BF16)
            grad_rows_ref[...] = grad_sum[...].astype(BF16)

    @pl.when(jnp.logical_not(used))
    def _():
        for ref in (hidden_ref, grad_pre_ref, made_ref, grad_rows_ref, pre_sum_ref, grads_sum_ref):
            ref[...] = jnp.zeros_like(ref)


def expert_weights_kernel(slots, pick_ref, used_ref, *refs):
    rows, grads, hidden, grad_pre, pre_sum, grads_sum = [
        refs[at * slots : (at + 1) * slots] for at in range(6)
    ]
    in_ref, out_ref, lines_ref, in_sum, out_sum, in_bias, out_bias = refs[6 * slots :]
    for total in (in_sum, out_sum, in_bias, out_bias):
        total[...] = jnp.zeros_like(total)
    for slot in range(slots):

        @pl.when(used_ref[slot] > 0)
        def _():
            pick = pick_ref[slot]
            in_sum[pick] += tn(rows[slot][...], grad_pre[slot][...])
            out_sum[pick] += tn(hidden[slot][...], grads[slot][...])
            in_bias[pick] += pre_sum[slot][...]
            out_bias[pick] += grads_sum[slot][...]

    in_ref[...] = in_sum[...].astype(BF16)
    out_ref[...] = out_sum[...].astype(BF16)
    tile, tiles = pl.program_id(0), pl.num_programs(0)
    count = in_bias.shape[0]

    @pl.when(tile == 0)
    def _():
        lines_ref[...] = jnp.zeros_like(lines_ref)

    for pick in range(count):
        lines_ref[pl.ds(pick * tiles + tile, 1), :] = in_bias[pick]
        lines_ref[pl.ds(count * tiles + pick, 1), :] = out_bias[pick]


def plan_kernel(
    shifts,
    local_count,
    place_ref,
    expert_ref,
    target_ref,
    cotangent_ref,
    order_ref,
    pick_ref,
    used_ref,
    slot_ref,
    spot_ref,
    *grads_refs,
):
    groups, seqs = len(shifts), cotangent_ref.shape[0]
    own, column, places = place_ref[0], place_ref[1], place_ref[2]
    own_ids = [expert_ref[(own * places + column) * seqs + at] for at in range(seqs)]
    distance = [lax.rem(lax.div(item, local_count) - own + groups, groups) for item in own_ids]
    slots = [
        sum((jnp.where(item == shift, at, 0) for at, shift in enumerate(shifts)), jnp.int32(0))
        for item in distance
    ]
    for slot in range(groups):
        spot_ref[slot] = 0
        source = lax.rem(own - shifts[slot] + groups, groups)
        pick, used = jnp.int32(0), jnp.int32(0)
        for at in range(seqs):
            item = expert_ref[(source * places + column) * seqs + at]
            here = lax.div(item, local_count) == own
            pick = jnp.where(here, lax.rem(item, local_count), pick)
            used = jnp.where(here, 1, used)
        pick_ref[slot] = pick
        used_ref[slot] = used
    for at in range(seqs):
        spot = sum((jnp.where(other < slots[at], 1, 0) for other in slots), jnp.int32(0))
        order_ref[spot] = at
        slot_ref[spot] = slots[at]
        spot_ref[slots[at]] = spot
    order_ref[seqs] = order_ref[0]
    length = cotangent_ref.shape[1]
    for slot in range(groups):
        sequence = order_ref[spot_ref[slot]]
        valid = valid_rows_of(target_ref[sequence], length)
        grads_refs[slot][...] = (cotangent_ref[sequence].astype(F32) * valid).astype(BF16)


def output_kernel(slots, order_ref, target_ref, later_ref, *refs):
    made, output_ref = refs[:slots], refs[slots]
    position = pl.program_id(0)
    valid = valid_rows_of(target_ref[order_ref[position]], later_ref.shape[1])
    for at in range(slots):

        @pl.when(position == at)
        def _():
            output_ref[0] = ((later_ref[0] + made[at][...].astype(F32)) * valid).astype(BF16)


def open_sums(first, weight_sum, vector_sum, given):
    @pl.when(pl.program_id(0) == 0)
    def _():
        if first:
            weight_sum[...] = jnp.zeros_like(weight_sum)
            vector_sum[...] = jnp.zeros_like(vector_sum)
        else:
            weight_sum[...] = given[0][...]
            vector_sum[...] = given[1][...]


def put_halves(squares, lines, high, keep_ref, give_ref):
    height = squares[0].shape[0]
    half = height * len(squares) // 2
    for top, (low_ref, high_ref) in ((0, (keep_ref, give_ref)), (1, (give_ref, keep_ref))):

        @pl.when(high == top)
        def _():
            for at, square in enumerate(squares):
                for part, ref in enumerate((low_ref, high_ref)):
                    start, stop = max(at * height, part * half), min((at + 1) * height, (part + 1) * half)
                    if start < stop:
                        rows = square[start - at * height : stop - at * height]
                        ref[start - part * half : stop - part * half] = rows.astype(BF16)

    if lines is not None:
        keep_ref[half:] = lines.astype(BF16)
        give_ref[half:] = lines.astype(BF16)


def close_sums(final, weight_sum, vector_sum, high, outs):
    @pl.when(pl.program_id(0) == pl.num_programs(0) - 1)
    def _():
        outs[-1][...] = vector_sum[...]
        if final:
            squares = [weight_sum[0].T] + [weight_sum[at] for at in range(1, weight_sum.shape[0])]
            put_halves(squares, None, high, outs[0], outs[1])
        else:
            outs[0][...] = weight_sum[...]


def cross_back_kernel(
    start_at, first, final, slots, order_ref, target_ref, memory_length_ref, high_ref, *refs
):
    grad_normed, refs = refs[:slots], refs[slots:]
    given, refs = (None, refs) if first else (refs[:2], refs[2:])
    (
        cotangent_ref,
        memory_ref,
        later_ref,
        middle_ref,
        query_ref,
        key_ref,
        value_ref,
        context_ref,
        logsum_ref,
        context_one_ref,
        vectors_ref,
        cross_query,
        cross_key,
        cross_value,
        cross_out,
        grad_middle_ref,
        grad_key_ref,
        grad_value_ref,
        *outs,
        weight_sum,
        vector_sum,
        grad_expert,
        key_t,
        grad_context,
        delta,
        grad_query_t,
    ) = refs
    step = pl.program_id(0)
    sequence = order_ref[lax.rem(start_at + step, order_ref.shape[0] - 1)]
    length = cotangent_ref.shape[1]
    vector = lambda at: vectors_ref[at : at + 1, :]
    open_sums(first, weight_sum, vector_sum, given)

    for at in range(slots):

        @pl.when(step == at)
        def _():
            grad_expert[...] = grad_normed[at][...]

    def add_vector(at, value):
        vector_sum[at : at + 1, :] += value

    valid = valid_rows_of(target_ref[sequence], length)
    normed, inverse = normalise(later_ref[0])
    grad = grad_expert[...].astype(F32)
    add_vector(0, column_sum(grad * normed))
    add_vector(1, column_sum(grad))
    grad_later = cotangent_ref[0].astype(F32) * valid + normalise_back(
        grad, normed, inverse, vector(10)
    )
    branch = grad_later.astype(BF16)
    grad_middle_ref[0] = grad_later
    add_vector(2, column_sum(branch))
    weight_sum[3] += nn(context_ref[0], branch)
    context_grad = nt(branch, cross_out[...]).astype(BF16)
    grad_context[...] = context_grad
    delta[...] = head_sums(context_grad, context_ref[0])
    key_t[...] = key_ref[0].T
    attend_cross_back(
        query_ref.at[0],
        key_ref.at[0],
        value_ref.at[0],
        key_t,
        grad_context,
        delta,
        logsum_ref.at[0],
        grad_query_t,
        grad_key_ref.at[0],
        grad_value_ref.at[0],
        key_bias(memory_length_ref[sequence], memory_ref.shape[1]),
    )
    memory_t = memory_ref[0].T
    weight_sum[1] += nn(memory_t, grad_key_ref[0])
    weight_sum[2] += nn(memory_t, grad_value_ref[0])
    add_vector(3, column_sum(grad_value_ref[0]))
    normed, inverse = normalise(middle_ref[0])
    weight_sum[0] += nn(grad_query_t[...], (normed * vector(5) + vector(6)).astype(BF16))
    grad_query = grad_query_t[...].T
    add_vector(4, column_sum(grad_query))
    grad = nt(grad_query, cross_query[...])
    add_vector(5, column_sum(grad * normed))
    add_vector(6, column_sum(grad))
    grad_middle = grad_middle_ref[0] + normalise_back(grad, normed, inverse, vector(5))
    grad_middle_ref[0] = grad_middle
    branch = grad_middle.astype(BF16)
    add_vector(7, column_sum(branch))
    weight_sum[4] += nn(context_one_ref[0], branch)
    close_sums(final, weight_sum, vector_sum, high_ref[0], outs)


def self_back_kernel(start_at, first, final, order_ref, target_ref, high_ref, *refs):
    given, refs = (None, refs) if first else (refs[:2], refs[2:])
    cross_lines_ref, expert_lines_ref = refs[:2]
    refs = refs[2:]
    (
        tokens_ref,
        grad_middle_ref,
        query_ref,
        key_ref,
        value_ref,
        context_ref,
        logsum_ref,
        columns_ref,
        self_query,
        self_key,
        self_value,
        self_out,
        grad_query_ref,
        grad_key_ref,
        grad_value_ref,
        first_ref,
        second_ref,
        weight_sum,
        vector_sum,
        key_t,
        grad_context,
        delta,
        grad_query_t,
    ) = refs
    step = pl.program_id(0)
    sequence = order_ref[lax.rem(start_at + step, order_ref.shape[0] - 1)]
    length = tokens_ref.shape[1]
    open_sums(first, weight_sum, vector_sum, given)

    valid = valid_rows_of(target_ref[sequence], length)
    context_grad = nt(grad_middle_ref[0].astype(BF16), self_out[...]).astype(BF16)
    grad_context[...] = context_grad
    delta[...] = head_sums(context_grad, context_ref[0])
    key_t[...] = key_ref[0].T
    attend_self_back(
        query_ref.at[0],
        key_ref.at[0],
        value_ref.at[0],
        key_t,
        grad_context,
        delta,
        logsum_ref.at[0],
        grad_query_t,
        grad_key_ref.at[0],
        grad_value_ref.at[0],
    )
    normed = normalise(tokens_ref[0].astype(F32) * valid)[0].astype(BF16)
    normed_t = normed.T
    weight_sum[0] += nn(grad_query_t[...], normed)
    weight_sum[1] += nn(normed_t, grad_key_ref[0])
    weight_sum[2] += nn(normed_t, grad_value_ref[0])
    grad_query = grad_query_t[...].T
    grad_query_ref[0] = grad_query
    for at, item in enumerate((grad_query, grad_key_ref[0], grad_value_ref[0])):
        vector_sum[at : at + 1, :] += column_sum(item)

    @pl.when(step == pl.num_programs(0) - 1)
    def _():
        if not final:
            first_ref[...] = weight_sum[...]
            second_ref[...] = vector_sum[...]
            return
        width = weight_sum.shape[1]
        gain, shift = columns_ref[:, 0:1], columns_ref[:, 1:2]
        gain_grad = jnp.zeros((width, 1), F32)
        shift_grad = jnp.zeros((width, 1), F32)
        squares = []
        for at, matrix in enumerate((self_query, self_key, self_value)):
            total = weight_sum[at].T if at == 0 else weight_sum[at]
            column = vector_sum[at : at + 1, :]
            weights = matrix[...].astype(F32)
            gain_grad += jnp.sum(weights * total, axis=1, keepdims=True)
            shift_grad += jnp.sum(weights * column, axis=1, keepdims=True)
            squares.append((total * gain + shift * column).astype(BF16))
        lane = lax.broadcasted_iota(jnp.int32, (width, 128), 1)
        both = jnp.where(lane == 0, gain_grad, jnp.where(lane == 1, shift_grad, 0.0)).T
        lines = jnp.concatenate(
            [
                vector_sum[0:1, :],
                vector_sum[2:3, :],
                both[0:2, :],
                jnp.zeros((4, width), F32),
                cross_lines_ref[...],
                expert_lines_ref[...],
            ],
            axis=0,
        )
        put_halves(squares, lines, high_ref[0], first_ref, second_ref)


def tokens_back_kernel(
    start_at,
    order_ref,
    target_ref,
    tokens_ref,
    grad_middle_ref,
    grad_query_ref,
    grad_key_ref,
    grad_value_ref,
    vectors_ref,
    self_query,
    self_key,
    self_value,
    tokens_grad_ref,
):
    sequence = order_ref[lax.rem(start_at + pl.program_id(0), order_ref.shape[0] - 1)]
    valid = valid_rows_of(target_ref[sequence], tokens_ref.shape[1])
    normed, inverse = normalise(tokens_ref[0].astype(F32) * valid)
    grad = (
        nt(grad_query_ref[0], self_query[...])
        + nt(grad_key_ref[0], self_key[...])
        + nt(grad_value_ref[0], self_value[...])
    )
    tokens_grad_ref[0] = (
        grad_middle_ref[0] + normalise_back(grad, normed, inverse, vectors_ref[0:1, :])
    ) * valid


def memory_back_kernel(order_ref, grad_key_ref, grad_value_ref, cross_key, cross_value, memory_grad_ref):
    memory_grad_ref[0] = nt(grad_key_ref[0], cross_key[...]) + nt(
        grad_value_ref[0], cross_value[...]
    )


def apart(at, count, turn):
    return at ^ turn if count & (count - 1) == 0 else lax.rem(at + turn, count)


def heard(at, count, turn):
    return at ^ turn if count & (count - 1) == 0 else lax.rem(at + count - turn, count)


def fold_kernel(items, lines, shared, count, at_ref, *refs):
    parts, outs = refs[:items], refs[items:]
    total = parts[0][...].astype(F32)
    for part in parts[1:]:
        total = total + part[...].astype(F32)
    height = total.shape[0] - lines
    if count == 1:
        outs[0][...] = total[:height].astype(BF16)
        if lines:
            outs[1][...] = total[height:]
        return
    share, at = height // count, at_ref[0]
    stack = refs[-1]
    stack[...] = total[:height].astype(BF16)
    for turn in range(count):
        which = pl.multiple_of(apart(at, count, turn) * share, 16)
        outs[turn][:share] = stack[pl.ds(which, share), :]
        if shared:
            outs[turn][share:] = total[height : height + shared].astype(BF16)
    if lines > shared:
        outs[count][...] = total[height + shared :]


def spread_kernel(count, at_ref, *refs):
    parts, out = refs[:count], refs[count]
    share = parts[0].shape[0]
    for turn in range(count):
        place = pl.multiple_of(heard(at_ref[0], count, turn) * share, 16)
        out[pl.ds(place, share), :] = parts[turn][...]


def finish_kernel(high_ref, own_ref, got_ref, *outs):
    own, got = own_ref[...].astype(F32), got_ref[...].astype(F32)
    top = high_ref[0] > 0
    whole = [jnp.where(top, got, own), jnp.where(top, own, got)]
    height, half = outs[0].shape[0], own.shape[0]
    for at, out in enumerate(outs):
        start, stop = at * height, (at + 1) * height
        for part in (0, 1):
            low, top_row = max(start, part * half), min(stop, (part + 1) * half)
            if low < top_row:
                out[low - start : top_row - start] = whole[part][low - part * half : top_row - part * half]


def cast_kernel(*refs):
    count = len(refs) // 2
    for source, out in zip(refs[:count], refs[count:]):
        out[...] = source[...].astype(F32)


def fixed(shape):
    return pl.BlockSpec(shape, lambda *_: (0,) * len(shape))


def once(shape):
    return pl.BlockSpec(shape, lambda *_: (0,) * len(shape), pipeline_mode=pl.Buffered(1))


def at_position(shape, start, count):
    return pl.BlockSpec(
        (1,) + shape, lambda step, *_: (lax.rem(start + step, count),) + (0,) * len(shape)
    )


def at_sequence(shape, start, count):
    return pl.BlockSpec(
        (1,) + shape,
        lambda step, order, *_: (order[lax.rem(start + step, count)],) + (0,) * len(shape),
    )


def struct(shape, kind):
    return jax.ShapeDtypeStruct(shape, kind)


def launch(
    kernel,
    name,
    grid,
    scalars,
    inputs,
    in_specs,
    outs,
    out_specs,
    scratch=(),
    micros=10,
    after=(),
    into=None,
    carry=(),
):
    into = into or {}
    extra = list(after) + list(into.values()) + list(carry)
    lead, made = len(scalars) + len(inputs), len(outs)
    anywhere = pl.BlockSpec(memory_space=pl.ANY)

    def body(*refs):
        rest = refs[lead + len(extra) :]
        kernel(*refs[:lead], *rest[:made], *rest[made + len(carry) :])

    aliases = {lead + len(after) + at: out for at, out in enumerate(into)}
    first = lead + len(after) + len(into)
    aliases.update({first + at: made + at for at in range(len(carry))})
    return pl.pallas_call(
        body,
        grid_spec=pltpu.PrefetchScalarGridSpec(
            num_scalar_prefetch=len(scalars),
            grid=grid,
            in_specs=list(in_specs) + [anywhere] * len(extra),
            out_specs=list(out_specs) + [anywhere] * len(carry),
            scratch_shapes=list(scratch),
        ),
        out_shape=[struct(shape, kind) for shape, kind in outs]
        + [struct(item.shape, item.dtype) for item in carry],
        input_output_aliases=aliases,
        compiler_params=pltpu.CompilerParams(
            dimension_semantics=("arbitrary",) * len(grid), vmem_limit_bytes=VMEM_LIMIT
        ),
        cost_estimate=pl.CostEstimate(
            flops=int(micros * 1.0e9), bytes_accessed=int(micros * 2.0e6), transcendentals=0
        ),
        name=name,
    )(*scalars, *inputs, *extra)


def exchange(rows, way, turn):
    axis, stride, count = way
    route = []
    for place in range(lax.axis_size(axis)):
        at = (place // stride) % count
        other = at ^ turn if count & (count - 1) == 0 else (at + turn) % count
        route.append((place, place + (other - at) * stride))
    return lax.ppermute(rows, axis, route)


def coordinate(way):
    axis, stride, count = way
    return ((lax.axis_index(axis) // stride) % count).astype(jnp.int32)


def fold(parts, lines, way, shared=0, after=()):
    count = 1 if way is None else way[2]
    height, width = parts[0].shape[0] - lines, parts[0].shape[1]
    share = height // count
    outs = [((share + shared, width), BF16)] * count
    if way is None:
        outs += [((lines, width), F32)] if lines else []
    elif lines > shared:
        outs += [((lines - shared, width), F32)]
    if share % 16 == 0:
        at = coordinate(way).reshape(1) if way else jnp.zeros((1,), jnp.int32)
        return launch(
            functools.partial(fold_kernel, len(parts), lines, shared, count),
            "fold",
            (1,),
            (at,),
            tuple(parts),
            [fixed(parts[0].shape)] * len(parts),
            outs,
            [fixed(shape) for shape, _ in outs],
            [pltpu.VMEM((height, width), BF16)] if count > 1 else [],
            micros=2,
            after=after,
        )
    total = sum(part.astype(F32) for part in parts)
    if way is None:
        return [total[:height].astype(BF16)] + ([total[height:]] if lines else [])
    at = coordinate(way)
    results = [
        jnp.concatenate(
            [
                lax.dynamic_slice_in_dim(total, apart(at, count, turn) * share, share, 0),
                total[height : height + shared],
            ],
            axis=0,
        ).astype(BF16)
        for turn in range(count)
    ]
    return results + ([total[height + shared :]] if lines > shared else [])


def swap(gives, way):
    return [gives[0]] + [exchange(gives[turn], way, turn) for turn in range(1, way[2])]


def fetch(own, way):
    return [own] + [exchange(own, way, turn) for turn in range(1, way[2])]


def spread(parts, way, after=()):
    own, count = parts[0], way[2]
    share, width = own.shape
    at = coordinate(way)
    if share % 16 == 0:
        (whole,) = launch(
            functools.partial(spread_kernel, count),
            "spread",
            (1,),
            (at.reshape(1),),
            tuple(parts),
            [fixed(own.shape)] * count,
            [((share * count, width), BF16)],
            [fixed((share * count, width))],
            micros=2,
            after=after,
        )
        return whole
    stack = jnp.stack(parts)
    turns = [at ^ place if count & (count - 1) == 0 else (at - place) % count for place in range(count)]
    return jnp.concatenate(
        [lax.dynamic_index_in_dim(stack, turn, 0, False) for turn in turns], axis=0
    )


def finish(own, got, width, squares, after):
    high = (lax.axis_index("dp") % 2).astype(jnp.int32).reshape(1)
    return launch(
        finish_kernel,
        "finish",
        (1,),
        (high,),
        (own, got),
        [fixed(own.shape)] * 2,
        [((width, width), F32)] * squares,
        [fixed((width, width))] * squares,
        micros=2,
        after=after,
    )


def on_device(
    tokens,
    memory,
    cotangent,
    target_length,
    memory_length,
    expert_of,
    self_norm_gain,
    self_norm_bias,
    self_query,
    self_key,
    self_value,
    self_out,
    self_query_bias,
    self_value_bias,
    self_out_bias,
    cross_norm_gain,
    cross_norm_bias,
    cross_query,
    cross_key,
    cross_value,
    cross_out,
    cross_attention_query_bias,
    cross_value_bias,
    cross_out_bias,
    expert_norm_gain,
    expert_norm_bias,
    expert_in,
    expert_in_bias,
    expert_out,
    expert_out_bias,
):
    seqs, length, width = tokens.shape
    mem_rows = memory.shape[1]
    local_count, _, hidden_width = expert_in.shape
    groups = lax.axis_size("expert")
    places = lax.axis_size("dp")
    own_group = lax.axis_index("expert")
    column = lax.axis_index("dp")

    shifts = list(range(1, groups)) + [0]
    whole = groups == seqs
    rows_shape, square = (length, width), (width, width)
    mem_shape, heads_shape = (mem_rows, width), (HEADS, length)
    turned = (width, length)
    in_smem = pl.BlockSpec(memory_space=pltpu.SMEM)
    order, picks, used, slot_of, spot_of, *grads = pl.pallas_call(
        functools.partial(plan_kernel, shifts, local_count),
        in_specs=[in_smem] * 3 + [pl.BlockSpec(memory_space=pltpu.VMEM)],
        out_specs=[in_smem] * 5 + [pl.BlockSpec(memory_space=pltpu.VMEM)] * groups,
        out_shape=[
            struct((seqs + 1,), jnp.int32),
            struct((groups,), jnp.int32),
            struct((groups,), jnp.int32),
            struct((seqs,), jnp.int32),
            struct((groups,), jnp.int32),
        ]
        + [struct(rows_shape, BF16)] * groups,
        compiler_params=pltpu.CompilerParams(vmem_limit_bytes=VMEM_LIMIT),
        name="plan",
    )(
        jnp.stack([own_group, column, jnp.int32(places)]).astype(jnp.int32),
        expert_of,
        target_length,
        cotangent,
    )

    def move(rows, slot, back=False):
        shift = shifts[slot]
        if shift == 0:
            return rows
        turn = -shift if back else shift
        return lax.ppermute(rows, "expert", [(g, (g + turn) % groups) for g in range(groups)])

    def arranged(per_slot):
        if whole:
            return per_slot
        stack = jnp.stack(per_slot)
        return [lax.dynamic_index_in_dim(stack, slot_of[at], 0, False) for at in range(seqs)]

    position = lambda shape, start=0: at_position(shape, start, seqs)
    sequence = lambda shape, start=0: at_sequence(shape, start, seqs)
    vectors = jnp.stack(
        [
            self_norm_gain,
            self_norm_bias,
            self_query_bias,
            self_value_bias,
            self_out_bias,
            cross_norm_gain,
            cross_norm_bias,
            cross_attention_query_bias,
            cross_value_bias,
            cross_out_bias,
            expert_norm_gain,
            expert_norm_bias,
        ]
        + [jnp.zeros_like(self_norm_gain)] * 4
    )
    self_matrices = (self_query, self_key, self_value, self_out)
    cross_matrices = (cross_query, cross_key, cross_value, cross_out)
    half = seqs // 2
    high = (column % 2).astype(jnp.int32).reshape(1)
    grads_in = [move(grads[slot], slot) for slot in range(groups)]

    saved = [
        (rows_shape, F32),
        (rows_shape, F32),
        (rows_shape, BF16),
        (rows_shape, BF16),
        (rows_shape, BF16),
        (turned, BF16),
        (heads_shape, F32),
        (rows_shape, BF16),
        (mem_shape, BF16),
        (mem_shape, BF16),
        (turned, BF16),
        (heads_shape, F32),
    ]

    def forward(start, steps, kept, after):
        results = launch(
            functools.partial(forward_kernel, start, steps),
            "forward",
            (steps,),
            (order, target_length, memory_length),
            (tokens, memory, vectors) + self_matrices + cross_matrices,
            [sequence(rows_shape, start), sequence(mem_shape, start), fixed(vectors.shape)]
            + [fixed(square)] * 8,
            [(rows_shape, BF16)] * steps + [((seqs,) + shape, kind) for shape, kind in saved],
            [fixed(rows_shape)] * steps + [position(shape, start) for shape, _ in saved],
            [pltpu.VMEM(turned, BF16)],
            micros=12 * steps,
            after=after,
            into={at + steps: item for at, item in enumerate(kept)},
        )
        return results[:steps], results[steps:]

    normed_one, kept = forward(0, half, [], [])
    normed_two, kept = forward(half, seqs - half, kept, [grads_in[0]])
    normed = list(normed_one) + list(normed_two)
    (
        later,
        middle,
        query_one,
        key_one,
        value_one,
        context_one,
        logsum_one,
        query_two,
        key_two,
        value_two,
        context_two,
        logsum_two,
    ) = kept

    if whole:
        rows_in = [move(normed[slot], slot) for slot in range(groups)]
    else:
        joined = jnp.stack(normed)
        rows_in = [
            move(lax.dynamic_index_in_dim(joined, spot_of[slot], 0, False), slot)
            for slot in range(groups)
        ]
    tiles = 4
    tile_width = hidden_width // tiles
    hidden_tile = pl.BlockSpec((length, tile_width), lambda t, *_: (0, t))
    line_tile = pl.BlockSpec((1, tile_width), lambda t, *_: (0, t))
    hidden, grad_pre, made, grad_rows, pre_sum, grads_sum = {}, {}, {}, {}, {}, {}

    def expert(slot, after):
        results = launch(
            functools.partial(expert_kernel, slot),
            "expert",
            (tiles,),
            (picks, used),
            (rows_in[slot], grads_in[slot], expert_in, expert_in_bias, expert_out, expert_out_bias),
            [
                fixed(rows_shape),
                fixed(rows_shape),
                pl.BlockSpec((1, width, tile_width), lambda t, pick, _: (pick[slot], 0, t)),
                pl.BlockSpec((local_count, tile_width), lambda t, *_: (0, t)),
                pl.BlockSpec((1, tile_width, width), lambda t, pick, _: (pick[slot], t, 0)),
                fixed((local_count, width)),
            ],
            [((length, hidden_width), BF16)] * 2
            + [(rows_shape, BF16)] * 2
            + [((1, hidden_width), F32), ((1, width), F32)],
            [hidden_tile, hidden_tile, fixed(rows_shape), fixed(rows_shape), line_tile]
            + [fixed((1, width))],
            [pltpu.VMEM(rows_shape, F32)] * 2,
            micros=1,
            after=after,
        )
        for table, result in zip((hidden, grad_pre, made, grad_rows, pre_sum, grads_sum), results):
            table[slot] = result

    back_scratch = [
        pltpu.VMEM((width, mem_rows), BF16),
        pltpu.VMEM(rows_shape, BF16),
        pltpu.VMEM(heads_shape, F32),
        pltpu.VMEM(turned, BF16),
    ]

    def sums_shape(count, final, lines=0):
        if final:
            return [((count * width // 2 + lines, width), BF16)] * 2
        return [((count,) + square, F32)]

    def cross_back(start, steps, grads, given, filled, final, after, carry=()):
        first = given is None
        total = sums_shape(5, final)
        return launch(
            functools.partial(cross_back_kernel, start, first, final, steps),
            "cross_back",
            (steps,),
            (order, target_length, memory_length, high),
            tuple(grads)
            + (() if first else tuple(given))
            + (cotangent, memory, later, middle, query_two, key_two, value_two, context_two)
            + (logsum_two, context_one, vectors)
            + cross_matrices,
            [once(rows_shape)] * steps
            + ([] if first else [once((5,) + square), once((8, width))])
            + [
                sequence(rows_shape, start),
                sequence(mem_shape, start),
                position(rows_shape, start),
                position(rows_shape, start),
                position(rows_shape, start),
                position(mem_shape, start),
                position(mem_shape, start),
                position(turned, start),
                position(heads_shape, start),
                position(turned, start),
                fixed(vectors.shape),
            ]
            + [once(square)] * 4,
            [((seqs,) + rows_shape, F32)]
            + [((seqs,) + mem_shape, BF16)] * 2
            + total
            + [((8, width), F32)],
            [position(rows_shape, start), position(mem_shape, start), position(mem_shape, start)]
            + [fixed(shape) for shape, _ in total]
            + [fixed((8, width))],
            [pltpu.VMEM((5,) + square, F32), pltpu.VMEM((8, width), F32), pltpu.VMEM(rows_shape, BF16)]
            + back_scratch,
            micros=13 * steps,
            after=after,
            into={at: item for at, item in enumerate(filled)},
            carry=carry,
        )

    def self_back(start, steps, given, filled, final, after):
        first = given is None
        total = sums_shape(3, final, LINES) if final else sums_shape(3, final) + [((8, width), F32)]
        return launch(
            functools.partial(self_back_kernel, start, first, final),
            "self_back",
            (steps,),
            (order, target_length, high),
            (() if first else tuple(given))
            + (cross_lines, expert_lines)
            + (tokens, grad_middle, query_one, key_one, value_one, context_one, logsum_one, columns)
            + self_matrices,
            ([] if first else [once((3,) + square), once((8, width))])
            + [fixed((8, width)), fixed((EXPERT_LINES, width))]
            + [
                sequence(rows_shape, start),
                position(rows_shape, start),
                position(rows_shape, start),
                position(rows_shape, start),
                position(rows_shape, start),
                position(turned, start),
                position(heads_shape, start),
                fixed(columns.shape),
            ]
            + [once(square)] * 4,
            [((seqs,) + rows_shape, BF16)] * 3 + total,
            [position(rows_shape, start)] * 3 + [fixed(shape) for shape, _ in total],
            [pltpu.VMEM((3,) + square, F32), pltpu.VMEM((8, width), F32)] + back_scratch,
            micros=10 * steps,
            after=after,
            into={at: item for at, item in enumerate(filled)},
        )

    back = {}

    def send_back(slot):
        back[slot] = move(grad_rows[slot], slot, True)

    if whole:
        expert(3, [])
        expert(0, [made[3]])
        expert(1, [made[0]])
        expert(2, [made[1]])
        for slot in range(groups):
            send_back(slot)
    else:
        for slot in range(groups):
            expert(slot, [])
            send_back(slot)

    in_sums, out_sums, expert_lines = launch(
        functools.partial(expert_weights_kernel, groups),
        "expert_weights",
        (tiles,),
        (picks, used),
        tuple(rows_in)
        + tuple(grads_in)
        + tuple(table[slot] for table in (hidden, grad_pre, pre_sum, grads_sum) for slot in range(groups)),
        [once(rows_shape)] * (2 * groups)
        + [hidden_tile] * (2 * groups)
        + [line_tile] * groups
        + [fixed((1, width))] * groups,
        [
            ((local_count, width, hidden_width), BF16),
            ((local_count, hidden_width, width), BF16),
            ((EXPERT_LINES, width), F32),
        ],
        [
            pl.BlockSpec((local_count, width, tile_width), lambda t, *_: (0, 0, t)),
            pl.BlockSpec((local_count, tile_width, width), lambda t, *_: (0, t, 0)),
            fixed((EXPERT_LINES, width)),
        ],
        [
            pltpu.VMEM((local_count, width, tile_width), F32),
            pltpu.VMEM((local_count, tile_width, width), F32),
            pltpu.VMEM((local_count, 1, tile_width), F32),
            pltpu.VMEM((local_count, 1, width), F32),
        ],
        micros=17,
        after=[back[0]] if whole else [],
    )
    expert_in_grad = lax.psum_scatter(in_sums, "dp", scatter_dimension=1, tiled=True)
    expert_out_grad = lax.psum_scatter(out_sums, "dp", scatter_dimension=1, tiled=True)

    if whole:
        away = [slot for slot in range(groups) if shifts[slot]]
        results = cross_back(
            3, 2, [back[3], back[0]], None, [], False, [in_sums], [made[slot] for slot in away]
        )
        filled, (weights_run, vectors_run) = results[:3], results[3:5]
        for at, slot in enumerate(away):
            made[slot] = results[5 + at]
        made_home = [move(made[slot], slot, True) for slot in range(groups)]
        *results, cross_keep, cross_give, cross_lines = cross_back(
            1, 2, [back[1], back[2]], (weights_run, vectors_run), filled, True, []
        )
    else:
        *results, cross_keep, cross_give, cross_lines = cross_back(
            0, seqs, arranged([back[slot] for slot in range(groups)]), None, [], True, []
        )
        made_home = arranged([move(made[slot], slot, True) for slot in range(groups)])
    grad_middle, grad_key_two, grad_value_two = results

    chips = places // 2
    core, plane, line = ("dp", 1, 2), ("dp", 2, chips), ("expert", 1, groups)
    columns = jnp.concatenate([vectors.T, jnp.zeros((width, 128 - vectors.shape[0]), F32)], axis=1)

    cross_got = exchange(cross_give, core, 1)
    *filled, weights_run, vectors_run = self_back(0, half, None, [], False, made_home[:2])
    cross_parts = swap(fold([cross_keep, cross_got], 0, plane, after=filled[:1]), plane)
    *results, self_keep, self_give = self_back(
        half, seqs - half, (weights_run, vectors_run), filled, True, cross_parts[:1] + made_home[2:3]
    )
    grad_query_one, grad_key_one, grad_value_one = results

    def tokens_back(start, steps, filled, after):
        return launch(
            functools.partial(tokens_back_kernel, start),
            "tokens_back",
            (steps,),
            (order, target_length),
            (tokens, grad_middle, grad_query_one, grad_key_one, grad_value_one, vectors)
            + self_matrices[:3],
            [sequence(rows_shape, start)]
            + [position(rows_shape, start)] * 4
            + [fixed(vectors.shape)]
            + [once(square)] * 3,
            [((seqs,) + rows_shape, F32)],
            [sequence(rows_shape, start)],
            micros=4 * steps,
            after=after,
            into={at: item for at, item in enumerate(filled)},
        )

    self_got = exchange(self_give, core, 1)
    cross_line = swap(fold(cross_parts, 0, line, after=[self_give]), line)
    filled = tokens_back(0, half, [], cross_line[:1])

    self_parts = swap(fold([self_keep, self_got], LINES, plane, LINES, after=filled), plane)
    cross_share = fold(cross_line, 0, None, after=filled)[0]
    cross_got = fetch(cross_share, line)
    (tokens_grad,) = tokens_back(half, seqs - half, filled, [cross_share, self_parts[0]])

    *self_gives, own_lines = fold(self_parts, LINES, line, SHARED_LINES, after=[tokens_grad])
    self_line = swap(self_gives, line)
    cross_plane = spread(cross_got, line, after=[tokens_grad])
    cross_got = fetch(cross_plane, plane)
    (memory_grad,) = launch(
        memory_back_kernel,
        "memory_back",
        (seqs,),
        (order,),
        (grad_key_two, grad_value_two, cross_key, cross_value),
        [position(mem_shape)] * 2 + [once(square)] * 2,
        [((seqs,) + mem_shape, F32)],
        [sequence(mem_shape)],
        micros=5,
        after=[self_line[0], cross_plane],
    )

    self_share, totals = fold(self_line, SHARED_LINES, None, after=[memory_grad])
    self_got = fetch(self_share, line)
    cross_half = spread(cross_got, plane, after=[memory_grad])
    cross_got = exchange(cross_half, core, 1)
    (output,) = launch(
        functools.partial(output_kernel, seqs),
        "output",
        (seqs,),
        (order, target_length),
        (later, *made_home),
        [position(rows_shape)] + [once(rows_shape)] * seqs,
        [((seqs,) + rows_shape, BF16)],
        [sequence(rows_shape)],
        micros=5,
        after=[self_share, cross_half],
    )

    self_plane = spread(self_got, line, after=[output])
    self_got = fetch(self_plane, plane)
    cross_q, cross_k, cross_v, cross_o, self_o = finish(cross_half, cross_got, width, 5, [self_plane])
    shares = (expert_in_grad, expert_out_grad)
    expert_in_grad, expert_out_grad = launch(
        cast_kernel,
        "cast",
        (1,),
        (),
        shares,
        [fixed(item.shape) for item in shares],
        [(item.shape, F32) for item in shares],
        [fixed(item.shape) for item in shares],
        micros=3,
        after=[self_plane],
    )
    self_half = spread(self_got, plane, after=[cross_q, expert_in_grad])
    self_q, self_k, self_v = finish(self_half, exchange(self_half, core, 1), width, 3, [])

    in_count = local_count * hidden_width // width
    in_bias = own_lines[:in_count].reshape(local_count, hidden_width)
    out_bias = own_lines[in_count : in_count + local_count]
    in_share, out_share = hidden_width // places, width // places
    return (
        output,
        tokens_grad,
        memory_grad,
        totals[2],
        totals[3],
        self_q,
        self_k,
        self_v,
        self_o,
        totals[0],
        totals[1],
        totals[15],
        totals[13],
        totals[14],
        cross_q,
        cross_k,
        cross_v,
        cross_o,
        totals[12],
        totals[11],
        totals[10],
        totals[8],
        totals[9],
        expert_in_grad,
        lax.dynamic_slice_in_dim(in_bias, column * in_share, in_share, 1),
        expert_out_grad,
        lax.dynamic_slice_in_dim(out_bias, column * out_share, out_share, 1),
    )


def solution(mesh):
    rows = P(("expert", "dp"), None, None)
    counts = P(("expert", "dp"))
    split = (P("expert", None, None), P("expert", None)) * 2
    shares = (P("expert", "dp", None), P("expert", "dp")) * 2
    return jax.shard_map(
        on_device,
        mesh=mesh,
        in_specs=(rows,) * 3 + (counts,) * 2 + (P(),) * 21 + split,
        out_specs=(rows,) * 3 + (P(),) * 20 + shares,
        check_vma=False,
    )
```

time: 559 us -> 410 us (0.73)
  waiting for transfers between devices: 152 us -> 20.6 us
  Pallas kernels: 243 us -> 285 us
  blocking collectives: 38.1 us -> 0 us
  other arithmetic: 22.5 us -> 0.59 us
  local copies, waits for them, and re-layouts: 29.8 us -> 13.8 us
  starting transfers between devices: 52.2 us -> 68.2 us
    ppermute x12, waiting for transfers between devices: 108 us -> 12 us  [move(): lax.ppermute(rows, 'expert', [(g, (g + turn) % groups) for g in range(gro...]
    pallas_call x9 -> x29, Pallas kernels: 243 us -> 285 us  [the longest x28 282 us: launch(): pl.pallas_call(body, grid_spec=pltpu.PrefetchScalarGridSpec(num_scalar_pr...]
    psum x1 -> x0, blocking collectives: 38.1 us -> none  [on_device(): lax.psum(jnp.concatenate([self_sums, cross_sums], axis=0), ('expert', 'dp'))]
    ppermute x20 -> x28, waiting for transfers between devices: 42.9 us -> 8.5 us  [exchange(): return lax.ppermute(rows, axis, route)]
    ppermute x12, starting transfers between devices: 19.5 us -> 36.5 us  [move(): lax.ppermute(rows, 'expert', [(g, (g + turn) % groups) for g in range(gro...]
    convert_element_type x17 -> x0, other arithmetic: 14.4 us -> none  [the longest x10 3.72 us: halves_step(): kept.append((mine.astype(F32) + got.astype(F32)).astype(BF16))]
    ppermute x20 -> x28, starting transfers between devices: 32.6 us -> 31.6 us  [exchange(): return lax.ppermute(rows, axis, route)]
  transfers between devices with their start and end apart: 36 -> 42, of which waited for: 18 -> 6; matrix products, arithmetic and copies ran while one was open for 7% -> 1% of each run, Pallas kernels for 25% -> 64%
where the time goes in v2:
time: 410 us; the launch traced here: 403 us
  Pallas kernels  285 us (70%)
  starting transfers between devices  68.2 us (17%)
  waiting for transfers between devices  20.6 us (5%)
  between operations  14.9 us (4%)
  local copies, waits for them, and re-layouts  13.8 us (3%)
    pallas_call x28, Pallas kernels, launch(): pl.pallas_call(body, grid_spec=pltpu.PrefetchScalarGridSpec(num_scalar_pr...  282 us
    ppermute x12, starting transfers between devices, move(): lax.ppermute(rows, 'expert', [(g, (g + turn) % groups) for g in range(gro...  36.5 us
    ppermute x28, starting transfers between devices, exchange(): return lax.ppermute(rows, axis, route)  31.6 us
    ppermute x12, waiting for transfers between devices, move(): lax.ppermute(rows, 'expert', [(g, (g + turn) % groups) for g in range(gro...  12 us
    unnamed x73, local copies, waits for them, and re-layouts  9.98 us
    ppermute x28, waiting for transfers between devices, exchange(): return lax.ppermute(rows, axis, route)  8.5 us
  transfers between devices with their start and end apart: 42, of which 6 were waited for; matrix products, arithmetic and copies ran while one was open for 1% of the time, Pallas kernels for 64%

profile of v2, /device:TPU:0, one launch (start us, length us, event | category | flops | bytes accessed | tf_op | source)
XLA Modules:
  0.0 403.1 jit_solution(15373630457971370083)
XLA Ops:
  8.0 3.4 plan.1
  11.3 3.1 collective-permute-start
  14.4 2.6 collective-permute-start.5
  19.7 26.5 %forward.2 = (bf16[512,512]{1,0:T(8,128)(2,1)}, bf16[512,512]{1,0:T(8,128)(2,1)}, f32[4,512,512]{2,1,0:T(8,128)}, f32[4,512,512]{2,1,0:T(8,128)}, bf16[4,512,512...) custom-call(s32[5]{0:T(128)} %get-tuple-element.142.refs_0_, ...), custom_call_target="tpu_custom_call" | custom-call | flops 24000000000 | bytes 48000000 | tf_op jit(solution)/shard_map/forward/pallas_call | solution.py:922
  48.6 26.5 %forward.3 = (bf16[512,512]{1,0:T(8,128)(2,1)}, bf16[512,512]{1,0:T(8,128)(2,1)}, f32[4,512,512]{2,1,0:T(8,128)}, f32[4,512,512]{2,1,0:T(8,128)}, bf16[4,512,512...) custom-call(s32[5]{0:T(128)} %get-tuple-element.142.refs_0_, ...), custom_call_target="tpu_custom_call", output_to_operand_aliasing={{2}: (15, {}), {3}: (16, {}), {4}: (17, {}), {5}: (18, {}),... | custom-call | flops 24000000000 | bytes 48000000 | tf_op jit(solution)/shard_map/forward/pallas_call | solution.py:922
  75.1 2.8 collective-permute-start.4
  78.0 10.1 %expert.4 = (bf16[512,2048]{1,0:T(8,128)(2,1)}, bf16[512,2048]{1,0:T(8,128)(2,1)}, bf16[512,512]{1,0:T(8,128)(2,1)}, bf16[512,512]{1,0:T(8,128)(2,1)}, f32[1,2048]{1,0:T(1,128)}, /*index=5*/f32[1,512]{1,0:T(1,128)}) custom-call(s32[4]{0:T(128)} %get-tuple-element.157.refs_0_, s32[4]{0:T(128)} %get-tuple-element.158.refs_1_, ...), custom_call_target="tpu_custom_call" | custom-call | flops 1000000000 | bytes 2000000 | tf_op jit(solution)/shard_map/expert/pallas_call | solution.py:922
  88.1 10.1 %expert.5 = (bf16[512,2048]{1,0:T(8,128)(2,1)}, bf16[512,2048]{1,0:T(8,128)(2,1)}, bf16[512,512]{1,0:T(8,128)(2,1)}, bf16[512,512]{1,0:T(8,128)(2,1)}, f32[1,2048]{1,0:T(1,128)}, /*index=5*/f32[1,512]{1,0:T(1,128)}) custom-call(s32[4]{0:T(128)} %get-tuple-element.157.refs_0_, s32[4]{0:T(128)} %get-tuple-element.158.refs_1_, ...), custom_call_target="tpu_custom_call" | custom-call | flops 1000000000 | bytes 2000000 | tf_op jit(solution)/shard_map/expert/pallas_call | solution.py:922
  98.2 4.0 %collective-permute-start.2 = (bf16[512,512]{1,0:T(8,128)(2,1)}, bf16[512,512]{1,0:T(8,128)(2,1)}, u32[]{:S(2)}, u32[]{:S(2)}) collective-permute-start(bf16[512,512]{1,0:T(8,128)(2,1)} %get-tuple-element.164), channel_id=1, source_target_pairs={{0,24},{8,0},{16,8},{24,16},{1,25},{9,1},{17,9},{25,17},{2,26},{10... | collective-permute-start | bytes 1572872 | tf_op jit(solution)/shard_map/ppermute | solution.py:1121
  102.3 10.1 %expert.6 = (bf16[512,2048]{1,0:T(8,128)(2,1)}, bf16[512,2048]{1,0:T(8,128)(2,1)}, bf16[512,512]{1,0:T(8,128)(2,1)}, bf16[512,512]{1,0:T(8,128)(2,1)}, f32[1,2048]{1,0:T(1,128)}, /*index=5*/f32[1,512]{1,0:T(1,128)}) custom-call(s32[4]{0:T(128)} %get-tuple-element.157.refs_0_, s32[4]{0:T(128)} %get-tuple-element.158.refs_1_, ...), custom_call_target="tpu_custom_call" | custom-call | flops 1000000000 | bytes 2000000 | tf_op jit(solution)/shard_map/expert/pallas_call | solution.py:922
  113.2 10.1 %expert.7 = (bf16[512,2048]{1,0:T(8,128)(2,1)}, bf16[512,2048]{1,0:T(8,128)(2,1)}, bf16[512,512]{1,0:T(8,128)(2,1)}, bf16[512,512]{1,0:T(8,128)(2,1)}, f32[1,2048]{1,0:T(1,128)}, /*index=5*/f32[1,512]{1,0:T(1,128)}) custom-call(s32[4]{0:T(128)} %get-tuple-element.157.refs_0_, s32[4]{0:T(128)} %get-tuple-element.158.refs_1_, bf16[512,512]{1,0:T(8,128)(2,1)} %copy-done.1, ...), custom_call_target="tpu_custom_call" | custom-call | flops 1000000000 | bytes 2000000 | tf_op jit(solution)/shard_map/expert/pallas_call | solution.py:922
  123.3 20.0 %expert_weights.1 = (bf16[2,512,2048]{2,1,0:T(8,128)(2,1)}, bf16[2,2048,512]{2,1,0:T(8,128)(2,1)}, f32[16,512]{1,0:T(8,128)}) custom-call(s32[4]{0:T(128)} %get-tuple-element.157.refs_0_, s32[4]{0:T(128)} %get-tuple-element.158.refs_1_, bf16[512,512]{1,0:T(8,128)(2,1)} %collective-permute-done.1.refs_2_, ...), custom_call_target="tpu_custom_call" | custom-call | flops 16999999488 | bytes 34000000 | tf_op jit(solution)/shard_map/expert_weights/pallas_call | solution.py:922
  144.9 6.1 %collective-permute-start.10 = (bf16[512,512]{1,0:T(8,128)(2,1)}, bf16[512,512]{1,0:T(8,128)(2,1)}, u32[]{:S(2)}, u32[]{:S(2)}) collective-permute-start(bf16[512,512]{1,0:T(8,128)(2,1)} %get-tuple-element.199), channel_id=1, source_target_pairs={{0,16},{8,24},{16,0},{24,8},{1,17},{9,25},{17,1},{25,9},{2,18},{10... | collective-permute-start | bytes 1572872 | tf_op jit(solution)/shard_map/ppermute | solution.py:1121
  151.1 12.4 %collective-permute-start.11 = (bf16[512,512]{1,0:T(8,128)(2,1)}, bf16[512,512]{1,0:T(8,128)(2,1)}, u32[]{:S(2)}, u32[]{:S(2)}) collective-permute-start(bf16[512,512]{1,0:T(8,128)(2,1)} %get-tuple-element.200), channel_id=1, source_target_pairs={{0,8},{8,16},{16,24},{24,0},{1,9},{9,17},{17,25},{25,1},{2,10},{10... | collective-permute-start | bytes 1572872 | tf_op jit(solution)/shard_map/ppermute | solution.py:1121
  163.5 30.7 %cross_back.2 = (f32[4,512,512]{2,1,0:T(8,128)}, bf16[4,512,512]{2,1,0:T(8,128)(2,1)}, bf16[4,512,512]{2,1,0:T(8,128)(2,1)}, f32[5,512,512]{2,1,0:T(8,128)}, f32...) custom-call(s32[5]{0:T(128)} %get-tuple-element.142.refs_0_, ...), custom_call_target="tpu_custom_call", output_to_operand_aliasing={{5}: (22, {}), {6}: (23, {}), {7}: (24, {})} | custom-call | flops 25999998976 | bytes 52000000 | tf_op jit(solution)/shard_map/cross_back/pallas_call | solution.py:922
  196.7 30.9 %cross_back.3 = (f32[4,512,512]{2,1,0:T(8,128)}, bf16[4,512,512]{2,1,0:T(8,128)(2,1)}, bf16[4,512,512]{2,1,0:T(8,128)(2,1)}, bf16[1280,512]{1,0:T(8,128)(2,1)}, ...) custom-call(s32[5]{0:T(128)} %get-tuple-element.142.refs_0_, ...), custom_call_target="tpu_custom_call", output_to_operand_aliasing={{0}: (23, {}), {1}: (24, {}), {2}: (25, {})} | custom-call | flops 25999998976 | bytes 52000000 | tf_op jit(solution)/shard_map/cross_back/pallas_call | solution.py:922
  227.7 12.0 %collective-permute-done.8.refs_18_.refs_4_ = bf16[512,512]{1,0:T(8,128)(2,1)} collective-permute-done((bf16[512,512]{1,0:T(8,128)(2,1)}, bf16[512,512]{1,0:T(8,128)(2,1)}, u32[]{:S(2)}, u32[]{:S(2)}) %collective-permute-start.8) | collective-permute-done | bytes 524320 | tf_op jit(solution)/shard_map/ppermute | solution.py:1121
  239.7 22.8 %self_back.2 = (bf16[4,512,512]{2,1,0:T(8,128)(2,1)}, bf16[4,512,512]{2,1,0:T(8,128)(2,1)}, bf16[4,512,512]{2,1,0:T(8,128)(2,1)}, f32[3,512,512]{2,1,0:T(8,128)}, f32[8,512]{1,0:T(8,128)}) custom-call(s32[5]{0:T(128)} %get-tuple-element.142.refs_0_, s32[4]{0:T(128)} %refs_1_.17, s32[1]{0:T(128)} %bitcast.14.refs_3_.refs_2_.refs_0_, ...), custom_call_target="tpu_custom_call" | custom-call | flops 20000000000 | bytes 40000000 | tf_op jit(solution)/shard_map/self_back/pallas_call | solution.py:922
  262.5 3.5 fold.6
  269.5 24.8 %self_back.3 = (bf16[4,512,512]{2,1,0:T(8,128)(2,1)}, bf16[4,512,512]{2,1,0:T(8,128)(2,1)}, bf16[4,512,512]{2,1,0:T(8,128)(2,1)}, bf16[800,512]{1,0:T(8,128)(2,1)}, bf16[800,512]{1,0:T(8,128)(2,1)}) custom-call(s32[5]{0:T(128)} %get-tuple-element.142.refs_0_, s32[4]{0:T(128)} %refs_1_.17, ...), custom_call_target="tpu_custom_call", output_to_operand_aliasing={{0}: (21, {}), {1}: (22, {}), {2}: (23, {})} | custom-call | flops 20000000000 | bytes 40000000 | tf_op jit(solution)/shard_map/self_back/pallas_call | solution.py:922
  296.8 4.4 %collective-permute-start.22 = (bf16[80,512]{1,0:T(8,128)(2,1)}, bf16[80,512]{1,0:T(8,128)(2,1)}, u32[]{:S(2)}, u32[]{:S(2)}) collective-permute-start(bf16[80,512]{1,0:T(8,128)(2,1)} %get-tuple-element.236), channel_id=1, source_target_pairs={{0,24},{8,16},{16,8},{24,0},{1,25},{9,17},{17,9},{25,1},{2,26},{10... | collective-permute-start | bytes 245768 | tf_op jit(solution)/shard_map/ppermute | solution.py:951
  301.1 7.1 %tokens_back.2.refs_3_.refs_5_.refs_13_ = f32[4,512,512]{2,1,0:T(8,128)} custom-call(s32[5]{0:T(128)} %get-tuple-element.142.refs_0_, s32[4]{0:T(128)} %refs_1_.17, bf16[4,512,512]{2,1,0:T(8,128)(2,1)} %refs_2_.11, f32[4,512,512]{2,1,0:T(8,128)} %get-tuple-element.208.refs_6_.refs_8_.refs_3_, bf16[4,512,512]{2,1,0:T(8,128)(2,1)} %get-tuple-element.223.refs_4_, ...), custom_call_target="tpu_custom_call" | custom-call | flops 8000000000 | bytes 16000000 | tf_op jit(solution)/shard_map/tokens_back/pallas_call | solution.py:922
  311.9 3.2 collective-permute-start.26
  315.9 2.7 fold.8
  322.1 7.1 %tokens_back.3.refs_5_ = f32[4,512,512]{2,1,0:T(8,128)} custom-call(s32[5]{0:T(128)} %get-tuple-element.142.refs_0_, s32[4]{0:T(128)} %refs_1_.17, bf16[4,512,512]{2,1,0:T(8,128)(2,1)} %refs_2_.11, f32[4,512,512]{2,1,0:T(8,128)} %get-tuple-element.208.refs_6_.refs_8_.refs_3_, ...), custom_call_target="tpu_custom_call", output_to_operand_aliasing={{}: (13, {})} | custom-call | flops 8000000000 | bytes 16000000 | tf_op jit(solution)/shard_map/tokens_back/pallas_call | solution.py:922
  337.3 7.1 %memory_back.1.refs_5_ = f32[4,512,512]{2,1,0:T(8,128)} custom-call(s32[5]{0:T(128)} %get-tuple-element.142.refs_0_, bf16[4,512,512]{2,1,0:T(8,128)(2,1)} %get-tuple-element.241.refs_1_, bf16[4,512,512]{2,1,0:T(8,128)(2,1)} %get-tuple-element.242.refs_2_, bf16[512,512]{1,0:T(8,128)(2,1)} %refs_3_.5, bf16[512,512]{1,0:T(8,128)(2,1)} %refs_4_.13, ...), custom_call_target="tpu_custom_call" | custom-call | flops 5000000000 | bytes 10000000 | tf_op jit(solution)/shard_map/memory_back/pallas_call | solution.py:922
  344.4 3.0 collective-permute-done.30.refs_3_
  352.1 3.5 collective-permute-start.25
  356.9 3.4 collective-permute-done.24.refs_3_
  367.6 5.8 %output.1.refs_5_ = bf16[4,512,512]{2,1,0:T(8,128)(2,1)} custom-call(s32[5]{0:T(128)} %get-tuple-element.142.refs_0_, s32[4]{0:T(128)} %refs_1_.17, f32[4,512,512]{2,1,0:T(8,128)} %get-tuple-element.156.refs_8_.refs_10_.refs_2_, bf16[512,512]{1,0:T(8,128)(2,1)} %copy-done.19, bf16[512,512]{1,0:T(8,128)(2,1)} %collective-permute-done.8.refs_18_.refs_4_, ...), custom_call_target="tpu_custom_call" | custom-call | flops 5000000000 | bytes 10000000 | tf_op jit(solution)/shard_map/output/pallas_call | solution.py:922
  379.7 4.2 %finish.2 = (f32[512,512]{1,0:T(8,128)}, f32[512,512]{1,0:T(8,128)}, f32[512,512]{1,0:T(8,128)}, f32[512,512]{1,0:T(8,128)}, f32[512,512]{1,0:T(8,128)}) custom-call(s32[1]{0:T(128)} %bitcast.14.refs_3_.refs_2_.refs_0_, bf16[1280,512]{1,0:T(8,128)(2,1)} %spread.5.refs_8_.refs_1_, bf16[1280,512]{1,0:T(8,128)(2,1)} %collective-permute-done.38.refs_2_, ...), custom_call_target="tpu_custom_call" | custom-call | flops 2000000000 | bytes 4000000 | tf_op jit(solution)/shard_map/finish/pallas_call | solution.py:922
  392.9 3.2 finish.3
  (166 shorter events, 60.9 us)
Async XLA Ops:
  7.3 376.6 %reduce-scatter.5.cloned.1.call-start = ((), (), s32[]{:S(2)}) async-start(), calls=%async_computation.3 | async-start | bytes 4718592 | tf_op jit(solution)/shard_map/reduce_scatter | solution.py:1384
  11.3 36.4 %collective-permute-start = (bf16[512,512]{1,0:T(8,128)(2,1)}, bf16[512,512]{1,0:T(8,128)(2,1)S(1)}, u32[]{:S(2)}, u32[]{:S(2)}) collective-permute-start(bf16[512,512]{1,0:T(8,128)(2,1)} %get-tuple-element.143), channel_id=1, source_target_pairs={{0,8},{8,16},{16,24},{24,0},{1,9},{9,17},{17,25},{25,1},{2,10},{10... | collective-permute-start | bytes 1572872 | tf_op jit(solution)/shard_map/ppermute | solution.py:1121
  14.4 87.8 %collective-permute-start.5 = (bf16[512,512]{1,0:T(8,128)(2,1)}, bf16[512,512]{1,0:T(8,128)(2,1)}, u32[]{:S(2)}, u32[]{:S(2)}) collective-permute-start(bf16[512,512]{1,0:T(8,128)(2,1)} %get-tuple-element.174), channel_id=1, source_target_pairs={{0,16},{8,24},{16,0},{24,8},{1,17},{9,25},{17,1},{25,9},{2,18},{10... | collective-permute-start | bytes 1572872 | tf_op jit(solution)/shard_map/ppermute | solution.py:1121
  17.0 95.3 %collective-permute-start.6 = (bf16[512,512]{1,0:T(8,128)(2,1)}, bf16[512,512]{1,0:T(8,128)(2,1)}, u32[]{:S(2)}, u32[]{:S(2)}) collective-permute-start(bf16[512,512]{1,0:T(8,128)(2,1)} %get-tuple-element.175), channel_id=1, source_target_pairs={{0,24},{8,0},{16,8},{24,16},{1,25},{9,1},{17,9},{25,17},{2,26},{10... | collective-permute-start | bytes 1572872 | tf_op jit(solution)/shard_map/ppermute | solution.py:1121
  46.2 41.8 %collective-permute-start.1 = (bf16[512,512]{1,0:T(8,128)(2,1)}, bf16[512,512]{1,0:T(8,128)(2,1)}, u32[]{:S(2)}, u32[]{:S(2)}) collective-permute-start(bf16[512,512]{1,0:T(8,128)(2,1)} %get-tuple-element.162), channel_id=1, source_target_pairs={{0,8},{8,16},{16,24},{24,0},{1,9},{9,17},{17,25},{25,1},{2,10},{10... | collective-permute-start | bytes 1572872 | tf_op jit(solution)/shard_map/ppermute | solution.py:1121
  47.4 54.8 %collective-permute-start.3 = (bf16[512,512]{1,0:T(8,128)(2,1)}, bf16[512,512]{1,0:T(8,128)(2,1)}, u32[]{:S(2)}, u32[]{:S(2)}) collective-permute-start(bf16[512,512]{1,0:T(8,128)(2,1)} %get-tuple-element.172), channel_id=1, source_target_pairs={{0,16},{8,24},{16,0},{24,8},{1,17},{9,25},{17,1},{25,9},{2,18},{10... | collective-permute-start | bytes 1572872 | tf_op jit(solution)/shard_map/ppermute | solution.py:1121
  75.1 37.2 %collective-permute-start.4 = (bf16[512,512]{1,0:T(8,128)(2,1)}, bf16[512,512]{1,0:T(8,128)(2,1)S(1)}, u32[]{:S(2)}, u32[]{:S(2)}) collective-permute-start(bf16[512,512]{1,0:T(8,128)(2,1)} %get-tuple-element.173), channel_id=1, source_target_pairs={{0,24},{8,0},{16,8},{24,16},{1,25},{9,1},{17,9},{25,17},{2,26},{10... | collective-permute-start | bytes 1572872 | tf_op jit(solution)/shard_map/ppermute | solution.py:1121
  98.2 25.1 %collective-permute-start.2 = (bf16[512,512]{1,0:T(8,128)(2,1)}, bf16[512,512]{1,0:T(8,128)(2,1)}, u32[]{:S(2)}, u32[]{:S(2)}) collective-permute-start(bf16[512,512]{1,0:T(8,128)(2,1)} %get-tuple-element.164), channel_id=1, source_target_pairs={{0,24},{8,0},{16,8},{24,16},{1,25},{9,1},{17,9},{25,17},{2,26},{10... | collective-permute-start | bytes 1572872 | tf_op jit(solution)/shard_map/ppermute | solution.py:1121
  143.3 240.5 %reduce-scatter.3.cloned.1.call-start = ((), (), s32[]{:S(2)}) async-start(), calls=%async_computation.2 | async-start | bytes 4718592 | tf_op jit(solution)/shard_map/reduce_scatter | solution.py:1383
  144.9 51.7 %collective-permute-start.10 = (bf16[512,512]{1,0:T(8,128)(2,1)}, bf16[512,512]{1,0:T(8,128)(2,1)}, u32[]{:S(2)}, u32[]{:S(2)}) collective-permute-start(bf16[512,512]{1,0:T(8,128)(2,1)} %get-tuple-element.199), channel_id=1, source_target_pairs={{0,16},{8,24},{16,0},{24,8},{1,17},{9,25},{17,1},{25,9},{2,18},{10... | collective-permute-start | bytes 1572872 | tf_op jit(solution)/shard_map/ppermute | solution.py:1121
  151.1 45.6 %collective-permute-start.11 = (bf16[512,512]{1,0:T(8,128)(2,1)}, bf16[512,512]{1,0:T(8,128)(2,1)}, u32[]{:S(2)}, u32[]{:S(2)}) collective-permute-start(bf16[512,512]{1,0:T(8,128)(2,1)} %get-tuple-element.200), channel_id=1, source_target_pairs={{0,8},{8,16},{16,24},{24,0},{1,9},{9,17},{17,25},{25,1},{2,10},{10... | collective-permute-start | bytes 1572872 | tf_op jit(solution)/shard_map/ppermute | solution.py:1121
  194.2 33.5 %collective-permute-start.7 = (bf16[512,512]{1,0:T(8,128)(2,1)}, bf16[512,512]{1,0:T(8,128)(2,1)S(1)}, u32[]{:S(2)}, u32[]{:S(2)}) collective-permute-start(bf16[512,512]{1,0:T(8,128)(2,1)} %get-tuple-element.196), channel_id=1, source_target_pairs={{0,24},{8,0},{16,8},{24,16},{1,25},{9,1},{17,9},{25,17},{2,26},{10... | collective-permute-start | bytes 1572872 | tf_op jit(solution)/shard_map/ppermute | solution.py:1121
  194.3 45.4 %collective-permute-start.8 = (bf16[512,512]{1,0:T(8,128)(2,1)}, bf16[512,512]{1,0:T(8,128)(2,1)}, u32[]{:S(2)}, u32[]{:S(2)}) collective-permute-start(bf16[512,512]{1,0:T(8,128)(2,1)} %get-tuple-element.197), channel_id=1, source_target_pairs={{0,16},{8,24},{16,0},{24,8},{1,17},{9,25},{17,1},{25,9},{2,18},{10... | collective-permute-start | bytes 1572872 | tf_op jit(solution)/shard_map/ppermute | solution.py:1121
  195.5 74.0 %collective-permute-start.9 = (bf16[512,512]{1,0:T(8,128)(2,1)}, bf16[512,512]{1,0:T(8,128)(2,1)}, u32[]{:S(2)}, u32[]{:S(2)}) collective-permute-start(bf16[512,512]{1,0:T(8,128)(2,1)} %get-tuple-element.198), channel_id=1, source_target_pairs={{0,8},{8,16},{16,24},{24,0},{1,9},{9,17},{17,25},{25,1},{2,10},{10... | collective-permute-start | bytes 1572872 | tf_op jit(solution)/shard_map/ppermute | solution.py:1121
  227.6 35.0 %collective-permute-start.12 = (bf16[1280,512]{1,0:T(8,128)(2,1)}, bf16[1280,512]{1,0:T(8,128)(2,1)}, u32[]{:S(2)}, u32[]{:S(2)}) collective-permute-start(bf16[1280,512]{1,0:T(8,128)(2,1)} %get-tuple-element.216), channel_id=1, source_target_pairs={{0,1},{1,0},{2,3},{3,2},{4,5},{5,4},{6,7},{7,6},{8,9},{9,8},{10,11... | collective-permute-start | bytes 3932168 | tf_op jit(solution)/shard_map/ppermute | solution.py:951
  266.0 28.4 %collective-permute-start.14 = (bf16[320,512]{1,0:T(8,128)(2,1)}, bf16[320,512]{1,0:T(8,128)(2,1)}, u32[]{:S(2)}, u32[]{:S(2)}) collective-permute-start(bf16[320,512]{1,0:T(8,128)(2,1)} %get-tuple-element.226), channel_id=1, source_target_pairs={{0,2},{1,3},{2,0},{3,1},{4,6},{5,7},{6,4},{7,5},{8,10},{9,11},{10,... | collective-permute-start | bytes 983048 | tf_op jit(solution)/shard_map/ppermute | solution.py:951
  267.5 26.9 %collective-permute-start.15 = (bf16[320,512]{1,0:T(8,128)(2,1)}, bf16[320,512]{1,0:T(8,128)(2,1)}, u32[]{:S(2)}, u32[]{:S(2)}) collective-permute-start(bf16[320,512]{1,0:T(8,128)(2,1)} %get-tuple-element.227), channel_id=1, source_target_pairs={{0,4},{1,5},{2,6},{3,7},{4,0},{5,1},{6,2},{7,3},{8,12},{9,13},{10,... | collective-permute-start | bytes 983048 | tf_op jit(solution)/shard_map/ppermute | solution.py:951
  269.1 25.4 %collective-permute-start.16 = (bf16[320,512]{1,0:T(8,128)(2,1)}, bf16[320,512]{1,0:T(8,128)(2,1)}, u32[]{:S(2)}, u32[]{:S(2)}) collective-permute-start(bf16[320,512]{1,0:T(8,128)(2,1)} %get-tuple-element.228), channel_id=1, source_target_pairs={{0,6},{1,7},{2,4},{3,5},{4,2},{5,3},{6,0},{7,1},{8,14},{9,15},{10,... | collective-permute-start | bytes 983048 | tf_op jit(solution)/shard_map/ppermute | solution.py:951
  294.4 20.6 %collective-permute-start.13 = (bf16[800,512]{1,0:T(8,128)(2,1)}, bf16[800,512]{1,0:T(8,128)(2,1)S(1)}, u32[]{:S(2)}, u32[]{:S(2)}) collective-permute-start(bf16[800,512]{1,0:T(8,128)(2,1)} %get-tuple-element.222.refs_5_), channel_id=1, source_target_pairs={{0,1},{1,0},{2,3},{3,2},{4,5},{5,4},{6,7},{7,6},{8,9},{9,8},{10,11... | collective-permute-start | bytes 2457608 | tf_op jit(solution)/shard_map/ppermute | solution.py:951
  296.8 11.5 %collective-permute-start.20 = (bf16[80,512]{1,0:T(8,128)(2,1)}, bf16[80,512]{1,0:T(8,128)(2,1)S(1)}, u32[]{:S(2)}, u32[]{:S(2)}) collective-permute-start(bf16[80,512]{1,0:T(8,128)(2,1)} %get-tuple-element.234), channel_id=1, source_target_pairs={{0,8},{8,0},{16,24},{24,16},{1,9},{9,1},{17,25},{25,17},{2,10},{10... | collective-permute-start | bytes 245768 | tf_op jit(solution)/shard_map/ppermute | solution.py:951
  296.8 11.5 %collective-permute-start.21 = (bf16[80,512]{1,0:T(8,128)(2,1)}, bf16[80,512]{1,0:T(8,128)(2,1)S(1)}, u32[]{:S(2)}, u32[]{:S(2)}) collective-permute-start(bf16[80,512]{1,0:T(8,128)(2,1)} %get-tuple-element.235), channel_id=1, source_target_pairs={{0,16},{8,24},{16,0},{24,8},{1,17},{9,25},{17,1},{25,9},{2,18},{10... | collective-permute-start | bytes 245768 | tf_op jit(solution)/shard_map/ppermute | solution.py:951
  296.8 11.5 %collective-permute-start.22 = (bf16[80,512]{1,0:T(8,128)(2,1)}, bf16[80,512]{1,0:T(8,128)(2,1)}, u32[]{:S(2)}, u32[]{:S(2)}) collective-permute-start(bf16[80,512]{1,0:T(8,128)(2,1)} %get-tuple-element.236), channel_id=1, source_target_pairs={{0,24},{8,16},{16,8},{24,0},{1,25},{9,17},{17,9},{25,1},{2,26},{10... | collective-permute-start | bytes 245768 | tf_op jit(solution)/shard_map/ppermute | solution.py:951
  310.6 11.1 %collective-permute-start.28 = (bf16[80,512]{1,0:T(8,128)(2,1)}, bf16[80,512]{1,0:T(8,128)(2,1)S(1)}, u32[]{:S(2)}, u32[]{:S(2)}) collective-permute-start(bf16[80,512]{1,0:T(8,128)(2,1)} %fold.9.refs_11_.refs_1_), channel_id=1, source_target_pairs={{0,24},{8,16},{16,8},{24,0},{1,25},{9,17},{17,9},{25,1},{2,26},{10... | collective-permute-start | bytes 245768 | tf_op jit(solution)/shard_map/ppermute | solution.py:951
  310.6 18.6 %collective-permute-start.27 = (bf16[80,512]{1,0:T(8,128)(2,1)}, bf16[80,512]{1,0:T(8,128)(2,1)S(1)}, u32[]{:S(2)}, u32[]{:S(2)}) collective-permute-start(bf16[80,512]{1,0:T(8,128)(2,1)} %fold.9.refs_11_.refs_1_), channel_id=1, source_target_pairs={{0,16},{8,24},{16,0},{24,8},{1,17},{9,25},{17,1},{25,9},{2,18},{10... | collective-permute-start | bytes 245768 | tf_op jit(solution)/shard_map/ppermute | solution.py:951
  311.9 17.4 %collective-permute-start.26 = (bf16[80,512]{1,0:T(8,128)(2,1)}, bf16[80,512]{1,0:T(8,128)(2,1)}, u32[]{:S(2)}, u32[]{:S(2)}) collective-permute-start(bf16[80,512]{1,0:T(8,128)(2,1)} %fold.9.refs_11_.refs_1_), channel_id=1, source_target_pairs={{0,8},{8,0},{16,24},{24,16},{1,9},{9,1},{17,25},{25,17},{2,10},{10... | collective-permute-start | bytes 245768 | tf_op jit(solution)/shard_map/ppermute | solution.py:951
  318.6 16.0 %collective-permute-start.17 = (bf16[224,512]{1,0:T(8,128)(2,1)}, bf16[224,512]{1,0:T(8,128)(2,1)}, u32[]{:S(2)}, u32[]{:S(2)}) collective-permute-start(bf16[224,512]{1,0:T(8,128)(2,1)} %get-tuple-element.231), channel_id=1, source_target_pairs={{0,2},{1,3},{2,0},{3,1},{4,6},{5,7},{6,4},{7,5},{8,10},{9,11},{10,... | collective-permute-start | bytes 688136 | tf_op jit(solution)/shard_map/ppermute | solution.py:951
  320.2 15.0 %collective-permute-start.18 = (bf16[224,512]{1,0:T(8,128)(2,1)}, bf16[224,512]{1,0:T(8,128)(2,1)}, u32[]{:S(2)}, u32[]{:S(2)}) collective-permute-start(bf16[224,512]{1,0:T(8,128)(2,1)} %get-tuple-element.232), channel_id=1, source_target_pairs={{0,4},{1,5},{2,6},{3,7},{4,0},{5,1},{6,2},{7,3},{8,12},{9,13},{10,... | collective-permute-start | bytes 688136 | tf_op jit(solution)/shard_map/ppermute | solution.py:951
  321.7 13.4 %collective-permute-start.19 = (bf16[224,512]{1,0:T(8,128)(2,1)}, bf16[224,512]{1,0:T(8,128)(2,1)}, u32[]{:S(2)}, u32[]{:S(2)}) collective-permute-start(bf16[224,512]{1,0:T(8,128)(2,1)} %get-tuple-element.233), channel_id=1, source_target_pairs={{0,6},{1,7},{2,4},{3,5},{4,2},{5,3},{6,0},{7,1},{8,14},{9,15},{10,... | collective-permute-start | bytes 688136 | tf_op jit(solution)/shard_map/ppermute | solution.py:951
  331.7 12.7 %collective-permute-start.31 = (bf16[320,512]{1,0:T(8,128)(2,1)}, bf16[320,512]{1,0:T(8,128)(2,1)S(1)}, u32[]{:S(2)}, u32[]{:S(2)}) collective-permute-start(bf16[320,512]{1,0:T(8,128)(2,1)} %spread.4.refs_6_.refs_1_), channel_id=1, source_target_pairs={{0,6},{1,7},{2,4},{3,5},{4,2},{5,3},{6,0},{7,1},{8,14},{9,15},{10,... | collective-permute-start | bytes 983048 | tf_op jit(solution)/shard_map/ppermute | solution.py:951
  334.2 13.2 %collective-permute-start.30 = (bf16[320,512]{1,0:T(8,128)(2,1)}, bf16[320,512]{1,0:T(8,128)(2,1)S(1)}, u32[]{:S(2)}, u32[]{:S(2)}) collective-permute-start(bf16[320,512]{1,0:T(8,128)(2,1)} %spread.4.refs_6_.refs_1_), channel_id=1, source_target_pairs={{0,4},{1,5},{2,6},{3,7},{4,0},{5,1},{6,2},{7,3},{8,12},{9,13},{10,... | collective-permute-start | bytes 983048 | tf_op jit(solution)/shard_map/ppermute | solution.py:951
  334.7 12.8 %collective-permute-start.29 = (bf16[320,512]{1,0:T(8,128)(2,1)}, bf16[320,512]{1,0:T(8,128)(2,1)S(1)}, u32[]{:S(2)}, u32[]{:S(2)}) collective-permute-start(bf16[320,512]{1,0:T(8,128)(2,1)} %spread.4.refs_6_.refs_1_), channel_id=1, source_target_pairs={{0,2},{1,3},{2,0},{3,1},{4,6},{5,7},{6,4},{7,5},{8,10},{9,11},{10,... | collective-permute-start | bytes 983048 | tf_op jit(solution)/shard_map/ppermute | solution.py:951
  351.2 28.5 %collective-permute-start.38 = (bf16[1280,512]{1,0:T(8,128)(2,1)}, bf16[1280,512]{1,0:T(8,128)(2,1)}, u32[]{:S(2)}, u32[]{:S(2)}) collective-permute-start(bf16[1280,512]{1,0:T(8,128)(2,1)} %spread.5.refs_8_.refs_1_), channel_id=1, source_target_pairs={{0,1},{1,0},{2,3},{3,2},{4,5},{5,4},{6,7},{7,6},{8,9},{9,8},{10,11... | collective-permute-start | bytes 3932168 | tf_op jit(solution)/shard_map/ppermute | solution.py:951
  (46 other events, 257.2 us)
Sparse Core Ops, SparseCore 0:
  143.5 66.9 reduce-scatter.4
  214.2 51.3 reduce-scatter.2
